TPU v7x, 512 devices: a whole 4x8x8 slice. The times are simulated.
512 devices in a mesh: rows: 64 (over y, x, core), env: 8 (over z).
Axes of the slice: x: 4, y: 8, z: 8, core: 2. Of those that a mesh axis runs over, the one named last changes fastest.
Arguments:
- features: bfloat16 [16384, 1024], P('rows'), may hold values from -6 to 6
- environments: bfloat16 [2048, 1024], P('env'), may hold values from -0.1875 to 0.1875
- projector: bfloat16 [2048, 2048], P('env'), may hold values from -0.125 to 0.125
- metric: bfloat16 [512, 8, 32, 32], P('rows'), may hold values from -0.375 to 0.375
- neighbours: int32 [512, 8], P('rows'), may hold values from 0 to 511, as said below
- counts: int32 [512], P('rows'), may hold values from 16 to 32, as said below
- target: float32 [16384], P('rows'), may hold values from -6 to 6
Outputs:
- gram: float32 [2048, 2048], P('rows', 'env')
- rhs: float32 [2048], P('env')
Inputs may be any that keep to these rules, and one draw needn't show every extreme that they name: `neighbours`: slot 0 is the block itself; every neighbour lies within 8 blocks of its block. `counts`: some block is full in every draw.
All inputs are finite; a program needn't handle non-finite values.
Results may differ from a plain program's by a relative error of at most 0.0067.
Values may be sent and summed in bfloat16 or wider, within the bound.
No kernel may reach another device: no remote copies, remote signals or barrier semaphores. Data moves between devices by JAX's collectives and lax.ppermute only.
A program may use at most 64 MiB of HBM per device.

v0:
```python
import jax
import jax.numpy as jnp
from jax import lax
from jax.sharding import PartitionSpec as P


def padded(cells, sides, width):
    for axis, dim in sides:
        count = lax.axis_size(axis)
        ends = count - 1
        head = lax.slice_in_dim(cells, 0, width, axis=dim)
        tail = lax.slice_in_dim(cells, cells.shape[dim] - width, cells.shape[dim], axis=dim)
        cells = jnp.concatenate(
            [
                lax.ppermute(tail, axis, [(i, (i + 1) % count) for i in range(ends)]),
                cells,
                lax.ppermute(head, axis, [((i + 1) % count, i) for i in range(ends)]),
            ],
            axis=dim,
        )
    return cells


def per_device(features, environments, projector, metric, neighbours, counts, target):
    env_width = environments.shape[0]
    slab_rows = features.shape[0]
    blocks_here = counts.shape[0]
    block_rows = slab_rows // blocks_here
    slots = lax.broadcasted_iota(jnp.int32, (blocks_here, block_rows), 1)
    mask = (slots < counts[:, None]).astype(jnp.float32).reshape(slab_rows, 1)
    every_env = lax.all_gather(environments, "env", axis=0, tiled=True)
    kern = jnp.dot(features, every_env.T, preferred_element_type=jnp.float32)
    kern = (kern * kern).astype(jnp.bfloat16)
    column_start = lax.axis_index("env") * env_width
    own_cols = lax.dynamic_slice_in_dim(
        lax.all_gather(projector, "env", axis=0, tiled=True), column_start, env_width, 1
    )
    projected = jnp.dot(kern, own_cols, preferred_element_type=jnp.float32)
    psi_local = (projected * mask).astype(jnp.bfloat16)
    extended = padded(psi_local, (("rows", 0),), slab_rows)
    ext_blocks = extended.reshape(3 * blocks_here, block_rows, env_width)
    offset = (lax.axis_index("rows") - 1) * blocks_here
    local_index = neighbours - offset
    picked = ext_blocks[local_index]
    weighted = jnp.einsum("bjrc,bjcm->brm", metric, picked, preferred_element_type=jnp.float32)
    spsi_local = weighted.reshape(slab_rows, env_width).astype(jnp.bfloat16)
    factor = 1.0 / jnp.sqrt(jnp.float32(slab_rows * lax.axis_size("rows")))
    terms = lax.dot_general(
        lax.all_gather(spsi_local, "env", axis=1, tiled=True),
        psi_local,
        (((0,), (0,)), ((), ())),
        preferred_element_type=jnp.float32,
    )
    gram = lax.psum_scatter(terms, "rows", scatter_dimension=0, tiled=True) * factor
    partial_rhs = jnp.dot(target, spsi_local.astype(jnp.float32), precision=lax.Precision.HIGHEST)
    rhs = lax.psum(partial_rhs, "rows") * factor
    return (gram, rhs)


def solution(mesh):
    return jax.shard_map(
        per_device,
        mesh=mesh,
        in_specs=(
            P("rows", None),
            P("env", None),
            P("env", None),
            P("rows", None, None, None),
            P("rows", None),
            P("rows"),
            P("rows"),
        ),
        out_specs=(P("rows", "env"), P("env")),
        check_vma=False,
    )
```

profile of v0, /device:TPU:1, one launch (start us, length us, event | category | flops | bytes accessed | tf_op | source)
XLA Modules:
  0.0 385.0 jit_solution(6755113388133340611)
XLA Ops:
  7.2 0.0 copy-start
  7.2 0.0 all-gather.4.cloned.1.call-start
  7.2 0.7 all-gather.4.cloned.1.call-update
  7.9 0.0 all-gather.6.cloned.1.call-start
  8.0 0.7 all-gather.6.cloned.1.call-update
  8.7 0.0 all-gather.8.cloned.1.call-start
  8.7 0.7 fusion.4
  9.4 0.1 reshape.29
  9.5 64.3 %all-gather.4.cloned.1.call-done = bf16[2048,1024]{1,0:T(8,128)(2,1)} async-done(((bf16[256,1024]{1,0:T(8,128)(2,1)}), bf16[2048,1024]{1,0:T(8,128)(2,1)}) %all-gather.4.cloned.1.call-update) | async-done | bytes 4194320 | tf_op jit(solution)/shard_map/all_gather | solution.py:31
  73.9 97.8 %all-gather.6.cloned.1.call-done = bf16[2048,2048]{1,0:T(8,128)(2,1)} async-done(((bf16[256,2048]{1,0:T(8,128)(2,1)}), bf16[2048,2048]{1,0:T(8,128)(2,1)}) %all-gather.6.cloned.1.call-update) | async-done | bytes 8388624 | tf_op jit(solution)/shard_map/all_gather | solution.py:36
  171.6 0.0 copy-done
  171.6 4.2 %fusion.1 = bf16[256,256]{1,0:T(8,128)(2,1)S(1)} fusion(bf16[2048,2048]{1,0:T(8,128)(2,1)} %all-gather.6.cloned.1.call-done, s32[]{:T(128)S(6)} %select_n.6, bf16[256,1024]{1,0:T(8,128)(2,1)S(1)} %copy-done, bf16[2048,1024]{1,0:T(8,128)(2,1)} %all-gather.4.cloned.1.call-done, f32[256]{0:T(256)S(1)} %reshape.29), kind=kOutput, calls=%fused_computation.5 | convolution fusion | flops 1343356928 | bytes 5899268 | tf_op jit(solution)/shard_map/dot_general | solution.py:38
  175.8 3.7 collective-permute-start
  179.5 1.9 collective-permute-start.1
  181.4 0.0 copy-done.3
  181.4 0.1 reshape.32
  181.5 0.0 collective-permute-done
  181.5 4.2 %collective-permute-done.1 = bf16[256,256]{1,0:T(8,128)(2,1)S(1)} collective-permute-done((bf16[256,256]{1,0:T(8,128)(2,1)S(1)}, bf16[256,256]{1,0:T(8,128)(2,1)S(1)}, u32[]{:S(2)}, u32[]{:S(2)}) %collective-permute-start.1) | collective-permute-done | bytes 131104 | tf_op jit(solution)/shard_map/ppermute | solution.py:17
  185.8 0.0 copy-start.4
  185.8 0.6 gather_fusion
  186.4 0.0 copy-done.2
  186.4 1.0 fusion.2
  187.5 0.0 all-gather.8.cloned.1.call-update
  187.5 0.0 reduce-scatter.2.cloned.1.call-start
  187.5 38.5 %all-gather.8.cloned.1.call-done = bf16[256,2048]{1,0:T(8,128)(2,1)} async-done(((bf16[256,256]{1,0:T(8,128)(2,1)}), bf16[256,2048]{1,0:T(8,128)(2,1)}) %all-gather.8.cloned.1.call-update) | async-done | bytes 1048592 | tf_op jit(solution)/shard_map/all_gather | solution.py:49
  226.0 3.0 fusion.6
  229.0 0.0 reduce-scatter.2.cloned.1.call-update
  229.1 0.1 fusion.7
  229.2 128.4 %psum.7 = f32[256]{0:T(256)S(1)} all-reduce(f32[256]{0:T(256)S(1)} %bitcast.24), channel_id=1, replica_groups=mesh['rows'=64,'env'=8] {'rows'}, use_global_device_ids=true, to_apply=%region_1.0 | all-reduce | flops 256 | bytes 2048 | tf_op jit(solution)/shard_map/psum | solution.py:56
  357.6 0.6 broadcast_multiply_fusion.1
  358.2 18.9 %reduce-scatter.2.cloned.1.call-done = f32[32,256]{1,0:T(8,128)} async-done(((f32[2048,256]{1,0:T(8,128)}), f32[32,256]{1,0:T(8,128)}) %reduce-scatter.2.cloned.1.call-update) | async-done | bytes 32784 | tf_op jit(solution)/shard_map/reduce_scatter | solution.py:54
  377.1 1.4 broadcast_multiply_fusion
  (8 shorter events, 0.0 us)
Async XLA Ops:
  7.2 164.5 %copy-start = (bf16[256,1024]{1,0:T(8,128)(2,1)S(1)}, bf16[256,1024]{1,0:T(8,128)(2,1)}, u32[]{:S(2)}) copy-start(bf16[256,1024]{1,0:T(8,128)(2,1)} %param.7) | copy-start | bytes 1572868
  7.2 66.7 %all-gather.4.cloned.1.call-start = ((), (), s32[]{:S(2)}) async-start(), calls=%async_computation.1 | async-start | bytes 4718592 | tf_op jit(solution)/shard_map/all_gather | solution.py:31
  7.9 163.7 %all-gather.6.cloned.1.call-start = ((), (), s32[]{:S(2)}) async-start(), calls=%async_computation.2 | async-start | bytes 9437184 | tf_op jit(solution)/shard_map/all_gather | solution.py:36
  8.7 217.3 %all-gather.8.cloned.1.call-start = ((), (), s32[]{:S(2)}) async-start(), calls=%async_computation.3 | async-start | bytes 1179648 | tf_op jit(solution)/shard_map/all_gather | solution.py:49
  9.5 171.9 %copy-start.3 = (s32[8,8]{1,0:T(8,128)S(1)}, s32[8,8]{1,0:T(8,128)}, u32[]{:S(2)}) copy-start(s32[8,8]{1,0:T(8,128)} %param.11) | copy-start | bytes 772
  9.5 176.9 %copy-start.2 = (bf16[8,8,32,32]{3,2,1,0:T(8,128)(2,1)S(1)}, bf16[8,8,32,32]{3,2,1,0:T(8,128)(2,1)}, u32[]{:S(2)}) copy-start(bf16[8,8,32,32]{3,2,1,0:T(8,128)(2,1)} %param.10) | copy-start | bytes 393220
  175.8 5.7 %collective-permute-start = (bf16[256,256]{1,0:T(8,128)(2,1)S(1)}, bf16[256,256]{1,0:T(8,128)(2,1)S(1)}, u32[]{:S(2)}, u32[]{:S(2)}) collective-permute-start(bf16[256,256]{1,0:T(8,128)(2,1)S(1)} %fusion.1), channel_id=1, source_target_pairs={{0,8},{8,16},{16,24},{24,32},{32,40},{40,48},{48,56},{56,64},{64,7... | collective-permute-start | bytes 393224 | tf_op jit(solution)/shard_map/ppermute | solution.py:15
  179.5 6.3 %collective-permute-start.1 = (bf16[256,256]{1,0:T(8,128)(2,1)S(1)}, bf16[256,256]{1,0:T(8,128)(2,1)S(1)}, u32[]{:S(2)}, u32[]{:S(2)}) collective-permute-start(bf16[256,256]{1,0:T(8,128)(2,1)S(1)} %fusion.1), channel_id=1, source_target_pairs={{8,0},{16,8},{24,16},{32,24},{40,32},{48,40},{56,48},{64,56},{72,6... | collective-permute-start | bytes 393224 | tf_op jit(solution)/shard_map/ppermute | solution.py:17
  185.8 43.3 %copy-start.4 = (f32[256]{0:T(256)S(1)}, f32[256]{0:T(256)}, u32[]{:S(2)}) copy-start(f32[256]{0:T(256)} %param.13) | copy-start | bytes 3076
  187.4 41.6 %copy-start.1 = (bf16[8,256,32]{1,2,0:T(8,128)(2,1)S(1)}, bf16[8,256,32]{1,2,0:T(8,128)(2,1)}, u32[]{:S(2)}) copy-start(bf16[8,256,32]{1,2,0:T(8,128)(2,1)} %fusion.2) | copy-start | bytes 393220
  187.5 189.7 %reduce-scatter.2.cloned.1.call-start = ((), (), s32[]{:S(2)}) async-start(), calls=%async_computation.4 | async-start | bytes 2129920 | tf_op jit(solution)/shard_map/reduce_scatter | solution.py:54
Sparse Core Ops, SparseCore 0:
  10.1 63.7 all-gather.3
  75.9 95.6 all-gather.5
  187.6 38.3 all-gather.7
  230.5 146.6 reduce-scatter.1
where the time goes:
time: 389 us; the launch traced here: 385 us
  waiting for transfers between devices  225 us (58%)
  blocking collectives  128 us (33%)
  between operations  13.9 us (4%)
  matrix products  8.35 us (2%)
  starting transfers between devices  5.74 us (1%)
    psum x1, blocking collectives, per_device(): rhs = lax.psum(partial_rhs, 'rows') * factor  128 us
    all_gather x1, waiting for transfers between devices, per_device(): lax.all_gather(projector, 'env', axis=0, tiled=True)  97.8 us
    all_gather x1, waiting for transfers between devices, per_device(): every_env = lax.all_gather(environments, 'env', axis=0, tiled=True)  64.3 us
    all_gather x1, waiting for transfers between devices, per_device(): lax.all_gather(spsi_local, 'env', axis=1, tiled=True)  38.5 us
    reduce_scatter x1, waiting for transfers between devices, per_device(): lax.psum_scatter(terms, 'rows', scatter_dimension=0, tiled=True) * factor  18.9 us
  transfers between devices with their start and end apart: 6, of which 5 were waited for; matrix products, arithmetic and copies ran while one was open for 0% of the time, Pallas kernels for 0%

commit v1 on v0

v1 whole, which is shorter than its diff:
```python
import jax
import jax.numpy as jnp
from jax import lax
from jax.experimental import pallas as pl
from jax.experimental.pallas import tpu as pltpu
from jax.sharding import Mesh, PartitionSpec as P

BLK = 32
ROWS_AXES = ("y", "x", "core")
VMEM = pl.BlockSpec(memory_space=pltpu.VMEM)
SMEM = pl.BlockSpec(memory_space=pltpu.SMEM)
PARAMS = pltpu.CompilerParams(vmem_limit_bytes=48 * 1024 * 1024)


def dot(a, b, dims):
    return lax.dot_general(a, b, (dims, ((), ())), preferred_element_type=jnp.float32)


def project_kernel(counts, features, environments, projector, out):
    kern = dot(features[...], environments[...], ((1,), (1,)))
    kern = (kern * kern).astype(jnp.bfloat16)
    rows, width = kern.shape
    slots = lax.broadcasted_iota(jnp.int32, (BLK, width), 0)
    masked = jnp.concatenate(
        [
            jnp.where(slots < counts[b], kern[b * BLK:(b + 1) * BLK], jnp.bfloat16(0))
            for b in range(rows // BLK)
        ],
        axis=0,
    )
    for part in range(out.shape[0]):
        cols = slice(part * width, (part + 1) * width)
        out[part] = dot(masked, projector[:, cols], ((1,), (0,))).astype(jnp.bfloat16)


def sum_kernel(parts, out):
    total = parts[0].astype(jnp.float32)
    for part in range(1, parts.shape[0]):
        total = total + parts[part].astype(jnp.float32)
    out[...] = total.astype(jnp.bfloat16)


def metric_kernel(neighbours, before, own, after, metric, target, out, rhs, cells):
    rows = own.shape[0]
    cells[0:rows] = before[...]
    cells[rows:2 * rows] = own[...]
    cells[2 * rows:3 * rows] = after[...]
    first = neighbours[0, 0] - rows // BLK
    total = jnp.zeros((1, own.shape[1]), jnp.float32)
    for b in range(rows // BLK):
        picked = jnp.concatenate(
            [
                cells[pl.ds(pl.multiple_of((neighbours[b, j] - first) * BLK, BLK), BLK), :]
                for j in range(neighbours.shape[1])
            ],
            axis=0,
        )
        here = slice(b * BLK, (b + 1) * BLK)
        weighted = dot(metric[here, :], picked, ((1,), (0,))).astype(jnp.bfloat16)
        for copy in range(out.shape[0]):
            out[copy, here, :] = weighted
        total = total + jnp.sum(weighted.astype(jnp.float32) * target[here, :], axis=0, keepdims=True)
    rhs[...] = total


def gram_kernel(neighbours, weighted, psi, kept, sent, block):
    core = (neighbours[0, 0] // (psi.shape[0] // BLK)) % 2
    for part in range(weighted.shape[0]):
        block[...] = dot(weighted[part], psi[...], ((0,), (0,)))
        for x in range(kept.shape[1]):
            kept[part, x] = block[pl.ds(pl.multiple_of((2 * x + core) * BLK, BLK), BLK), :]
            sent[part, x] = block[
                pl.ds(pl.multiple_of((2 * x + 1 - core) * BLK, BLK), BLK), :
            ].astype(jnp.bfloat16)


def add_kernel(kept, received, out):
    for part in range(kept.shape[0]):
        out[part] = (kept[part] + received[part].astype(jnp.float32)).astype(jnp.bfloat16)


def final_kernel(parts, rhs_parts, gram, rhs, *, factor):
    total = parts[0].astype(jnp.float32)
    for part in range(1, parts.shape[0]):
        total = total + parts[part].astype(jnp.float32)
    gram[...] = total * factor
    rhs[...] = jnp.sum(rhs_parts[...], axis=0, keepdims=True) * factor


def per_device(features, environments, projector, metric, neighbours, counts, target):
    f32, bf16 = jnp.float32, jnp.bfloat16
    slab, width = features.shape[0], environments.shape[0]
    planes = lax.axis_size("env")
    ys, xs = lax.axis_size("y"), lax.axis_size("x")
    devices = ys * xs * lax.axis_size("core")
    shape = jax.ShapeDtypeStruct

    metric_rows = metric.transpose(0, 2, 1, 3).reshape(slab, -1)
    target_column = target.reshape(slab, 1)

    partial = pl.pallas_call(
        project_kernel,
        out_shape=shape((planes, slab, width), bf16),
        in_specs=[SMEM, VMEM, VMEM, VMEM],
        out_specs=VMEM,
        compiler_params=PARAMS,
    )(counts, features, environments, projector)
    partial = lax.all_to_all(partial, "env", 0, 0, tiled=True)
    psi = pl.pallas_call(
        sum_kernel,
        out_shape=shape((slab, width), bf16),
        in_specs=[VMEM],
        out_specs=VMEM,
        compiler_params=PARAMS,
    )(partial)

    before = lax.ppermute(psi, ROWS_AXES, [(i, i + 1) for i in range(devices - 1)])
    after = lax.ppermute(psi, ROWS_AXES, [(i + 1, i) for i in range(devices - 1)])
    weighted, partial_rhs = pl.pallas_call(
        metric_kernel,
        out_shape=(shape((planes, slab, width), bf16), shape((1, width), f32)),
        in_specs=[SMEM, VMEM, VMEM, VMEM, VMEM, VMEM],
        out_specs=(VMEM, VMEM),
        scratch_shapes=[pltpu.VMEM((3 * slab, width), bf16)],
        compiler_params=PARAMS,
    )(neighbours, before, psi, after, metric_rows, target_column)
    every_rhs = lax.all_gather(partial_rhs, ROWS_AXES, axis=0, tiled=True)
    weighted = lax.all_to_all(weighted, "env", 0, 0, tiled=True)

    kept, sent = pl.pallas_call(
        gram_kernel,
        out_shape=(shape((ys, xs, BLK, width), f32), shape((ys, xs, BLK, width), bf16)),
        in_specs=[SMEM, VMEM, VMEM],
        out_specs=(VMEM, VMEM),
        scratch_shapes=[pltpu.VMEM((width, width), f32)],
        compiler_params=PARAMS,
    )(neighbours, weighted, psi)
    received = lax.ppermute(sent, "core", [(0, 1), (1, 0)])
    both = pl.pallas_call(
        add_kernel,
        out_shape=shape((ys, xs, BLK, width), bf16),
        in_specs=[VMEM, VMEM],
        out_specs=VMEM,
        compiler_params=PARAMS,
    )(kept, received)
    parts = lax.all_to_all(both.reshape(ys * xs, BLK, width), ("y", "x"), 0, 0, tiled=True)

    def finish(parts, rhs_parts, gram, rhs):
        final_kernel(parts, rhs_parts, gram, rhs, factor=1.0 / (slab * devices) ** 0.5)

    gram, rhs = pl.pallas_call(
        finish,
        out_shape=(shape((BLK, width), f32), shape((1, width), f32)),
        in_specs=[VMEM, VMEM],
        out_specs=(VMEM, VMEM),
        compiler_params=PARAMS,
    )(parts, every_rhs)
    return gram, rhs.reshape(width)


def solution(mesh):
    ys, xs, cores = 8, 4, 2
    split = Mesh(mesh.devices.reshape(ys, xs, cores, mesh.shape["env"]), ("y", "x", "core", "env"))
    rows = P(ROWS_AXES)
    return jax.shard_map(
        per_device,
        mesh=split,
        in_specs=(
            P(ROWS_AXES, None),
            P("env", None),
            P("env", None),
            P(ROWS_AXES, None, None, None),
            P(ROWS_AXES, None),
            rows,
            rows,
        ),
        out_specs=(P(ROWS_AXES, "env"), P("env")),
        check_vma=False,
    )
```

time: 389 us -> 151 us (0.39)
  waiting for transfers between devices: 225 us -> 4.82 us
  starting transfers between devices: 5.74 us -> 21.1 us
  blocking collectives: 128 us -> 113 us
  between operations: 13.9 us -> 0.75 us
  matrix products: 8.35 us -> 0 us
  Pallas kernels: 0 us -> 5.71 us
  local copies, waits for them, and re-layouts: 0.8 us -> 5.34 us
    all_gather x3 -> x0, waiting for transfers between devices: 201 us -> none  [the longest x1 97.8 us: per_device(): lax.all_gather(projector, 'env', axis=0, tiled=True)]
    psum x1 -> x0, blocking collectives: 128 us -> none  [per_device(): rhs = lax.psum(partial_rhs, 'rows') * factor]
    all_to_all x0 -> x2, blocking collectives: none -> 66.7 us  [the longest x1 37.9 us: per_device(): partial = lax.all_to_all(partial, 'env', 0, 0, tiled=True)]
    all_gather x0 -> x1, blocking collectives: none -> 46.4 us  [per_device(): every_rhs = lax.all_gather(partial_rhs, ROWS_AXES, axis=0, tiled=True)]
    reduce_scatter x1 -> x0, waiting for transfers between devices: 18.9 us -> none  [per_device(): lax.psum_scatter(terms, 'rows', scatter_dimension=0, tiled=True) * factor]
    all_to_all x0 -> x1, starting transfers between devices: none -> 11.7 us  [per_device(): lax.all_to_all(both.reshape(ys * xs, BLK, width), ('y', 'x'), 0, 0, tiled...]
    dot_general x4 -> x0, matrix products: 8.35 us -> none  [the longest x1 4.16 us: per_device(): projected = jnp.dot(kern, own_cols, preferred_element_type=jnp.float32)]
    pallas_call x0 -> x6, Pallas kernels: none -> 5.71 us  [the longest x1 1.54 us: per_device(): pl.pallas_call(gram_kernel, out_shape=(shape((ys, xs, BLK, width), f32),...]
  transfers between devices with their start and end apart: 6 -> 4, of which waited for: 5 -> 2; matrix products, arithmetic and copies ran while one was open for 0% -> 0% of each run, Pallas kernels for 0% -> 0%
where the time goes in v1:
time: 151 us
  blocking collectives  113 us (75%)
  starting transfers between devices  21.1 us (14%)
  Pallas kernels  5.71 us (4%)
  local copies, waits for them, and re-layouts  5.34 us (4%)
  waiting for transfers between devices  4.82 us (3%)
    all_gather x1, blocking collectives, per_device(): every_rhs = lax.all_gather(partial_rhs, ROWS_AXES, axis=0, tiled=True)  46.4 us
    all_to_all x1, blocking collectives, per_device(): partial = lax.all_to_all(partial, 'env', 0, 0, tiled=True)  37.9 us
    all_to_all x1, blocking collectives, per_device(): weighted = lax.all_to_all(weighted, 'env', 0, 0, tiled=True)  28.8 us
    all_to_all x1, starting transfers between devices, per_device(): lax.all_to_all(both.reshape(ys * xs, BLK, width), ('y', 'x'), 0, 0, tiled...  11.7 us
    ppermute x1, starting transfers between devices, per_device(): lax.ppermute(psi, ROWS_AXES, [(i, i + 1) for i in range(devices - 1)])  5.58 us
    unnamed x15, local copies, waits for them, and re-layouts  4.64 us
  transfers between devices with their start and end apart: 4, of which 2 were waited for; matrix products, arithmetic and copies ran while one was open for 0% of the time, Pallas kernels for 0%

profile of v1, /device:TPU:1, one launch (start us, length us, event | category | flops | bytes accessed | tf_op | source)
XLA Modules:
  0.0 150.9 jit_solution(8061824854337084216)
XLA Ops:
  0.6 0.0 copy-start
  0.6 1.2 copy-done
  1.9 0.0 copy-start.1
  1.9 1.0 copy-done.1
  2.9 0.0 copy-start.2
  2.9 1.0 copy-done.2
  3.9 0.0 copy-start.4
  3.9 0.7 copy-done.4
  4.6 1.5 shard_map.86
  6.1 37.9 %all_to_all.15.parts = bf16[8,256,256]{2,1,0:T(8,128)(2,1)S(1)} all-to-all(bf16[8,256,256]{2,1,0:T(8,128)(2,1)S(1)} %shard_map.86), channel_id=1, replica_groups=mesh['y'=8,'x'=4,'core'=2,'env'=8] {'env'}, dimensions={0} | all-to-all | bytes 2097152 | tf_op jit(solution)/shard_map/all_to_all | solution.py:108
  44.0 0.1 shard_map.87.own.psi
  44.1 5.6 %collective-permute-start = (bf16[256,256]{1,0:T(8,128)(2,1)S(1)}, bf16[256,256]{1,0:T(8,128)(2,1)S(1)}, u32[]{:S(2)}, u32[]{:S(2)}) collective-permute-start(bf16[256,256]{1,0:T(8,128)(2,1)S(1)} %shard_map.87.own.psi), channel_id=1, source_target_pairs={{0,8},{8,16},{16,24},{24,32},{32,40},{40,48},{48,56},{56,64},{64,7... | collective-permute-start | bytes 393224 | tf_op jit(solution)/shard_map/ppermute | solution.py:117
  49.7 1.9 %collective-permute-start.1 = (bf16[256,256]{1,0:T(8,128)(2,1)S(1)}, bf16[256,256]{1,0:T(8,128)(2,1)S(1)}, u32[]{:S(2)}, u32[]{:S(2)}) collective-permute-start(bf16[256,256]{1,0:T(8,128)(2,1)S(1)} %shard_map.87.own.psi), channel_id=1, source_target_pairs={{8,0},{16,8},{24,16},{32,24},{40,32},{48,40},{56,48},{64,56},{72,6... | collective-permute-start | bytes 393224 | tf_op jit(solution)/shard_map/ppermute | solution.py:118
  51.7 0.0 copy-done.5
  51.7 0.2 copy.12
  51.9 0.4 reshape.16.metric
  52.2 0.0 copy-start.6
  52.3 0.7 copy-done.6
  52.9 0.1 copy.13.target
  53.1 0.0 collective-permute-done.before
  53.1 2.9 %collective-permute-done.1.after = bf16[256,256]{1,0:T(8,128)(2,1)S(1)} collective-permute-done((bf16[256,256]{1,0:T(8,128)(2,1)S(1)}, bf16[256,256]{1,0:T(8,128)(2,1)S(1)}, u32[]{:S(2)}, u32[]{:S(2)}) %collective-permute-start.1) | collective-permute-done | bytes 131104 | tf_op jit(solution)/shard_map/ppermute | solution.py:118
  56.0 0.0 copy-done.3
  56.0 0.9 shard_map.88
  56.9 28.8 %all_to_all.16.weighted = bf16[8,256,256]{2,1,0:T(8,128)(2,1)S(1)} all-to-all(bf16[8,256,256]{2,1,0:T(8,128)(2,1)S(1)} %get-tuple-element.8), channel_id=1, replica_groups=mesh['y'=8,'x'=4,'core'=2,'env'=8] {'env'}, dimensions={0} | all-to-all | bytes 2097152 | tf_op jit(solution)/shard_map/all_to_all | solution.py:128
  85.8 1.5 %shard_map.89 = (f32[8,4,32,256]{3,2,1,0:T(8,128)S(1)}, bf16[8,4,32,256]{3,2,1,0:T(8,128)(2,1)S(1)}) custom-call(s32[8,8]{1,0:T(8,128)S(1)} %copy-done.3, bf16[8,256,256]{2,1,0:T(8,128)(2,1)S(1)} %all_to_all.16.weighted, bf16[256,256]{1,0:T(8,128)(2,1)S(1)} %shard_map.87.own.psi), custom_call_target="tpu_custom_call" | custom-call | tf_op jit(solution)/shard_map/pallas_call | solution.py:130
  87.3 1.9 %collective-permute-start.2 = (bf16[8,4,32,256]{3,2,1,0:T(8,128)(2,1)S(1)}, bf16[8,4,32,256]{3,2,1,0:T(8,128)(2,1)S(1)}, u32[]{:S(2)}, u32[]{:S(2)}) collective-permute-start(bf16[8,4,32,256]{3,2,1,0:T(8,128)(2,1)S(1)} %get-tuple-element.10), channel_id=1, source_target_pairs={{0,8},{8,0},{1,9},{9,1},{2,10},{10,2},{3,11},{11,3},{4,12},{12,4},... | collective-permute-start | bytes 1572872 | tf_op jit(solution)/shard_map/ppermute | solution.py:138
  89.3 1.9 %collective-permute-done.2.received = bf16[8,4,32,256]{3,2,1,0:T(8,128)(2,1)S(1)} collective-permute-done((bf16[8,4,32,256]{3,2,1,0:T(8,128)(2,1)S(1)}, bf16[8,4,32,256]{3,2,1,0:T(8,128)(2,1)S(1)}, u32[]{:S(2)}, u32[]{:S(2)}) %collective-permute-start.2) | collective-permute-done | bytes 524320 | tf_op jit(solution)/shard_map/ppermute | solution.py:138
  91.1 0.9 shard_map.90
  92.0 11.7 %all-to-all-start.2 = ((bf16[32,32,256]{2,1,0:T(8,128)(2,1)}), bf16[32,32,256]{2,1,0:T(8,128)(2,1)S(1)}, u32[]{:S(2)}, u32[]{:S(2)}) async-start(bf16[32,32,256]{2,1,0:T(8,128)(2,1)} %bitcast.2), calls=%async_computation.2 | async-start | bytes 1048576 | tf_op jit(solution)/shard_map/all_to_all | solution.py:146
  103.7 46.4 %all-gather = f32[64,1,256]{2,1,0:T(1,128)S(1)} all-gather(f32[1,1,256]{2,1,0:T(1,128)S(1)} %bitcast.11), channel_id=1, replica_groups=mesh['y'=8,'x'=4,'core'=2,'env'=8] {'y','x','core'}, dimensions={0}, use_global_device_ids=true | all-gather | bytes 66560 | tf_op jit(solution)/shard_map/all_gather | solution.py:127
  150.1 0.0 all-to-all-done.2.parts
  150.2 0.7 shard_map.91
  (3 shorter events, 0.0 us)
Async XLA Ops:
  0.6 1.2 copy-start
  1.9 1.0 copy-start.1
  2.9 1.0 copy-start.2
  3.9 0.7 copy-start.4
  44.0 7.7 %copy-start.5 = (bf16[8,8,32,32]{3,2,1,0:T(8,128)(2,1)S(1)}, bf16[8,8,32,32]{3,2,1,0:T(8,128)(2,1)}, u32[]{:S(2)}) copy-start(bf16[8,8,32,32]{3,2,1,0:T(8,128)(2,1)} %param.10) | copy-start | bytes 393220
  44.1 8.9 %collective-permute-start = (bf16[256,256]{1,0:T(8,128)(2,1)S(1)}, bf16[256,256]{1,0:T(8,128)(2,1)S(1)}, u32[]{:S(2)}, u32[]{:S(2)}) collective-permute-start(bf16[256,256]{1,0:T(8,128)(2,1)S(1)} %shard_map.87.own.psi), channel_id=1, source_target_pairs={{0,8},{8,16},{16,24},{24,32},{32,40},{40,48},{48,56},{56,64},{64,7... | collective-permute-start | bytes 393224 | tf_op jit(solution)/shard_map/ppermute | solution.py:117
  49.7 6.3 %collective-permute-start.1 = (bf16[256,256]{1,0:T(8,128)(2,1)S(1)}, bf16[256,256]{1,0:T(8,128)(2,1)S(1)}, u32[]{:S(2)}, u32[]{:S(2)}) collective-permute-start(bf16[256,256]{1,0:T(8,128)(2,1)S(1)} %shard_map.87.own.psi), channel_id=1, source_target_pairs={{8,0},{16,8},{24,16},{32,24},{40,32},{48,40},{56,48},{64,56},{72,6... | collective-permute-start | bytes 393224 | tf_op jit(solution)/shard_map/ppermute | solution.py:118
  52.2 0.7 copy-start.6
  52.9 3.1 %copy-start.3 = (s32[8,8]{1,0:T(8,128)S(1)}, s32[8,8]{1,0:T(8,128)}, u32[]{:S(2)}) copy-start(s32[8,8]{1,0:T(8,128)} %neighbours.3) | copy-start | bytes 772
  87.3 3.8 %collective-permute-start.2 = (bf16[8,4,32,256]{3,2,1,0:T(8,128)(2,1)S(1)}, bf16[8,4,32,256]{3,2,1,0:T(8,128)(2,1)S(1)}, u32[]{:S(2)}, u32[]{:S(2)}) collective-permute-start(bf16[8,4,32,256]{3,2,1,0:T(8,128)(2,1)S(1)} %get-tuple-element.10), channel_id=1, source_target_pairs={{0,8},{8,0},{1,9},{9,1},{2,10},{10,2},{3,11},{11,3},{4,12},{12,4},... | collective-permute-start | bytes 1572872 | tf_op jit(solution)/shard_map/ppermute | solution.py:138
  92.0 58.1 %all-to-all-start.2 = ((bf16[32,32,256]{2,1,0:T(8,128)(2,1)}), bf16[32,32,256]{2,1,0:T(8,128)(2,1)S(1)}, u32[]{:S(2)}, u32[]{:S(2)}) async-start(bf16[32,32,256]{2,1,0:T(8,128)(2,1)} %bitcast.2), calls=%async_computation.2 | async-start | bytes 1048576 | tf_op jit(solution)/shard_map/all_to_all | solution.py:146

commit v2 on v1

v2 whole, which is shorter than its diff:
```python
import jax
import jax.numpy as jnp
from jax import lax
from jax.experimental import pallas as pl
from jax.experimental.pallas import tpu as pltpu
from jax.sharding import Mesh, PartitionSpec as P

BLK = 32
EXTRA = 16
ROWS_AXES = ("y", "x", "core")
VMEM = pl.BlockSpec(memory_space=pltpu.VMEM)
SMEM = pl.BlockSpec(memory_space=pltpu.SMEM)
ANY = pl.BlockSpec(memory_space=pl.ANY)
PARAMS = pltpu.CompilerParams(vmem_limit_bytes=48 * 1024 * 1024)


def dot(a, b, dims):
    return lax.dot_general(a, b, (dims, ((), ())), preferred_element_type=jnp.float32)


def project_kernel(counts, features, environments, projector, out, slots_used, left, right, weights, sems):
    copies = [
        pltpu.make_async_copy(source, target, sems.at[i])
        for i, (source, target) in enumerate(
            [(features, left), (environments, right), (counts, slots_used), (projector, weights)]
        )
    ]
    for copy in copies:
        copy.start()
    for copy in copies[:3]:
        copy.wait()
    kern = dot(left[...], right[...], ((1,), (1,)))
    kern = (kern * kern).astype(jnp.bfloat16)
    rows, width = kern.shape
    slots = lax.broadcasted_iota(jnp.int32, (BLK, width), 0)
    masked = jnp.concatenate(
        [
            jnp.where(slots < slots_used[b], kern[b * BLK:(b + 1) * BLK], jnp.bfloat16(0))
            for b in range(rows // BLK)
        ],
        axis=0,
    )
    copies[3].wait()
    for part in range(out.shape[0]):
        cols = slice(part * width, (part + 1) * width)
        out[part] = dot(masked, weights[:, cols], ((1,), (0,))).astype(jnp.bfloat16)


def sum_kernel(parts, out):
    total = parts[0].astype(jnp.float32)
    for part in range(1, parts.shape[0]):
        total = total + parts[part].astype(jnp.float32)
    out[...] = total.astype(jnp.bfloat16)


def high_low(row, extra):
    high = row.astype(jnp.bfloat16)
    low = (row - high.astype(jnp.float32)).astype(jnp.bfloat16)
    line = lax.broadcasted_iota(jnp.int32, (extra, row.shape[1]), 0)
    return jnp.where(line == 0, high, jnp.where(line == 1, low, jnp.bfloat16(0)))


def metric_kernel(neighbours, before, own, after, metric, target, out, carried, cells):
    rows, width = own.shape
    cells[0:rows] = before[...]
    cells[rows:2 * rows] = own[...]
    cells[2 * rows:3 * rows] = after[...]
    first = neighbours[0, 0] - rows // BLK
    total = jnp.zeros((1, width), jnp.float32)
    blocks = []
    for b in range(rows // BLK):
        picked = jnp.concatenate(
            [
                cells[pl.ds(pl.multiple_of((neighbours[b, j] - first) * BLK, BLK), BLK), :]
                for j in range(neighbours.shape[1])
            ],
            axis=0,
        )
        here = slice(b * BLK, (b + 1) * BLK)
        weighted = dot(metric[here, :], picked, ((1,), (0,))).astype(jnp.bfloat16)
        blocks.append(weighted)
        total = total + jnp.sum(weighted.astype(jnp.float32) * target[here, :], axis=0, keepdims=True)
    weighted = jnp.concatenate(blocks, axis=0)
    unit = (
        lax.broadcasted_iota(jnp.int32, (rows, rows), 0) == lax.broadcasted_iota(jnp.int32, (rows, rows), 1)
    ).astype(jnp.bfloat16)
    turned = dot(weighted, unit, ((0,), (0,))).astype(jnp.bfloat16)
    group = width // BLK
    planes = out.shape[0] // group
    for j in range(group):
        for z in range(planes):
            out[j * planes + z] = turned[j * BLK:(j + 1) * BLK, :]
    carried[0:rows] = own[...]
    carried[rows:] = high_low(total, carried.shape[0] - rows)


def gram_kernel(weighted, carried, out):
    group = carried.shape[0]
    planes = weighted.shape[0] // group
    rows, width = weighted.shape[2], carried.shape[2]
    total = jnp.zeros((planes * BLK, width), jnp.float32)
    rhs = jnp.zeros((1, width), jnp.float32)
    for j in range(group):
        turned = weighted[j * planes:(j + 1) * planes].reshape(planes * BLK, rows)
        total = total + dot(turned, carried[j, 0:rows], ((1,), (0,)))
        tail = carried[j, rows:].astype(jnp.float32)
        rhs = rhs + (tail[0:1] + tail[1:2])
    extra = out.shape[1] - BLK
    lines = high_low(rhs, extra)
    for z in range(planes):
        out[z, 0:BLK] = total[z * BLK:(z + 1) * BLK].astype(jnp.bfloat16)
        out[z, BLK:] = lines


def final_kernel(parts, gram, rhs, *, factor):
    total = parts[0].astype(jnp.float32)
    for part in range(1, parts.shape[0]):
        total = total + parts[part].astype(jnp.float32)
    gram[...] = total[0:BLK] * factor
    rhs[...] = (total[BLK:BLK + 1] + total[BLK + 1:BLK + 2]) * factor


def per_device(features, environments, projector, metric, neighbours, counts, target):
    f32, bf16 = jnp.float32, jnp.bfloat16
    slab, width = features.shape[0], environments.shape[0]
    planes, ys = lax.axis_size("env"), lax.axis_size("y")
    group = lax.axis_size("x") * lax.axis_size("core")
    devices = ys * group
    shape = jax.ShapeDtypeStruct

    metric_rows = metric.transpose(0, 2, 1, 3).reshape(slab, -1)
    target_column = target.reshape(slab, 1)

    partial = pl.pallas_call(
        project_kernel,
        out_shape=shape((planes, slab, width), bf16),
        in_specs=[ANY] * 4,
        out_specs=VMEM,
        scratch_shapes=[
            pltpu.SMEM(counts.shape, jnp.int32),
            pltpu.VMEM(features.shape, bf16),
            pltpu.VMEM(environments.shape, bf16),
            pltpu.VMEM(projector.shape, bf16),
            pltpu.SemaphoreType.DMA((4,)),
        ],
        compiler_params=PARAMS,
    )(counts, features, environments, projector)
    partial = lax.all_to_all(partial, "env", 0, 0, tiled=True)
    psi = pl.pallas_call(
        sum_kernel,
        out_shape=shape((slab, width), bf16),
        in_specs=[VMEM],
        out_specs=VMEM,
        compiler_params=PARAMS,
    )(partial)

    before = lax.ppermute(psi, ROWS_AXES, [(i, i + 1) for i in range(devices - 1)])
    after = lax.ppermute(psi, ROWS_AXES, [(i + 1, i) for i in range(devices - 1)])
    weighted, carried = pl.pallas_call(
        metric_kernel,
        out_shape=(shape((group * planes, BLK, slab), bf16), shape((slab + EXTRA, width), bf16)),
        in_specs=[SMEM, VMEM, VMEM, VMEM, VMEM, VMEM],
        out_specs=(VMEM, VMEM),
        scratch_shapes=[pltpu.VMEM((3 * slab, width), bf16)],
        compiler_params=PARAMS,
    )(neighbours, before, psi, after, metric_rows, target_column)
    carried = lax.all_gather(carried, ("x", "core"), axis=0)
    weighted = lax.all_to_all(weighted, ("x", "core", "env"), 0, 0, tiled=True)
    terms = pl.pallas_call(
        gram_kernel,
        out_shape=shape((ys, BLK + EXTRA, width), bf16),
        in_specs=[VMEM, VMEM],
        out_specs=VMEM,
        compiler_params=PARAMS,
    )(weighted, carried)
    terms = lax.all_to_all(terms, "y", 0, 0, tiled=True)

    def finish(parts, gram, rhs):
        final_kernel(parts, gram, rhs, factor=1.0 / (slab * devices) ** 0.5)

    gram, rhs = pl.pallas_call(
        finish,
        out_shape=(shape((BLK, width), f32), shape((1, width), f32)),
        in_specs=[VMEM],
        out_specs=(VMEM, VMEM),
        compiler_params=PARAMS,
    )(terms)
    return gram, rhs.reshape(width)


def solution(mesh):
    ys, xs, cores = 8, 4, 2
    split = Mesh(mesh.devices.reshape(ys, xs, cores, mesh.shape["env"]), ("y", "x", "core", "env"))
    rows = P(ROWS_AXES)
    return jax.shard_map(
        per_device,
        mesh=split,
        in_specs=(
            P(ROWS_AXES, None),
            P("env", None),
            P("env", None),
            P(ROWS_AXES, None, None, None),
            P(ROWS_AXES, None),
            rows,
            rows,
        ),
        out_specs=(P(ROWS_AXES, "env"), P("env")),
        check_vma=False,
    )
```

time: 151 us -> 132 us (0.87)
  blocking collectives: 113 us -> 53.7 us
  waiting for transfers between devices: 4.82 us -> 38.1 us
  between operations: 0.75 us -> 14.1 us
  starting transfers between devices: 21.1 us -> 14.4 us
    all_gather x1 -> x0, blocking collectives: 46.4 us -> none  [per_device(): every_rhs = lax.all_gather(partial_rhs, ROWS_AXES, axis=0, tiled=True)]
    all_gather x0 -> x1, waiting for transfers between devices: none -> 33.8 us  [per_device(): carried = lax.all_gather(carried, ('x', 'core'), axis=0)]
    all_to_all x1, blocking collectives: 28.8 us -> 15.8 us  [per_device(): terms = lax.all_to_all(terms, 'y', 0, 0, tiled=True)]
    all_to_all x1, starting transfers between devices: 11.7 us -> 6.82 us  [per_device(): weighted = lax.all_to_all(weighted, ('x', 'core', 'env'), 0, 0, tiled=True)]
    ppermute x1 -> x0, starting transfers between devices: 1.92 us -> none  [per_device(): received = lax.ppermute(sent, 'core', [(0, 1), (1, 0)])]
    ppermute x1 -> x0, waiting for transfers between devices: 1.88 us -> none  [per_device(): received = lax.ppermute(sent, 'core', [(0, 1), (1, 0)])]
    pallas_call x3 -> x2, Pallas kernels: 3.37 us -> 2.56 us  [the longest x1 2.13 us: per_device(): pl.pallas_call(metric_kernel, out_shape=(shape((group * planes, BLK, slab...]
    unnamed x15 -> x16, local copies, waits for them, and re-layouts: 4.64 us -> 5.22 us
  transfers between devices with their start and end apart: 4 -> 4, of which waited for: 2 -> 2; matrix products, arithmetic and copies ran while one was open for 0% -> 1% of each run, Pallas kernels for 0% -> 0%
where the time goes in v2:
time: 132 us; the launch traced here: 131 us
  blocking collectives  53.7 us (41%)
  waiting for transfers between devices  38.1 us (29%)
  starting transfers between devices  14.4 us (11%)
  between operations  14.1 us (11%)
  local copies, waits for them, and re-layouts  5.91 us (4%)
  Pallas kernels  5.02 us (4%)
    all_to_all x1, blocking collectives, per_device(): partial = lax.all_to_all(partial, 'env', 0, 0, tiled=True)  37.9 us
    all_gather x1, waiting for transfers between devices, per_device(): carried = lax.all_gather(carried, ('x', 'core'), axis=0)  33.8 us
    all_to_all x1, blocking collectives, per_device(): terms = lax.all_to_all(terms, 'y', 0, 0, tiled=True)  15.8 us
    all_to_all x1, starting transfers between devices, per_device(): weighted = lax.all_to_all(weighted, ('x', 'core', 'env'), 0, 0, tiled=True)  6.82 us
    ppermute x1, starting transfers between devices, per_device(): lax.ppermute(psi, ROWS_AXES, [(i, i + 1) for i in range(devices - 1)])  5.61 us
    unnamed x16, local copies, waits for them, and re-layouts  5.22 us
    ppermute x1, waiting for transfers between devices, per_device(): lax.ppermute(psi, ROWS_AXES, [(i + 1, i) for i in range(devices - 1)])  3.61 us
  transfers between devices with their start and end apart: 4, of which 2 were waited for; matrix products, arithmetic and copies ran while one was open for 1% of the time, Pallas kernels for 0%

profile of v2, /device:TPU:1, one launch (start us, length us, event | category | flops | bytes accessed | tf_op | source)
XLA Modules:
  0.0 131.3 jit_solution(13086379658265364102)
XLA Ops:
  7.2 0.0 copy-start.1
  7.2 1.2 copy-done.1
  8.4 0.0 copy-start.2
  8.4 1.0 copy-done.2
  9.4 0.0 copy-start.3
  9.4 1.0 copy-done.3
  10.5 0.7 copy-done.5
  11.1 1.7 %shard_map.86 = bf16[8,256,256]{2,1,0:T(8,128)(2,1)S(1)} custom-call(s32[8]{0:T(128)S(1)} %copy-done.5, bf16[256,1024]{1,0:T(8,128)(2,1)S(1)} %copy-done.2, bf16[256,1024]{1,0:T(8,128)(2,1)S(1)} %copy-done.3, bf16[256,2048]{1,0:T(8,128)(2,1)S(1)} %copy-done.1), custom_call_target="tpu_custom_call" | custom-call | tf_op jit(solution)/shard_map/pallas_call | solution.py:134
  12.8 37.9 %all_to_all.15.parts = bf16[8,256,256]{2,1,0:T(8,128)(2,1)S(1)} all-to-all(bf16[8,256,256]{2,1,0:T(8,128)(2,1)S(1)} %shard_map.86), channel_id=1, replica_groups=mesh['y'=8,'x'=4,'core'=2,'env'=8] {'env'}, dimensions={0} | all-to-all | bytes 2097152 | tf_op jit(solution)/shard_map/all_to_all | solution.py:148
  50.7 0.1 shard_map.87.own
  50.8 0.0 copy-start.7
  50.9 0.0 copy-start.4
  50.9 5.6 %collective-permute-start = (bf16[256,256]{1,0:T(8,128)(2,1)S(1)}, bf16[256,256]{1,0:T(8,128)(2,1)S(1)}, u32[]{:S(2)}, u32[]{:S(2)}) collective-permute-start(bf16[256,256]{1,0:T(8,128)(2,1)S(1)} %shard_map.87.own), channel_id=1, source_target_pairs={{0,8},{8,16},{16,24},{24,32},{32,40},{40,48},{48,56},{56,64},{64,7... | collective-permute-start | bytes 393224 | tf_op jit(solution)/shard_map/ppermute | solution.py:157
  56.5 1.9 %collective-permute-start.1 = (bf16[256,256]{1,0:T(8,128)(2,1)S(1)}, bf16[256,256]{1,0:T(8,128)(2,1)S(1)}, u32[]{:S(2)}, u32[]{:S(2)}) collective-permute-start(bf16[256,256]{1,0:T(8,128)(2,1)S(1)} %shard_map.87.own), channel_id=1, source_target_pairs={{8,0},{16,8},{24,16},{32,24},{40,32},{48,40},{56,48},{64,56},{72,6... | collective-permute-start | bytes 393224 | tf_op jit(solution)/shard_map/ppermute | solution.py:158
  58.4 0.0 copy-done.6
  58.4 0.2 copy.10
  58.6 0.4 reshape.13.metric
  59.0 0.0 copy-done.7
  59.0 0.1 copy.11.target
  59.1 0.0 collective-permute-done.before
  59.2 3.6 %collective-permute-done.1.after = bf16[256,256]{1,0:T(8,128)(2,1)S(1)} collective-permute-done((bf16[256,256]{1,0:T(8,128)(2,1)S(1)}, bf16[256,256]{1,0:T(8,128)(2,1)S(1)}, u32[]{:S(2)}, u32[]{:S(2)}) %collective-permute-start.1) | collective-permute-done | bytes 131104 | tf_op jit(solution)/shard_map/ppermute | solution.py:158
  62.8 0.0 copy-done.4
  62.8 2.1 %shard_map.88 = (bf16[64,32,256]{2,1,0:T(8,128)(2,1)}, bf16[272,256]{1,0:T(8,128)(2,1)}) custom-call(s32[8,8]{1,0:T(8,128)S(1)} %copy-done.4, bf16[256,256]{1,0:T(8,128)(2,1)S(1)} %collective-permute-done.before, bf16[256,256]{1,0:T(8,128)(2,1)S(1)} %shard_map.87.own, bf16[256,256]{1,0:T(8,128)(2,1)S(1)} %collective-permute-done.1.after, ...), custom_call_target="tpu_custom_call" | custom-call | tf_op jit(solution)/shard_map/pallas_call | solution.py:159
  64.9 6.8 %all-to-all-start.1 = ((bf16[64,32,256]{2,1,0:T(8,128)(2,1)}), bf16[64,32,256]{2,1,0:T(8,128)(2,1)S(1)}, u32[]{:S(2)}, u32[]{:S(2)}) async-start(bf16[64,32,256]{2,1,0:T(8,128)(2,1)} %get-tuple-element.6), calls=%async_computation.1 | async-start | bytes 2097152 | tf_op jit(solution)/shard_map/all_to_all | solution.py:168
  71.7 0.0 all-gather.3.cloned.1.call-start
  71.8 0.7 all-gather.3.cloned.1.call-update
  72.5 33.8 %all-gather.3.cloned.1.call-done = bf16[2176,256]{1,0:T(8,128)(2,1)} async-done(((bf16[272,256]{1,0:T(8,128)(2,1)}), bf16[2176,256]{1,0:T(8,128)(2,1)}) %all-gather.3.cloned.1.call-update) | async-done | bytes 1114128 | tf_op jit(solution)/shard_map/all_gather | solution.py:167
  106.3 0.0 all-to-all-done.1.weighted
  106.3 1.2 copy-done
  107.5 0.4 shard_map.89
  108.0 15.8 %all_to_all.16.parts = bf16[8,48,256]{2,1,0:T(8,128)(2,1)S(1)} all-to-all(bf16[8,48,256]{2,1,0:T(8,128)(2,1)S(1)} %shard_map.89), channel_id=1, replica_groups=mesh['y'=8,'x'=4,'core'=2,'env'=8] {'y'}, dimensions={0} | all-to-all | bytes 393216 | tf_op jit(solution)/shard_map/all_to_all | solution.py:176
  123.8 0.6 shard_map.90
  (3 shorter events, 0.0 us)
Async XLA Ops:
  7.2 1.2 copy-start.1
  8.4 1.0 copy-start.2
  9.4 1.0 copy-start.3
  10.5 0.7 copy-start.5
  50.7 7.7 %copy-start.6 = (bf16[8,8,32,32]{3,2,1,0:T(8,128)(2,1)S(1)}, bf16[8,8,32,32]{3,2,1,0:T(8,128)(2,1)}, u32[]{:S(2)}) copy-start(bf16[8,8,32,32]{3,2,1,0:T(8,128)(2,1)} %param.10) | copy-start | bytes 393220
  50.8 8.2 %copy-start.7 = (f32[256]{0:T(256)S(1)}, f32[256]{0:T(256)}, u32[]{:S(2)}) copy-start(f32[256]{0:T(256)} %param.13) | copy-start | bytes 3076
  50.9 11.9 %copy-start.4 = (s32[8,8]{1,0:T(8,128)S(1)}, s32[8,8]{1,0:T(8,128)}, u32[]{:S(2)}) copy-start(s32[8,8]{1,0:T(8,128)} %neighbours.1) | copy-start | bytes 772
  50.9 8.3 %collective-permute-start = (bf16[256,256]{1,0:T(8,128)(2,1)S(1)}, bf16[256,256]{1,0:T(8,128)(2,1)S(1)}, u32[]{:S(2)}, u32[]{:S(2)}) collective-permute-start(bf16[256,256]{1,0:T(8,128)(2,1)S(1)} %shard_map.87.own), channel_id=1, source_target_pairs={{0,8},{8,16},{16,24},{24,32},{32,40},{40,48},{48,56},{56,64},{64,7... | collective-permute-start | bytes 393224 | tf_op jit(solution)/shard_map/ppermute | solution.py:157
  56.5 6.3 %collective-permute-start.1 = (bf16[256,256]{1,0:T(8,128)(2,1)S(1)}, bf16[256,256]{1,0:T(8,128)(2,1)S(1)}, u32[]{:S(2)}, u32[]{:S(2)}) collective-permute-start(bf16[256,256]{1,0:T(8,128)(2,1)S(1)} %shard_map.87.own), channel_id=1, source_target_pairs={{8,0},{16,8},{24,16},{32,24},{40,32},{48,40},{56,48},{64,56},{72,6... | collective-permute-start | bytes 393224 | tf_op jit(solution)/shard_map/ppermute | solution.py:158
  64.9 41.4 %all-to-all-start.1 = ((bf16[64,32,256]{2,1,0:T(8,128)(2,1)}), bf16[64,32,256]{2,1,0:T(8,128)(2,1)S(1)}, u32[]{:S(2)}, u32[]{:S(2)}) async-start(bf16[64,32,256]{2,1,0:T(8,128)(2,1)} %get-tuple-element.6), calls=%async_computation.1 | async-start | bytes 2097152 | tf_op jit(solution)/shard_map/all_to_all | solution.py:168
  71.7 34.6 %all-gather.3.cloned.1.call-start = ((), (), s32[]{:S(2)}) async-start(), calls=%async_computation.3 | async-start | bytes 1253376 | tf_op jit(solution)/shard_map/all_gather | solution.py:167
  106.3 1.2 copy-start
Sparse Core Ops, SparseCore 0:
  74.7 31.5 all-gather.2

commit v3 on v2

--- a/solution.py
+++ b/solution.py
@@ -11,7 +11,8 @@
 VMEM = pl.BlockSpec(memory_space=pltpu.VMEM)
 SMEM = pl.BlockSpec(memory_space=pltpu.SMEM)
 ANY = pl.BlockSpec(memory_space=pl.ANY)
-PARAMS = pltpu.CompilerParams(vmem_limit_bytes=48 * 1024 * 1024)
+PARAMS = pltpu.CompilerParams(vmem_limit_bytes=40 * 1024 * 1024)
+WHOLE = pltpu.CompilerParams(vmem_limit_bytes=60 * 1024 * 1024)
 
 
 def dot(a, b, dims):
@@ -85,47 +86,62 @@
         lax.broadcasted_iota(jnp.int32, (rows, rows), 0) == lax.broadcasted_iota(jnp.int32, (rows, rows), 1)
     ).astype(jnp.bfloat16)
     turned = dot(weighted, unit, ((0,), (0,))).astype(jnp.bfloat16)
-    group = width // BLK
-    planes = out.shape[0] // group
-    for j in range(group):
+    pieces, chunk = out.shape[0], out.shape[1]
+    group = width // chunk
+    planes = pieces // group
+    for part in range(group):
         for z in range(planes):
-            out[j * planes + z] = turned[j * BLK:(j + 1) * BLK, :]
+            out[part * planes + z] = turned[part * chunk:(part + 1) * chunk, :]
     carried[0:rows] = own[...]
     carried[rows:] = high_low(total, carried.shape[0] - rows)
 
 
-def gram_kernel(weighted, carried, out):
-    group = carried.shape[0]
+def gram_kernel(neighbours, weighted, own, *rest):
+    carried, out = (own,) + rest[:-1], rest[-1]
+    group = len(carried)
     planes = weighted.shape[0] // group
-    rows, width = weighted.shape[2], carried.shape[2]
-    total = jnp.zeros((planes * BLK, width), jnp.float32)
+    chunk, rows, width = weighted.shape[1], weighted.shape[2], own.shape[1]
+    x = neighbours[0, 0] // (2 * (rows // BLK)) % group
+    total = jnp.zeros((planes * chunk, width), jnp.float32)
     rhs = jnp.zeros((1, width), jnp.float32)
-    for j in range(group):
-        turned = weighted[j * planes:(j + 1) * planes].reshape(planes * BLK, rows)
-        total = total + dot(turned, carried[j, 0:rows], ((1,), (0,)))
-        tail = carried[j, rows:].astype(jnp.float32)
+    for step, cells in enumerate(carried):
+        source = (x + group - step) % group
+        turned = weighted[pl.ds(source * planes, planes)].reshape(planes * chunk, rows)
+        total = total + dot(turned, cells[0:rows], ((1,), (0,)))
+        tail = cells[rows:].astype(jnp.float32)
         rhs = rhs + (tail[0:1] + tail[1:2])
-    extra = out.shape[1] - BLK
-    lines = high_low(rhs, extra)
-    for z in range(planes):
-        out[z, 0:BLK] = total[z * BLK:(z + 1) * BLK].astype(jnp.bfloat16)
-        out[z, BLK:] = lines
+    lines = high_low(rhs, EXTRA)
+    half = width // 2
+    lines = jnp.where(
+        lax.broadcasted_iota(jnp.int32, (EXTRA, half), 0) < 2,
+        lines[:, :half],
+        jnp.concatenate([lines[EXTRA - 2:, half:], lines[:EXTRA - 2, half:]], axis=0),
+    )
+    for part in range(out.shape[0]):
+        here = total[part * BLK:(part + 1) * BLK].astype(jnp.bfloat16)
+        out[part, 0:BLK] = here[:, :half]
+        out[part, BLK:2 * BLK] = here[:, half:]
+        out[part, 2 * BLK:] = lines
 
 
 def final_kernel(parts, gram, rhs, *, factor):
     total = parts[0].astype(jnp.float32)
     for part in range(1, parts.shape[0]):
         total = total + parts[part].astype(jnp.float32)
-    gram[...] = total[0:BLK] * factor
-    rhs[...] = (total[BLK:BLK + 1] + total[BLK + 1:BLK + 2]) * factor
+    half = total.shape[1]
+    gram[:, :half] = total[0:BLK] * factor
+    gram[:, half:] = total[BLK:2 * BLK] * factor
+    tail = 2 * BLK
+    rhs[:, :half] = (total[tail:tail + 1] + total[tail + 1:tail + 2]) * factor
+    rhs[:, half:] = (total[tail + 2:tail + 3] + total[tail + 3:tail + 4]) * factor
 
 
 def per_device(features, environments, projector, metric, neighbours, counts, target):
     f32, bf16 = jnp.float32, jnp.bfloat16
     slab, width = features.shape[0], environments.shape[0]
     planes, ys = lax.axis_size("env"), lax.axis_size("y")
-    group = lax.axis_size("x") * lax.axis_size("core")
-    devices = ys * group
+    group, cores = lax.axis_size("x"), lax.axis_size("core")
+    devices = ys * group * cores
     shape = jax.ShapeDtypeStruct
 
     metric_rows = metric.transpose(0, 2, 1, 3).reshape(slab, -1)
@@ -143,7 +159,7 @@
             pltpu.VMEM(projector.shape, bf16),
             pltpu.SemaphoreType.DMA((4,)),
         ],
-        compiler_params=PARAMS,
+        compiler_params=WHOLE,
     )(counts, features, environments, projector)
     partial = lax.all_to_all(partial, "env", 0, 0, tiled=True)
     psi = pl.pallas_call(
@@ -158,22 +174,25 @@
     after = lax.ppermute(psi, ROWS_AXES, [(i + 1, i) for i in range(devices - 1)])
     weighted, carried = pl.pallas_call(
         metric_kernel,
-        out_shape=(shape((group * planes, BLK, slab), bf16), shape((slab + EXTRA, width), bf16)),
+        out_shape=(shape((group * planes, width // group, slab), bf16), shape((slab + EXTRA, width), bf16)),
         in_specs=[SMEM, VMEM, VMEM, VMEM, VMEM, VMEM],
         out_specs=(VMEM, VMEM),
         scratch_shapes=[pltpu.VMEM((3 * slab, width), bf16)],
         compiler_params=PARAMS,
     )(neighbours, before, psi, after, metric_rows, target_column)
-    carried = lax.all_gather(carried, ("x", "core"), axis=0)
-    weighted = lax.all_to_all(weighted, ("x", "core", "env"), 0, 0, tiled=True)
+    shifted = [
+        lax.ppermute(carried, "x", [(i, (i + step) % group) for i in range(group)])
+        for step in range(1, group)
+    ]
+    weighted = lax.all_to_all(weighted, ("x", "env"), 0, 0, tiled=True)
     terms = pl.pallas_call(
         gram_kernel,
-        out_shape=shape((ys, BLK + EXTRA, width), bf16),
-        in_specs=[VMEM, VMEM],
+        out_shape=shape((ys * cores, 2 * BLK + EXTRA, width // 2), bf16),
+        in_specs=[SMEM] + [VMEM] * (1 + group),
         out_specs=VMEM,
         compiler_params=PARAMS,
-    )(weighted, carried)
-    terms = lax.all_to_all(terms, "y", 0, 0, tiled=True)
+    )(neighbours, weighted, carried, *shifted)
+    terms = lax.all_to_all(terms, ("y", "core"), 0, 0, tiled=True)
 
     def finish(parts, gram, rhs):
         final_kernel(parts, gram, rhs, factor=1.0 / (slab * devices) ** 0.5)

time: 132 us -> 113 us (0.86)
  waiting for transfers between devices: 38.1 us -> 19.2 us
  between operations: 14.1 us -> 0.76 us
  starting transfers between devices: 14.4 us -> 24.3 us
  blocking collectives: 53.7 us -> 59.9 us
  local copies, waits for them, and re-layouts: 5.91 us -> 1.37 us
  Pallas kernels: 5.02 us -> 7.21 us
    all_gather x1 -> x0, waiting for transfers between devices: 33.8 us -> none  [per_device(): carried = lax.all_gather(carried, ('x', 'core'), axis=0)]
    ppermute x0 -> x3, starting transfers between devices: none -> 10.5 us  [per_device(): lax.ppermute(carried, 'x', [(i, (i + step) % group) for i in range(group)])]
    all_to_all x1, waiting for transfers between devices: 0.01 us -> 9.28 us  [per_device(): weighted = lax.all_to_all(weighted, ('x', 'env'), 0, 0, tiled=True)]
    ppermute x0 -> x3, waiting for transfers between devices: none -> 6.97 us  [per_device(): lax.ppermute(carried, 'x', [(i, (i + step) % group) for i in range(group)])]
    all_to_all x1, blocking collectives: 15.8 us -> 21.8 us  [per_device(): terms = lax.all_to_all(terms, ('y', 'core'), 0, 0, tiled=True)]
    unnamed x16 -> x6, local copies, waits for them, and re-layouts: 5.22 us -> 0.68 us
    pallas_call x1, Pallas kernels: 1.68 us -> 3.25 us  [per_device(): pl.pallas_call(project_kernel, out_shape=shape((planes, slab, width), bf1...]
  transfers between devices with their start and end apart: 4 -> 6, of which waited for: 2 -> 4; matrix products, arithmetic and copies ran while one was open for 1% -> 1% of each run, Pallas kernels for 0% -> 0%
where the time goes in v3:
time: 113 us
  blocking collectives  59.9 us (53%)
  starting transfers between devices  24.3 us (22%)
  waiting for transfers between devices  19.2 us (17%)
  Pallas kernels  7.21 us (6%)
  local copies, waits for them, and re-layouts  1.37 us (1%)
    all_to_all x1, blocking collectives, per_device(): partial = lax.all_to_all(partial, 'env', 0, 0, tiled=True)  38.1 us
    all_to_all x1, blocking collectives, per_device(): terms = lax.all_to_all(terms, ('y', 'core'), 0, 0, tiled=True)  21.8 us
    ppermute x3, starting transfers between devices, per_device(): lax.ppermute(carried, 'x', [(i, (i + step) % group) for i in range(group)])  10.5 us
    all_to_all x1, waiting for transfers between devices, per_device(): weighted = lax.all_to_all(weighted, ('x', 'env'), 0, 0, tiled=True)  9.28 us
    ppermute x3, waiting for transfers between devices, per_device(): lax.ppermute(carried, 'x', [(i, (i + step) % group) for i in range(group)])  6.97 us
    all_to_all x1, starting transfers between devices, per_device(): weighted = lax.all_to_all(weighted, ('x', 'env'), 0, 0, tiled=True)  6.25 us
    ppermute x1, starting transfers between devices, per_device(): lax.ppermute(psi, ROWS_AXES, [(i, i + 1) for i in range(devices - 1)])  5.59 us
    pallas_call x1, Pallas kernels, per_device(): pl.pallas_call(project_kernel, out_shape=shape((planes, slab, width), bf1...  3.25 us
  transfers between devices with their start and end apart: 6, of which 4 were waited for; matrix products, arithmetic and copies ran while one was open for 1% of the time, Pallas kernels for 0%

profile of v3, /device:TPU:1, one launch (start us, length us, event | category | flops | bytes accessed | tf_op | source)
XLA Modules:
  0.0 112.8 jit_solution(9378417297890678326)
XLA Ops:
  0.6 3.3 %shard_map.86 = bf16[8,256,256]{2,1,0:T(8,128)(2,1)} custom-call(s32[8]{0:T(128)} %counts.1, bf16[256,1024]{1,0:T(8,128)(2,1)} %features.1, bf16[256,1024]{1,0:T(8,128)(2,1)} %environments.1, bf16[256,2048]{1,0:T(8,128)(2,1)} %projector.1), custom_call_target="tpu_custom_call" | custom-call | tf_op jit(solution)/shard_map/pallas_call | solution.py:150
  3.9 38.1 %all_to_all.15.parts = bf16[8,256,256]{2,1,0:T(8,128)(2,1)S(1)} all-to-all(bf16[8,256,256]{2,1,0:T(8,128)(2,1)} %shard_map.86), channel_id=1, replica_groups=mesh['y'=8,'x'=4,'core'=2,'env'=8] {'env'}, dimensions={0} | all-to-all | bytes 2097152 | tf_op jit(solution)/shard_map/all_to_all | solution.py:164
  42.0 0.0 copy-start.1
  42.0 0.1 shard_map.87.own
  42.1 5.6 %collective-permute-start = (bf16[256,256]{1,0:T(8,128)(2,1)S(1)}, bf16[256,256]{1,0:T(8,128)(2,1)S(1)}, u32[]{:S(2)}, u32[]{:S(2)}) collective-permute-start(bf16[256,256]{1,0:T(8,128)(2,1)S(1)} %shard_map.87.own), channel_id=1, source_target_pairs={{0,8},{8,16},{16,24},{24,32},{32,40},{40,48},{48,56},{56,64},{64,7... | collective-permute-start | bytes 393224 | tf_op jit(solution)/shard_map/ppermute | solution.py:173
  47.7 1.9 %collective-permute-start.1 = (bf16[256,256]{1,0:T(8,128)(2,1)S(1)}, bf16[256,256]{1,0:T(8,128)(2,1)S(1)}, u32[]{:S(2)}, u32[]{:S(2)}) collective-permute-start(bf16[256,256]{1,0:T(8,128)(2,1)S(1)} %shard_map.87.own), channel_id=1, source_target_pairs={{8,0},{16,8},{24,16},{32,24},{40,32},{48,40},{56,48},{64,56},{72,6... | collective-permute-start | bytes 393224 | tf_op jit(solution)/shard_map/ppermute | solution.py:174
  49.7 0.0 copy-done.1
  49.7 0.2 copy.10
  49.9 0.3 reshape.13.metric
  50.2 0.0 copy-start.2
  50.3 0.7 copy-done.2
  50.9 0.0 copy-start
  50.9 0.1 copy.11.target
  51.1 0.0 collective-permute-done.before
  51.1 2.9 %collective-permute-done.1.after = bf16[256,256]{1,0:T(8,128)(2,1)S(1)} collective-permute-done((bf16[256,256]{1,0:T(8,128)(2,1)S(1)}, bf16[256,256]{1,0:T(8,128)(2,1)S(1)}, u32[]{:S(2)}, u32[]{:S(2)}) %collective-permute-start.1) | collective-permute-done | bytes 131104 | tf_op jit(solution)/shard_map/ppermute | solution.py:174
  54.0 0.0 copy-done
  54.0 2.1 %shard_map.88 = (bf16[32,64,256]{2,1,0:T(8,128)(2,1)}, bf16[272,256]{1,0:T(8,128)(2,1)S(1)}) custom-call(s32[8,8]{1,0:T(8,128)S(1)} %copy-done, bf16[256,256]{1,0:T(8,128)(2,1)S(1)} %collective-permute-done.before, bf16[256,256]{1,0:T(8,128)(2,1)S(1)} %shard_map.87.own, bf16[256,256]{1,0:T(8,128)(2,1)S(1)} %collective-permute-done.1.after, ...), custom_call_target="tpu_custom_call" | custom-call | tf_op jit(solution)/shard_map/pallas_call | solution.py:175
  56.1 6.3 %all-to-all-start.1 = ((bf16[32,64,256]{2,1,0:T(8,128)(2,1)}), bf16[32,64,256]{2,1,0:T(8,128)(2,1)S(1)}, u32[]{:S(2)}, u32[]{:S(2)}) async-start(bf16[32,64,256]{2,1,0:T(8,128)(2,1)} %get-tuple-element.6), calls=%async_computation.1 | async-start | bytes 2097152 | tf_op jit(solution)/shard_map/all_to_all | solution.py:187
  62.4 3.1 %collective-permute-start.2 = (bf16[272,256]{1,0:T(8,128)(2,1)S(1)}, bf16[272,256]{1,0:T(8,128)(2,1)S(1)}, u32[]{:S(2)}, u32[]{:S(2)}) collective-permute-start(bf16[272,256]{1,0:T(8,128)(2,1)S(1)} %get-tuple-element.7.own), channel_id=1, source_target_pairs={{0,16},{16,32},{32,48},{48,0},{1,17},{17,33},{33,49},{49,1},{2,18}... | collective-permute-start | bytes 417800 | tf_op jit(solution)/shard_map/ppermute | solution.py:184
  65.6 4.3 %collective-permute-start.3 = (bf16[272,256]{1,0:T(8,128)(2,1)S(1)}, bf16[272,256]{1,0:T(8,128)(2,1)S(1)}, u32[]{:S(2)}, u32[]{:S(2)}) collective-permute-start(bf16[272,256]{1,0:T(8,128)(2,1)S(1)} %get-tuple-element.7.own), channel_id=1, source_target_pairs={{0,32},{16,48},{32,0},{48,16},{1,33},{17,49},{33,1},{49,17},{2,34}... | collective-permute-start | bytes 417800 | tf_op jit(solution)/shard_map/ppermute | solution.py:184
  69.9 3.1 %collective-permute-start.4 = (bf16[272,256]{1,0:T(8,128)(2,1)S(1)}, bf16[272,256]{1,0:T(8,128)(2,1)S(1)}, u32[]{:S(2)}, u32[]{:S(2)}) collective-permute-start(bf16[272,256]{1,0:T(8,128)(2,1)S(1)} %get-tuple-element.7.own), channel_id=1, source_target_pairs={{0,48},{16,0},{32,16},{48,32},{1,49},{17,1},{33,17},{49,33},{2,50}... | collective-permute-start | bytes 417800 | tf_op jit(solution)/shard_map/ppermute | solution.py:184
  73.0 0.0 collective-permute-done.2.rest_0_
  73.0 6.0 %collective-permute-done.3.rest_1_ = bf16[272,256]{1,0:T(8,128)(2,1)S(1)} collective-permute-done((bf16[272,256]{1,0:T(8,128)(2,1)S(1)}, bf16[272,256]{1,0:T(8,128)(2,1)S(1)}, u32[]{:S(2)}, u32[]{:S(2)}) %collective-permute-start.3) | collective-permute-done | bytes 139296 | tf_op jit(solution)/shard_map/ppermute | solution.py:184
  79.0 0.9 collective-permute-done.4.rest_2_
  79.9 9.3 %all-to-all-done.1.weighted = bf16[32,64,256]{2,1,0:T(8,128)(2,1)S(1)} async-done(((bf16[32,64,256]{2,1,0:T(8,128)(2,1)}), bf16[32,64,256]{2,1,0:T(8,128)(2,1)S(1)}, u32[]{:S(2)}, u32[]{:S(2)}) %all-to-all-start.1) | async-done | bytes 1048608 | tf_op jit(solution)/shard_map/all_to_all | solution.py:187
  89.2 1.0 shard_map.89
  90.3 21.8 %all_to_all.16.parts = bf16[16,80,128]{2,1,0:T(8,128)(2,1)S(1)} all-to-all(bf16[16,80,128]{2,1,0:T(8,128)(2,1)S(1)} %shard_map.89), channel_id=1, replica_groups=mesh['y'=8,'x'=4,'core'=2,'env'=8] {'y','core'}, dimensions={0} | all-to-all | bytes 655360 | tf_op jit(solution)/shard_map/all_to_all | solution.py:195
  112.1 0.7 shard_map.90
Async XLA Ops:
  42.0 7.7 %copy-start.1 = (bf16[8,8,32,32]{3,2,1,0:T(8,128)(2,1)S(1)}, bf16[8,8,32,32]{3,2,1,0:T(8,128)(2,1)}, u32[]{:S(2)}) copy-start(bf16[8,8,32,32]{3,2,1,0:T(8,128)(2,1)} %param.10) | copy-start | bytes 393220
  42.1 8.9 %collective-permute-start = (bf16[256,256]{1,0:T(8,128)(2,1)S(1)}, bf16[256,256]{1,0:T(8,128)(2,1)S(1)}, u32[]{:S(2)}, u32[]{:S(2)}) collective-permute-start(bf16[256,256]{1,0:T(8,128)(2,1)S(1)} %shard_map.87.own), channel_id=1, source_target_pairs={{0,8},{8,16},{16,24},{24,32},{32,40},{40,48},{48,56},{56,64},{64,7... | collective-permute-start | bytes 393224 | tf_op jit(solution)/shard_map/ppermute | solution.py:173
  47.7 6.3 %collective-permute-start.1 = (bf16[256,256]{1,0:T(8,128)(2,1)S(1)}, bf16[256,256]{1,0:T(8,128)(2,1)S(1)}, u32[]{:S(2)}, u32[]{:S(2)}) collective-permute-start(bf16[256,256]{1,0:T(8,128)(2,1)S(1)} %shard_map.87.own), channel_id=1, source_target_pairs={{8,0},{16,8},{24,16},{32,24},{40,32},{48,40},{56,48},{64,56},{72,6... | collective-permute-start | bytes 393224 | tf_op jit(solution)/shard_map/ppermute | solution.py:174
  50.2 0.7 copy-start.2
  50.9 3.1 %copy-start = (s32[8,8]{1,0:T(8,128)S(1)}, s32[8,8]{1,0:T(8,128)}, u32[]{:S(2)}) copy-start(s32[8,8]{1,0:T(8,128)} %neighbours.3) | copy-start | bytes 772
  56.1 33.1 %all-to-all-start.1 = ((bf16[32,64,256]{2,1,0:T(8,128)(2,1)}), bf16[32,64,256]{2,1,0:T(8,128)(2,1)S(1)}, u32[]{:S(2)}, u32[]{:S(2)}) async-start(bf16[32,64,256]{2,1,0:T(8,128)(2,1)} %get-tuple-element.6), calls=%async_computation.1 | async-start | bytes 2097152 | tf_op jit(solution)/shard_map/all_to_all | solution.py:187
  62.4 10.6 %collective-permute-start.2 = (bf16[272,256]{1,0:T(8,128)(2,1)S(1)}, bf16[272,256]{1,0:T(8,128)(2,1)S(1)}, u32[]{:S(2)}, u32[]{:S(2)}) collective-permute-start(bf16[272,256]{1,0:T(8,128)(2,1)S(1)} %get-tuple-element.7.own), channel_id=1, source_target_pairs={{0,16},{16,32},{32,48},{48,0},{1,17},{17,33},{33,49},{49,1},{2,18}... | collective-permute-start | bytes 417800 | tf_op jit(solution)/shard_map/ppermute | solution.py:184
  65.6 13.5 %collective-permute-start.3 = (bf16[272,256]{1,0:T(8,128)(2,1)S(1)}, bf16[272,256]{1,0:T(8,128)(2,1)S(1)}, u32[]{:S(2)}, u32[]{:S(2)}) collective-permute-start(bf16[272,256]{1,0:T(8,128)(2,1)S(1)} %get-tuple-element.7.own), channel_id=1, source_target_pairs={{0,32},{16,48},{32,0},{48,16},{1,33},{17,49},{33,1},{49,17},{2,34}... | collective-permute-start | bytes 417800 | tf_op jit(solution)/shard_map/ppermute | solution.py:184
  69.9 10.0 %collective-permute-start.4 = (bf16[272,256]{1,0:T(8,128)(2,1)S(1)}, bf16[272,256]{1,0:T(8,128)(2,1)S(1)}, u32[]{:S(2)}, u32[]{:S(2)}) collective-permute-start(bf16[272,256]{1,0:T(8,128)(2,1)S(1)} %get-tuple-element.7.own), channel_id=1, source_target_pairs={{0,48},{16,0},{32,16},{48,32},{1,49},{17,1},{33,17},{49,33},{2,50}... | collective-permute-start | bytes 417800 | tf_op jit(solution)/shard_map/ppermute | solution.py:184

commit v4 on v3

--- a/solution.py
+++ b/solution.py
@@ -7,6 +7,7 @@
 
 BLK = 32
 EXTRA = 16
+LANES = 128
 ROWS_AXES = ("y", "x", "core")
 VMEM = pl.BlockSpec(memory_space=pltpu.VMEM)
 SMEM = pl.BlockSpec(memory_space=pltpu.SMEM)
@@ -47,66 +48,78 @@
         out[part] = dot(masked, weights[:, cols], ((1,), (0,))).astype(jnp.bfloat16)
 
 
-def sum_kernel(parts, out):
+def sum_kernel(parts, psi, out):
     total = parts[0].astype(jnp.float32)
     for part in range(1, parts.shape[0]):
         total = total + parts[part].astype(jnp.float32)
-    out[...] = total.astype(jnp.bfloat16)
-
-
-def high_low(row, extra):
-    high = row.astype(jnp.bfloat16)
-    low = (row - high.astype(jnp.float32)).astype(jnp.bfloat16)
-    line = lax.broadcasted_iota(jnp.int32, (extra, row.shape[1]), 0)
-    return jnp.where(line == 0, high, jnp.where(line == 1, low, jnp.bfloat16(0)))
-
-
-def metric_kernel(neighbours, before, own, after, metric, target, out, carried, cells):
-    rows, width = own.shape
-    cells[0:rows] = before[...]
-    cells[rows:2 * rows] = own[...]
-    cells[2 * rows:3 * rows] = after[...]
-    first = neighbours[0, 0] - rows // BLK
-    total = jnp.zeros((1, width), jnp.float32)
-    blocks = []
-    for b in range(rows // BLK):
-        picked = jnp.concatenate(
-            [
-                cells[pl.ds(pl.multiple_of((neighbours[b, j] - first) * BLK, BLK), BLK), :]
-                for j in range(neighbours.shape[1])
-            ],
-            axis=0,
-        )
-        here = slice(b * BLK, (b + 1) * BLK)
-        weighted = dot(metric[here, :], picked, ((1,), (0,))).astype(jnp.bfloat16)
-        blocks.append(weighted)
-        total = total + jnp.sum(weighted.astype(jnp.float32) * target[here, :], axis=0, keepdims=True)
-    weighted = jnp.concatenate(blocks, axis=0)
+    total = total.astype(jnp.bfloat16)
+    psi[...] = total
+    rows, width = total.shape
     unit = (
         lax.broadcasted_iota(jnp.int32, (rows, rows), 0) == lax.broadcasted_iota(jnp.int32, (rows, rows), 1)
     ).astype(jnp.bfloat16)
-    turned = dot(weighted, unit, ((0,), (0,))).astype(jnp.bfloat16)
+    turned = dot(total, unit, ((0,), (0,))).astype(jnp.bfloat16)
     pieces, chunk = out.shape[0], out.shape[1]
     group = width // chunk
     planes = pieces // group
     for part in range(group):
         for z in range(planes):
             out[part * planes + z] = turned[part * chunk:(part + 1) * chunk, :]
-    carried[0:rows] = own[...]
-    carried[rows:] = high_low(total, carried.shape[0] - rows)
-
-
-def gram_kernel(neighbours, weighted, own, *rest):
+
+
+def high_low(row, extra):
+    high = row.astype(jnp.bfloat16)
+    low = (row - high.astype(jnp.float32)).astype(jnp.bfloat16)
+    line = lax.broadcasted_iota(jnp.int32, (extra, row.shape[1]), 0)
+    return jnp.where(line == 0, high, jnp.where(line == 1, low, jnp.bfloat16(0)))
+
+
+def spread_kernel(neighbours, psi, metric, target, before, own, after, cells):
+    rows, width = psi.shape
+    cells[...] = jnp.zeros_like(cells)
+    first = neighbours[0, 0] - rows // BLK
+    high = target[...].astype(jnp.bfloat16)
+    low = (target[...] - high.astype(jnp.float32)).astype(jnp.bfloat16)
+    lane = lax.broadcasted_iota(jnp.int32, (rows, LANES), 1)
+    column = jnp.where(lane == 0, high, jnp.where(lane == 1, low, jnp.bfloat16(0)))
+    wide = jnp.concatenate([psi[...], column], axis=1)
+    for b in range(rows // BLK):
+        here = slice(b * BLK, (b + 1) * BLK)
+        terms = dot(metric[here, :], wide[here, :], ((0,), (0,)))
+        for j in range(neighbours.shape[1]):
+            there = pl.ds(pl.multiple_of((neighbours[b, j] - first) * BLK, BLK), BLK)
+            cells[there, :] = cells[there, :] + terms[j * BLK:(j + 1) * BLK]
+    lane = lax.broadcasted_iota(jnp.int32, (rows, LANES), 1)
+    for out, start in ((before, 0), (after, 2 * rows)):
+        block = cells[start:start + rows]
+        weight = block[:, width:width + 1] + block[:, width + 1:width + 2]
+        high = weight.astype(jnp.bfloat16)
+        low = (weight - high.astype(jnp.float32)).astype(jnp.bfloat16)
+        out[:, :width] = block[:, :width].astype(jnp.bfloat16)
+        out[:, width:] = jnp.where(lane == 0, high, jnp.where(lane == 1, low, jnp.bfloat16(0)))
+    own[...] = cells[rows:2 * rows]
+
+
+def weighted_kernel(psi, own, left, right, carried):
+    rows, width = psi.shape
+    total = own[...] + left[...].astype(jnp.float32) + right[...].astype(jnp.float32)
+    carried[0:rows] = total[:, :width].astype(jnp.bfloat16)
+    weight = total[:, width:width + 1] + total[:, width + 1:width + 2]
+    rhs = jnp.sum(psi[...].astype(jnp.float32) * weight, axis=0, keepdims=True)
+    carried[rows:] = high_low(rhs, carried.shape[0] - rows)
+
+
+def gram_kernel(neighbours, pieces, own, *rest):
     carried, out = (own,) + rest[:-1], rest[-1]
     group = len(carried)
-    planes = weighted.shape[0] // group
-    chunk, rows, width = weighted.shape[1], weighted.shape[2], own.shape[1]
+    planes = pieces.shape[0] // group
+    chunk, rows, width = pieces.shape[1], pieces.shape[2], own.shape[1]
     x = neighbours[0, 0] // (2 * (rows // BLK)) % group
     total = jnp.zeros((planes * chunk, width), jnp.float32)
     rhs = jnp.zeros((1, width), jnp.float32)
     for step, cells in enumerate(carried):
         source = (x + group - step) % group
-        turned = weighted[pl.ds(source * planes, planes)].reshape(planes * chunk, rows)
+        turned = pieces[pl.ds(source * planes, planes)].reshape(planes * chunk, rows)
         total = total + dot(turned, cells[0:rows], ((1,), (0,)))
         tail = cells[rows:].astype(jnp.float32)
         rhs = rhs + (tail[0:1] + tail[1:2])
@@ -162,36 +175,43 @@
         compiler_params=WHOLE,
     )(counts, features, environments, projector)
     partial = lax.all_to_all(partial, "env", 0, 0, tiled=True)
-    psi = pl.pallas_call(
+    psi, turned = pl.pallas_call(
         sum_kernel,
-        out_shape=shape((slab, width), bf16),
+        out_shape=(shape((slab, width), bf16), shape((group * planes, width // group, slab), bf16)),
         in_specs=[VMEM],
+        out_specs=(VMEM, VMEM),
+        compiler_params=PARAMS,
+    )(partial)
+    wide = shape((slab, width + LANES), bf16)
+    to_before, own, to_after = pl.pallas_call(
+        spread_kernel,
+        out_shape=(wide, shape(wide.shape, f32), wide),
+        in_specs=[SMEM, VMEM, VMEM, VMEM],
+        out_specs=(VMEM, VMEM, VMEM),
+        scratch_shapes=[pltpu.VMEM((3 * slab, width + LANES), f32)],
+        compiler_params=PARAMS,
+    )(neighbours, psi, metric_rows, target_column)
+    from_after = lax.ppermute(to_before, ROWS_AXES, [(i + 1, i) for i in range(devices - 1)])
+    from_before = lax.ppermute(to_after, ROWS_AXES, [(i, i + 1) for i in range(devices - 1)])
+    turned = lax.all_to_all(turned, ("x", "env"), 0, 0, tiled=True)
+    carried = pl.pallas_call(
+        weighted_kernel,
+        out_shape=shape((slab + EXTRA, width), bf16),
+        in_specs=[VMEM] * 4,
         out_specs=VMEM,
         compiler_params=PARAMS,
-    )(partial)
-
-    before = lax.ppermute(psi, ROWS_AXES, [(i, i + 1) for i in range(devices - 1)])
-    after = lax.ppermute(psi, ROWS_AXES, [(i + 1, i) for i in range(devices - 1)])
-    weighted, carried = pl.pallas_call(
-        metric_kernel,
-        out_shape=(shape((group * planes, width // group, slab), bf16), shape((slab + EXTRA, width), bf16)),
-        in_specs=[SMEM, VMEM, VMEM, VMEM, VMEM, VMEM],
-        out_specs=(VMEM, VMEM),
-        scratch_shapes=[pltpu.VMEM((3 * slab, width), bf16)],
-        compiler_params=PARAMS,
-    )(neighbours, before, psi, after, metric_rows, target_column)
+    )(psi, own, from_before, from_after)
     shifted = [
         lax.ppermute(carried, "x", [(i, (i + step) % group) for i in range(group)])
         for step in range(1, group)
     ]
-    weighted = lax.all_to_all(weighted, ("x", "env"), 0, 0, tiled=True)
     terms = pl.pallas_call(
         gram_kernel,
         out_shape=shape((ys * cores, 2 * BLK + EXTRA, width // 2), bf16),
         in_specs=[SMEM] + [VMEM] * (1 + group),
         out_specs=VMEM,
         compiler_params=PARAMS,
-    )(neighbours, weighted, carried, *shifted)
+    )(neighbours, turned, carried, *shifted)
     terms = lax.all_to_all(terms, ("y", "core"), 0, 0, tiled=True)
 
     def finish(parts, gram, rhs):

time: 113 us -> 104 us (0.920)
  waiting for transfers between devices: 19.2 us -> 10.8 us
  starting transfers between devices: 24.3 us -> 22.8 us
    all_to_all x1, waiting for transfers between devices: 9.28 us -> 0.01 us  [per_device(): turned = lax.all_to_all(turned, ('x', 'env'), 0, 0, tiled=True)]
    ppermute x2, waiting for transfers between devices: 2.94 us -> 7.1 us  [the longest x1 5.33 us: per_device(): lax.ppermute(to_before, ROWS_AXES, [(i + 1, i) for i in range(devices - 1)])]
    ppermute x3, waiting for transfers between devices: 6.97 us -> 3.71 us  [per_device(): lax.ppermute(carried, 'x', [(i, (i + step) % group) for i in range(group)])]
    pallas_call x2 -> x3, Pallas kernels: 2.25 us -> 3.11 us  [the longest x1 1.56 us: per_device(): pl.pallas_call(spread_kernel, out_shape=(wide, shape(wide.shape, f32), wi...]
  transfers between devices with their start and end apart: 6 -> 6, of which waited for: 4 -> 4; matrix products, arithmetic and copies ran while one was open for 1% -> 1% of each run, Pallas kernels for 0% -> 2%
where the time goes in v4:
time: 104 us; the launch traced here: 103 us
  blocking collectives  59.1 us (57%)
  starting transfers between devices  22.8 us (22%)
  waiting for transfers between devices  10.8 us (10%)
  Pallas kernels  8.07 us (8%)
  local copies, waits for them, and re-layouts  1.92 us (2%)
    all_to_all x1, blocking collectives, per_device(): partial = lax.all_to_all(partial, 'env', 0, 0, tiled=True)  38.1 us
    all_to_all x1, blocking collectives, per_device(): terms = lax.all_to_all(terms, ('y', 'core'), 0, 0, tiled=True)  21 us
    ppermute x3, starting transfers between devices, per_device(): lax.ppermute(carried, 'x', [(i, (i + step) % group) for i in range(group)])  10.3 us
    all_to_all x1, starting transfers between devices, per_device(): turned = lax.all_to_all(turned, ('x', 'env'), 0, 0, tiled=True)  5.62 us
    ppermute x1, waiting for transfers between devices, per_device(): lax.ppermute(to_before, ROWS_AXES, [(i + 1, i) for i in range(devices - 1)])  5.33 us
    ppermute x1, starting transfers between devices, per_device(): lax.ppermute(to_after, ROWS_AXES, [(i, i + 1) for i in range(devices - 1)])  4.96 us
    ppermute x3, waiting for transfers between devices, per_device(): lax.ppermute(carried, 'x', [(i, (i + step) % group) for i in range(group)])  3.71 us
    pallas_call x1, Pallas kernels, per_device(): pl.pallas_call(project_kernel, out_shape=shape((planes, slab, width), bf1...  3.26 us
  transfers between devices with their start and end apart: 6, of which 4 were waited for; matrix products, arithmetic and copies ran while one was open for 1% of the time, Pallas kernels for 2%

profile of v4, /device:TPU:1, one launch (start us, length us, event | category | flops | bytes accessed | tf_op | source)
XLA Modules:
  0.0 103.4 jit_solution(15668301181956375125)
XLA Ops:
  0.6 3.3 %shard_map.86 = bf16[8,256,256]{2,1,0:T(8,128)(2,1)} custom-call(s32[8]{0:T(128)} %counts.1, bf16[256,1024]{1,0:T(8,128)(2,1)} %features.1, bf16[256,1024]{1,0:T(8,128)(2,1)} %environments.1, bf16[256,2048]{1,0:T(8,128)(2,1)} %projector.1), custom_call_target="tpu_custom_call" | custom-call | tf_op jit(solution)/shard_map/pallas_call | solution.py:163
  3.9 38.1 %all_to_all.15.parts = bf16[8,256,256]{2,1,0:T(8,128)(2,1)S(1)} all-to-all(bf16[8,256,256]{2,1,0:T(8,128)(2,1)} %shard_map.86), channel_id=1, replica_groups=mesh['y'=8,'x'=4,'core'=2,'env'=8] {'env'}, dimensions={0} | all-to-all | bytes 2097152 | tf_op jit(solution)/shard_map/all_to_all | solution.py:177
  42.0 1.3 %shard_map.87 = (bf16[256,256]{1,0:T(8,128)(2,1)S(1)}, bf16[32,64,256]{2,1,0:T(8,128)(2,1)}) custom-call(bf16[8,256,256]{2,1,0:T(8,128)(2,1)S(1)} %all_to_all.15.parts), custom_call_target="tpu_custom_call" | custom-call | tf_op jit(solution)/shard_map/pallas_call | solution.py:178
  43.3 0.0 copy-start.1
  43.3 5.6 %all-to-all-start.1 = ((bf16[32,64,256]{2,1,0:T(8,128)(2,1)}), bf16[32,64,256]{2,1,0:T(8,128)(2,1)S(1)}, u32[]{:S(2)}, u32[]{:S(2)}) async-start(bf16[32,64,256]{2,1,0:T(8,128)(2,1)} %get-tuple-element.9), calls=%async_computation.1 | async-start | bytes 2097152 | tf_op jit(solution)/shard_map/all_to_all | solution.py:196
  49.0 0.0 copy-done.1
  49.0 0.2 copy.10
  49.2 0.4 reshape.13.metric
  49.6 0.0 copy-start.2
  49.6 0.7 copy-done.2
  50.2 0.0 copy-start
  50.2 0.1 copy.11.target
  50.4 0.5 copy-done
  50.9 1.6 %shard_map.88 = (bf16[256,384]{1,0:T(8,128)(2,1)S(1)}, f32[256,384]{1,0:T(8,128)S(1)}, bf16[256,384]{1,0:T(8,128)(2,1)S(1)}) custom-call(s32[8,8]{1,0:T(8,128)S(1)} %copy-done, bf16[256,256]{1,0:T(8,128)(2,1)S(1)} %get-tuple-element.10.psi, bf16[256,256]{1,0:T(8,128)(2,1)S(1)} %reshape.13.metric, f32[256,1]{1,0:T(8,128)S(1)} %copy.11.target), custom_call_target="tpu_custom_call" | custom-call | tf_op jit(solution)/shard_map/pallas_call | solution.py:186
  52.5 5.0 %collective-permute-start = (bf16[256,384]{1,0:T(8,128)(2,1)S(1)}, bf16[256,384]{1,0:T(8,128)(2,1)S(1)}, u32[]{:S(2)}, u32[]{:S(2)}) collective-permute-start(bf16[256,384]{1,0:T(8,128)(2,1)S(1)} %get-tuple-element.12), channel_id=1, source_target_pairs={{0,8},{8,16},{16,24},{24,32},{32,40},{40,48},{48,56},{56,64},{64,7... | collective-permute-start | bytes 589832 | tf_op jit(solution)/shard_map/ppermute | solution.py:195
  57.5 1.9 %collective-permute-start.1 = (bf16[256,384]{1,0:T(8,128)(2,1)S(1)}, bf16[256,384]{1,0:T(8,128)(2,1)S(1)}, u32[]{:S(2)}, u32[]{:S(2)}) collective-permute-start(bf16[256,384]{1,0:T(8,128)(2,1)S(1)} %get-tuple-element.13), channel_id=1, source_target_pairs={{8,0},{16,8},{24,16},{32,24},{40,32},{48,40},{56,48},{64,56},{72,6... | collective-permute-start | bytes 589832 | tf_op jit(solution)/shard_map/ppermute | solution.py:194
  59.4 1.8 %collective-permute-done.left = bf16[256,384]{1,0:T(8,128)(2,1)S(1)} collective-permute-done((bf16[256,384]{1,0:T(8,128)(2,1)S(1)}, bf16[256,384]{1,0:T(8,128)(2,1)S(1)}, u32[]{:S(2)}, u32[]{:S(2)}) %collective-permute-start) | collective-permute-done | bytes 196640 | tf_op jit(solution)/shard_map/ppermute | solution.py:195
  61.2 5.3 %collective-permute-done.1.right = bf16[256,384]{1,0:T(8,128)(2,1)S(1)} collective-permute-done((bf16[256,384]{1,0:T(8,128)(2,1)S(1)}, bf16[256,384]{1,0:T(8,128)(2,1)S(1)}, u32[]{:S(2)}, u32[]{:S(2)}) %collective-permute-start.1) | collective-permute-done | bytes 196640 | tf_op jit(solution)/shard_map/ppermute | solution.py:194
  66.5 0.2 shard_map.89.own
  66.7 3.1 %collective-permute-start.2 = (bf16[272,256]{1,0:T(8,128)(2,1)S(1)}, bf16[272,256]{1,0:T(8,128)(2,1)S(1)}, u32[]{:S(2)}, u32[]{:S(2)}) collective-permute-start(bf16[272,256]{1,0:T(8,128)(2,1)S(1)} %shard_map.89.own), channel_id=1, source_target_pairs={{0,16},{16,32},{32,48},{48,0},{1,17},{17,33},{33,49},{49,1},{2,18}... | collective-permute-start | bytes 417800 | tf_op jit(solution)/shard_map/ppermute | solution.py:205
  69.8 5.0 %collective-permute-start.3 = (bf16[272,256]{1,0:T(8,128)(2,1)S(1)}, bf16[272,256]{1,0:T(8,128)(2,1)S(1)}, u32[]{:S(2)}, u32[]{:S(2)}) collective-permute-start(bf16[272,256]{1,0:T(8,128)(2,1)S(1)} %shard_map.89.own), channel_id=1, source_target_pairs={{0,32},{16,48},{32,0},{48,16},{1,33},{17,49},{33,1},{49,17},{2,34}... | collective-permute-start | bytes 417800 | tf_op jit(solution)/shard_map/ppermute | solution.py:205
  74.8 2.2 %collective-permute-start.4 = (bf16[272,256]{1,0:T(8,128)(2,1)S(1)}, bf16[272,256]{1,0:T(8,128)(2,1)S(1)}, u32[]{:S(2)}, u32[]{:S(2)}) collective-permute-start(bf16[272,256]{1,0:T(8,128)(2,1)S(1)} %shard_map.89.own), channel_id=1, source_target_pairs={{0,48},{16,0},{32,16},{48,32},{1,49},{17,1},{33,17},{49,33},{2,50}... | collective-permute-start | bytes 417800 | tf_op jit(solution)/shard_map/ppermute | solution.py:205
  77.0 0.0 collective-permute-done.2.rest_0_
  77.0 2.9 %collective-permute-done.3.rest_1_ = bf16[272,256]{1,0:T(8,128)(2,1)S(1)} collective-permute-done((bf16[272,256]{1,0:T(8,128)(2,1)S(1)}, bf16[272,256]{1,0:T(8,128)(2,1)S(1)}, u32[]{:S(2)}, u32[]{:S(2)}) %collective-permute-start.3) | collective-permute-done | bytes 139296 | tf_op jit(solution)/shard_map/ppermute | solution.py:205
  79.9 0.8 collective-permute-done.4.rest_2_
  80.7 0.0 all-to-all-done.1.pieces
  80.7 1.0 %shard_map.90 = bf16[16,80,128]{2,1,0:T(8,128)(2,1)S(1)} custom-call(s32[8,8]{1,0:T(8,128)S(1)} %copy-done, bf16[32,64,256]{2,1,0:T(8,128)(2,1)S(1)} %all-to-all-done.1.pieces, bf16[272,256]{1,0:T(8,128)(2,1)S(1)} %shard_map.89.own, bf16[272,256]{1,0:T(8,128)(2,1)S(1)} %collective-permute-done.2.rest_0_, ...), custom_call_target="tpu_custom_call" | custom-call | tf_op jit(solution)/shard_map/pallas_call | solution.py:208
  81.8 21.0 %all_to_all.16.parts = bf16[16,80,128]{2,1,0:T(8,128)(2,1)S(1)} all-to-all(bf16[16,80,128]{2,1,0:T(8,128)(2,1)S(1)} %shard_map.90), channel_id=1, replica_groups=mesh['y'=8,'x'=4,'core'=2,'env'=8] {'y','core'}, dimensions={0} | all-to-all | bytes 655360 | tf_op jit(solution)/shard_map/all_to_all | solution.py:215
  102.7 0.7 shard_map.91
Async XLA Ops:
  43.3 5.6 %copy-start.1 = (bf16[8,8,32,32]{3,2,1,0:T(8,128)(2,1)S(1)}, bf16[8,8,32,32]{3,2,1,0:T(8,128)(2,1)}, u32[]{:S(2)}) copy-start(bf16[8,8,32,32]{3,2,1,0:T(8,128)(2,1)} %param.10) | copy-start | bytes 393220
  43.3 37.4 %all-to-all-start.1 = ((bf16[32,64,256]{2,1,0:T(8,128)(2,1)}), bf16[32,64,256]{2,1,0:T(8,128)(2,1)S(1)}, u32[]{:S(2)}, u32[]{:S(2)}) async-start(bf16[32,64,256]{2,1,0:T(8,128)(2,1)} %get-tuple-element.9), calls=%async_computation.1 | async-start | bytes 2097152 | tf_op jit(solution)/shard_map/all_to_all | solution.py:196
  49.6 0.7 copy-start.2
  50.2 0.7 copy-start
  52.5 8.7 %collective-permute-start = (bf16[256,384]{1,0:T(8,128)(2,1)S(1)}, bf16[256,384]{1,0:T(8,128)(2,1)S(1)}, u32[]{:S(2)}, u32[]{:S(2)}) collective-permute-start(bf16[256,384]{1,0:T(8,128)(2,1)S(1)} %get-tuple-element.12), channel_id=1, source_target_pairs={{0,8},{8,16},{16,24},{24,32},{32,40},{40,48},{48,56},{56,64},{64,7... | collective-permute-start | bytes 589832 | tf_op jit(solution)/shard_map/ppermute | solution.py:195
  57.5 9.0 %collective-permute-start.1 = (bf16[256,384]{1,0:T(8,128)(2,1)S(1)}, bf16[256,384]{1,0:T(8,128)(2,1)S(1)}, u32[]{:S(2)}, u32[]{:S(2)}) collective-permute-start(bf16[256,384]{1,0:T(8,128)(2,1)S(1)} %get-tuple-element.13), channel_id=1, source_target_pairs={{8,0},{16,8},{24,16},{32,24},{40,32},{48,40},{56,48},{64,56},{72,6... | collective-permute-start | bytes 589832 | tf_op jit(solution)/shard_map/ppermute | solution.py:194
  66.7 10.3 %collective-permute-start.2 = (bf16[272,256]{1,0:T(8,128)(2,1)S(1)}, bf16[272,256]{1,0:T(8,128)(2,1)S(1)}, u32[]{:S(2)}, u32[]{:S(2)}) collective-permute-start(bf16[272,256]{1,0:T(8,128)(2,1)S(1)} %shard_map.89.own), channel_id=1, source_target_pairs={{0,16},{16,32},{32,48},{48,0},{1,17},{17,33},{33,49},{49,1},{2,18}... | collective-permute-start | bytes 417800 | tf_op jit(solution)/shard_map/ppermute | solution.py:205
  69.8 10.1 %collective-permute-start.3 = (bf16[272,256]{1,0:T(8,128)(2,1)S(1)}, bf16[272,256]{1,0:T(8,128)(2,1)S(1)}, u32[]{:S(2)}, u32[]{:S(2)}) collective-permute-start(bf16[272,256]{1,0:T(8,128)(2,1)S(1)} %shard_map.89.own), channel_id=1, source_target_pairs={{0,32},{16,48},{32,0},{48,16},{1,33},{17,49},{33,1},{49,17},{2,34}... | collective-permute-start | bytes 417800 | tf_op jit(solution)/shard_map/ppermute | solution.py:205
  74.8 5.9 %collective-permute-start.4 = (bf16[272,256]{1,0:T(8,128)(2,1)S(1)}, bf16[272,256]{1,0:T(8,128)(2,1)S(1)}, u32[]{:S(2)}, u32[]{:S(2)}) collective-permute-start(bf16[272,256]{1,0:T(8,128)(2,1)S(1)} %shard_map.89.own), channel_id=1, source_target_pairs={{0,48},{16,0},{32,16},{48,32},{1,49},{17,1},{33,17},{49,33},{2,50}... | collective-permute-start | bytes 417800 | tf_op jit(solution)/shard_map/ppermute | solution.py:205

commit v5 on v4

--- a/solution.py
+++ b/solution.py
@@ -20,7 +20,9 @@
     return lax.dot_general(a, b, (dims, ((), ())), preferred_element_type=jnp.float32)
 
 
-def project_kernel(counts, features, environments, projector, out, slots_used, left, right, weights, sems):
+def project_kernel(
+    counts, features, environments, projector, out, slots_used, left, right, weights, parts, sems, sent
+):
     copies = [
         pltpu.make_async_copy(source, target, sems.at[i])
         for i, (source, target) in enumerate(
@@ -45,10 +47,14 @@
     copies[3].wait()
     for part in range(out.shape[0]):
         cols = slice(part * width, (part + 1) * width)
-        out[part] = dot(masked, weights[:, cols], ((1,), (0,))).astype(jnp.bfloat16)
-
-
-def sum_kernel(parts, psi, out):
+        parts[part] = dot(masked, weights[:, cols], ((1,), (0,))).astype(jnp.bfloat16)
+        pltpu.make_async_copy(parts.at[part], out.at[part], sent.at[part]).start()
+    for part in range(out.shape[0]):
+        pltpu.make_async_copy(parts.at[part], out.at[part], sent.at[part]).wait()
+
+
+def sum_kernel(parts, metric, target, psi, out):
+    del metric, target
     total = parts[0].astype(jnp.float32)
     for part in range(1, parts.shape[0]):
         total = total + parts[part].astype(jnp.float32)
@@ -110,7 +116,7 @@
 
 
 def gram_kernel(neighbours, pieces, own, *rest):
-    carried, out = (own,) + rest[:-1], rest[-1]
+    carried, (kept, sent, block) = (own,) + rest[:-3], rest[-3:]
     group = len(carried)
     planes = pieces.shape[0] // group
     chunk, rows, width = pieces.shape[1], pieces.shape[2], own.shape[1]
@@ -125,16 +131,38 @@
         rhs = rhs + (tail[0:1] + tail[1:2])
     lines = high_low(rhs, EXTRA)
     half = width // 2
-    lines = jnp.where(
-        lax.broadcasted_iota(jnp.int32, (EXTRA, half), 0) < 2,
-        lines[:, :half],
-        jnp.concatenate([lines[EXTRA - 2:, half:], lines[:EXTRA - 2, half:]], axis=0),
-    )
+    block[...] = total
+    core = neighbours[0, 0] // (rows // BLK) % 2
+    row = lax.broadcasted_iota(jnp.int32, (EXTRA, half), 0)
+    tail = jnp.where(row == 0, rhs[:, :half], jnp.where(row == 2, rhs[:, half:], 0.0))
+    for part in range(kept.shape[0]):
+        here = block[pl.ds(pl.multiple_of((2 * part + core) * BLK, BLK), BLK), :]
+        kept[part, 0:BLK] = here[:, :half]
+        kept[part, BLK:2 * BLK] = here[:, half:]
+        kept[part, 2 * BLK:] = tail
+        here = block[pl.ds(pl.multiple_of((2 * part + 1 - core) * BLK, BLK), BLK), :].astype(jnp.bfloat16)
+        sent[part, 0:BLK] = here[:, :half]
+        sent[part, BLK:2 * BLK] = here[:, half:]
+        sent[part, 2 * BLK:] = split_rows(tail)
+
+
+def split_rows(tail):
+    high = tail.astype(jnp.bfloat16)
+    low = (tail - high.astype(jnp.float32)).astype(jnp.bfloat16)
+    low = jnp.concatenate([low[-1:], low[:-1]], axis=0)
+    row = lax.broadcasted_iota(jnp.int32, tail.shape, 0)
+    return jnp.where(row % 2 == 0, high, low)
+
+
+def add_kernel(kept, received, out):
+    total = kept[...] + received[...].astype(jnp.float32)
+    tail = total[0, 2 * BLK:]
+    row = lax.broadcasted_iota(jnp.int32, tail.shape, 0)
+    first, second = tail[0:1] + tail[1:2], tail[2:3] + tail[3:4]
+    tail = split_rows(jnp.where(row == 0, first, jnp.where(row == 2, second, 0.0)))
     for part in range(out.shape[0]):
-        here = total[part * BLK:(part + 1) * BLK].astype(jnp.bfloat16)
-        out[part, 0:BLK] = here[:, :half]
-        out[part, BLK:2 * BLK] = here[:, half:]
-        out[part, 2 * BLK:] = lines
+        out[part, 0:2 * BLK] = total[part, 0:2 * BLK].astype(jnp.bfloat16)
+        out[part, 2 * BLK:] = tail
 
 
 def final_kernel(parts, gram, rhs, *, factor):
@@ -164,13 +192,15 @@
         project_kernel,
         out_shape=shape((planes, slab, width), bf16),
         in_specs=[ANY] * 4,
-        out_specs=VMEM,
+        out_specs=ANY,
         scratch_shapes=[
             pltpu.SMEM(counts.shape, jnp.int32),
             pltpu.VMEM(features.shape, bf16),
             pltpu.VMEM(environments.shape, bf16),
             pltpu.VMEM(projector.shape, bf16),
+            pltpu.VMEM((planes, slab, width), bf16),
             pltpu.SemaphoreType.DMA((4,)),
+            pltpu.SemaphoreType.DMA((planes,)),
         ],
         compiler_params=WHOLE,
     )(counts, features, environments, projector)
@@ -178,10 +208,10 @@
     psi, turned = pl.pallas_call(
         sum_kernel,
         out_shape=(shape((slab, width), bf16), shape((group * planes, width // group, slab), bf16)),
-        in_specs=[VMEM],
+        in_specs=[VMEM] * 3,
         out_specs=(VMEM, VMEM),
         compiler_params=PARAMS,
-    )(partial)
+    )(partial, metric_rows, target_column)
     wide = shape((slab, width + LANES), bf16)
     to_before, own, to_after = pl.pallas_call(
         spread_kernel,
@@ -205,14 +235,24 @@
         lax.ppermute(carried, "x", [(i, (i + step) % group) for i in range(group)])
         for step in range(1, group)
     ]
+    parts = (ys, 2 * BLK + EXTRA, width // 2)
+    kept, sent = pl.pallas_call(
+        gram_kernel,
+        out_shape=(shape(parts, f32), shape(parts, bf16)),
+        in_specs=[SMEM] + [VMEM] * (1 + group),
+        out_specs=(VMEM, VMEM),
+        scratch_shapes=[pltpu.VMEM((planes * width // group, width), f32)],
+        compiler_params=PARAMS,
+    )(neighbours, turned, carried, *shifted)
+    received = lax.ppermute(sent, "core", [(0, 1), (1, 0)])
     terms = pl.pallas_call(
-        gram_kernel,
-        out_shape=shape((ys * cores, 2 * BLK + EXTRA, width // 2), bf16),
-        in_specs=[SMEM] + [VMEM] * (1 + group),
+        add_kernel,
+        out_shape=shape(parts, bf16),
+        in_specs=[VMEM, VMEM],
         out_specs=VMEM,
         compiler_params=PARAMS,
-    )(neighbours, turned, carried, *shifted)
-    terms = lax.all_to_all(terms, ("y", "core"), 0, 0, tiled=True)
+    )(kept, received)
+    terms = lax.all_to_all(terms, "y", 0, 0, tiled=True)
 
     def finish(parts, gram, rhs):
         final_kernel(parts, gram, rhs, factor=1.0 / (slab * devices) ** 0.5)

time: 104 us -> 102 us (0.981)
  blocking collectives: 59.1 us -> 15.3 us
  waiting for transfers between devices: 10.8 us -> 43.1 us
  starting transfers between devices: 22.8 us -> 33.4 us
    all_to_all x2 -> x1, blocking collectives: 59.1 us -> 15.3 us  [per_device(): terms = lax.all_to_all(terms, 'y', 0, 0, tiled=True)]
    all_to_all x0 -> x1, waiting for transfers between devices: none -> 27.8 us  [per_device(): partial = lax.all_to_all(partial, 'env', 0, 0, tiled=True)]
    all_to_all x0 -> x1, starting transfers between devices: none -> 11 us  [per_device(): partial = lax.all_to_all(partial, 'env', 0, 0, tiled=True)]
    ppermute x3, waiting for transfers between devices: 3.71 us -> 7.17 us  [per_device(): lax.ppermute(carried, 'x', [(i, (i + step) % group) for i in range(group)])]
    ppermute x0 -> x1, starting transfers between devices: none -> 2.3 us  [per_device(): received = lax.ppermute(sent, 'core', [(0, 1), (1, 0)])]
    all_to_all x1, starting transfers between devices: 5.62 us -> 4.54 us  [per_device(): turned = lax.all_to_all(turned, ('x', 'env'), 0, 0, tiled=True)]
  transfers between devices with their start and end apart: 6 -> 8, of which waited for: 4 -> 7; matrix products, arithmetic and copies ran while one was open for 1% -> 1% of each run, Pallas kernels for 2% -> 2%
where the time goes in v5:
time: 102 us
  waiting for transfers between devices  43.1 us (42%)
  starting transfers between devices  33.4 us (33%)
  blocking collectives  15.3 us (15%)
  Pallas kernels  7.97 us (8%)
  local copies, waits for them, and re-layouts  1.38 us (1%)
    all_to_all x1, waiting for transfers between devices, per_device(): partial = lax.all_to_all(partial, 'env', 0, 0, tiled=True)  27.8 us
    all_to_all x1, blocking collectives, per_device(): terms = lax.all_to_all(terms, 'y', 0, 0, tiled=True)  15.3 us
    all_to_all x1, starting transfers between devices, per_device(): partial = lax.all_to_all(partial, 'env', 0, 0, tiled=True)  11 us
    ppermute x3, starting transfers between devices, per_device(): lax.ppermute(carried, 'x', [(i, (i + step) % group) for i in range(group)])  9.53 us
    ppermute x3, waiting for transfers between devices, per_device(): lax.ppermute(carried, 'x', [(i, (i + step) % group) for i in range(group)])  7.17 us
    all_to_all x1, starting transfers between devices, per_device(): turned = lax.all_to_all(turned, ('x', 'env'), 0, 0, tiled=True)  4.54 us
    ppermute x1, waiting for transfers between devices, per_device(): lax.ppermute(to_before, ROWS_AXES, [(i + 1, i) for i in range(devices - 1)])  4.49 us
    ppermute x1, starting transfers between devices, per_device(): lax.ppermute(to_after, ROWS_AXES, [(i, i + 1) for i in range(devices - 1)])  4.08 us
  transfers between devices with their start and end apart: 8, of which 7 were waited for; matrix products, arithmetic and copies ran while one was open for 1% of the time, Pallas kernels for 2%

profile of v5, /device:TPU:1, one launch (start us, length us, event | category | flops | bytes accessed | tf_op | source)
XLA Modules:
  0.0 101.9 jit_solution(17321887558106466934)
XLA Ops:
  0.6 3.1 %shard_map.86 = bf16[8,256,256]{2,1,0:T(8,128)(2,1)} custom-call(s32[8]{0:T(128)} %counts.1, bf16[256,1024]{1,0:T(8,128)(2,1)} %features.1, bf16[256,1024]{1,0:T(8,128)(2,1)} %environments.1, bf16[256,2048]{1,0:T(8,128)(2,1)} %projector.1), custom_call_target="tpu_custom_call" | custom-call | tf_op jit(solution)/shard_map/pallas_call | solution.py:191
  3.7 0.0 copy-start.1
  3.7 11.0 %all-to-all-start = ((bf16[8,256,256]{2,1,0:T(8,128)(2,1)}), bf16[8,256,256]{2,1,0:T(8,128)(2,1)S(1)}, u32[]{:S(2)}, u32[]{:S(2)}) async-start(bf16[8,256,256]{2,1,0:T(8,128)(2,1)} %shard_map.86), calls=%async_computation | async-start | bytes 2097152 | tf_op jit(solution)/shard_map/all_to_all | solution.py:207
  14.7 0.0 copy-start.2
  14.7 0.7 copy-done.2
  15.4 0.1 copy.11.target
  15.5 0.0 copy-done.1
  15.6 0.2 copy.10
  15.8 0.4 reshape.13.metric
  16.1 27.8 %all-to-all-done.parts = bf16[8,256,256]{2,1,0:T(8,128)(2,1)S(1)} async-done(((bf16[8,256,256]{2,1,0:T(8,128)(2,1)}), bf16[8,256,256]{2,1,0:T(8,128)(2,1)S(1)}, u32[]{:S(2)}, u32[]{:S(2)}) %all-to-all-start) | async-done | bytes 1048608 | tf_op jit(solution)/shard_map/all_to_all | solution.py:207
  43.9 1.3 %shard_map.87 = (bf16[256,256]{1,0:T(8,128)(2,1)S(1)}, bf16[32,64,256]{2,1,0:T(8,128)(2,1)}) custom-call(bf16[8,256,256]{2,1,0:T(8,128)(2,1)S(1)} %all-to-all-done.parts, bf16[256,256]{1,0:T(8,128)(2,1)S(1)} %reshape.13.metric, f32[256,1]{1,0:T(8,128)S(1)} %copy.11.target), custom_call_target="tpu_custom_call" | custom-call | tf_op jit(solution)/shard_map/pallas_call | solution.py:208
  45.3 0.0 copy-start
  45.3 4.5 %all-to-all-start.1 = ((bf16[32,64,256]{2,1,0:T(8,128)(2,1)}), bf16[32,64,256]{2,1,0:T(8,128)(2,1)S(1)}, u32[]{:S(2)}, u32[]{:S(2)}) async-start(bf16[32,64,256]{2,1,0:T(8,128)(2,1)} %get-tuple-element.11), calls=%async_computation.1 | async-start | bytes 2097152 | tf_op jit(solution)/shard_map/all_to_all | solution.py:226
  49.8 0.0 copy-done
  49.8 1.6 %shard_map.88 = (bf16[256,384]{1,0:T(8,128)(2,1)S(1)}, f32[256,384]{1,0:T(8,128)S(1)}, bf16[256,384]{1,0:T(8,128)(2,1)S(1)}) custom-call(s32[8,8]{1,0:T(8,128)S(1)} %copy-done, bf16[256,256]{1,0:T(8,128)(2,1)S(1)} %get-tuple-element.12.psi, bf16[256,256]{1,0:T(8,128)(2,1)S(1)} %reshape.13.metric, f32[256,1]{1,0:T(8,128)S(1)} %copy.11.target), custom_call_target="tpu_custom_call" | custom-call | tf_op jit(solution)/shard_map/pallas_call | solution.py:216
  51.4 4.1 %collective-permute-start = (bf16[256,384]{1,0:T(8,128)(2,1)S(1)}, bf16[256,384]{1,0:T(8,128)(2,1)S(1)}, u32[]{:S(2)}, u32[]{:S(2)}) collective-permute-start(bf16[256,384]{1,0:T(8,128)(2,1)S(1)} %get-tuple-element.14), channel_id=1, source_target_pairs={{0,8},{8,16},{16,24},{24,32},{32,40},{40,48},{48,56},{56,64},{64,7... | collective-permute-start | bytes 589832 | tf_op jit(solution)/shard_map/ppermute | solution.py:225
  55.5 1.9 %collective-permute-start.1 = (bf16[256,384]{1,0:T(8,128)(2,1)S(1)}, bf16[256,384]{1,0:T(8,128)(2,1)S(1)}, u32[]{:S(2)}, u32[]{:S(2)}) collective-permute-start(bf16[256,384]{1,0:T(8,128)(2,1)S(1)} %get-tuple-element.15), channel_id=1, source_target_pairs={{8,0},{16,8},{24,16},{32,24},{40,32},{48,40},{56,48},{64,56},{72,6... | collective-permute-start | bytes 589832 | tf_op jit(solution)/shard_map/ppermute | solution.py:224
  57.4 2.6 %collective-permute-done.left = bf16[256,384]{1,0:T(8,128)(2,1)S(1)} collective-permute-done((bf16[256,384]{1,0:T(8,128)(2,1)S(1)}, bf16[256,384]{1,0:T(8,128)(2,1)S(1)}, u32[]{:S(2)}, u32[]{:S(2)}) %collective-permute-start) | collective-permute-done | bytes 196640 | tf_op jit(solution)/shard_map/ppermute | solution.py:225
  60.1 4.5 %collective-permute-done.1.right = bf16[256,384]{1,0:T(8,128)(2,1)S(1)} collective-permute-done((bf16[256,384]{1,0:T(8,128)(2,1)S(1)}, bf16[256,384]{1,0:T(8,128)(2,1)S(1)}, u32[]{:S(2)}, u32[]{:S(2)}) %collective-permute-start.1) | collective-permute-done | bytes 196640 | tf_op jit(solution)/shard_map/ppermute | solution.py:224
  64.5 0.2 shard_map.89.own
  64.7 5.1 %collective-permute-start.4 = (bf16[272,256]{1,0:T(8,128)(2,1)S(1)}, bf16[272,256]{1,0:T(8,128)(2,1)S(1)}, u32[]{:S(2)}, u32[]{:S(2)}) collective-permute-start(bf16[272,256]{1,0:T(8,128)(2,1)S(1)} %shard_map.89.own), channel_id=1, source_target_pairs={{0,48},{16,0},{32,16},{48,32},{1,49},{17,1},{33,17},{49,33},{2,50}... | collective-permute-start | bytes 417800 | tf_op jit(solution)/shard_map/ppermute | solution.py:235
  69.9 1.9 %collective-permute-start.3 = (bf16[272,256]{1,0:T(8,128)(2,1)S(1)}, bf16[272,256]{1,0:T(8,128)(2,1)S(1)}, u32[]{:S(2)}, u32[]{:S(2)}) collective-permute-start(bf16[272,256]{1,0:T(8,128)(2,1)S(1)} %shard_map.89.own), channel_id=1, source_target_pairs={{0,32},{16,48},{32,0},{48,16},{1,33},{17,49},{33,1},{49,17},{2,34}... | collective-permute-start | bytes 417800 | tf_op jit(solution)/shard_map/ppermute | solution.py:235
  71.8 2.5 %collective-permute-start.2 = (bf16[272,256]{1,0:T(8,128)(2,1)S(1)}, bf16[272,256]{1,0:T(8,128)(2,1)S(1)}, u32[]{:S(2)}, u32[]{:S(2)}) collective-permute-start(bf16[272,256]{1,0:T(8,128)(2,1)S(1)} %shard_map.89.own), channel_id=1, source_target_pairs={{0,16},{16,32},{32,48},{48,0},{1,17},{17,33},{33,49},{49,1},{2,18}... | collective-permute-start | bytes 417800 | tf_op jit(solution)/shard_map/ppermute | solution.py:235
  74.3 3.5 %collective-permute-done.4.rest_2_ = bf16[272,256]{1,0:T(8,128)(2,1)S(1)} collective-permute-done((bf16[272,256]{1,0:T(8,128)(2,1)S(1)}, bf16[272,256]{1,0:T(8,128)(2,1)S(1)}, u32[]{:S(2)}, u32[]{:S(2)}) %collective-permute-start.4) | collective-permute-done | bytes 139296 | tf_op jit(solution)/shard_map/ppermute | solution.py:235
  77.8 1.6 %collective-permute-done.3.rest_1_ = bf16[272,256]{1,0:T(8,128)(2,1)S(1)} collective-permute-done((bf16[272,256]{1,0:T(8,128)(2,1)S(1)}, bf16[272,256]{1,0:T(8,128)(2,1)S(1)}, u32[]{:S(2)}, u32[]{:S(2)}) %collective-permute-start.3) | collective-permute-done | bytes 139296 | tf_op jit(solution)/shard_map/ppermute | solution.py:235
  79.4 2.1 %collective-permute-done.2.rest_0_ = bf16[272,256]{1,0:T(8,128)(2,1)S(1)} collective-permute-done((bf16[272,256]{1,0:T(8,128)(2,1)S(1)}, bf16[272,256]{1,0:T(8,128)(2,1)S(1)}, u32[]{:S(2)}, u32[]{:S(2)}) %collective-permute-start.2) | collective-permute-done | bytes 139296 | tf_op jit(solution)/shard_map/ppermute | solution.py:235
  81.5 0.0 all-to-all-done.1.pieces
  81.5 1.1 %shard_map.90 = (f32[8,80,128]{2,1,0:T(8,128)S(1)}, bf16[8,80,128]{2,1,0:T(8,128)(2,1)S(1)}) custom-call(s32[8,8]{1,0:T(8,128)S(1)} %copy-done, bf16[32,64,256]{2,1,0:T(8,128)(2,1)S(1)} %all-to-all-done.1.pieces, bf16[272,256]{1,0:T(8,128)(2,1)S(1)} %shard_map.89.own, bf16[272,256]{1,0:T(8,128)(2,1)S(1)} %collective-permute-done.2.rest_0_, ...), custom_call_target="tpu_custom_call" | custom-call | tf_op jit(solution)/shard_map/pallas_call | solution.py:239
  82.6 2.3 %collective-permute-start.5 = (bf16[8,80,128]{2,1,0:T(8,128)(2,1)S(1)}, bf16[8,80,128]{2,1,0:T(8,128)(2,1)S(1)}, u32[]{:S(2)}, u32[]{:S(2)}) collective-permute-start(bf16[8,80,128]{2,1,0:T(8,128)(2,1)S(1)} %get-tuple-element.17), channel_id=1, source_target_pairs={{0,8},{8,0},{1,9},{9,1},{2,10},{10,2},{3,11},{11,3},{4,12},{12,4},... | collective-permute-start | bytes 491528 | tf_op jit(solution)/shard_map/ppermute | solution.py:247
  84.9 1.0 collective-permute-done.5.received
  86.0 15.3 %all_to_all.15.parts = bf16[8,80,128]{2,1,0:T(8,128)(2,1)S(1)} all-to-all(bf16[8,80,128]{2,1,0:T(8,128)(2,1)S(1)} %shard_map.91), channel_id=1, replica_groups=mesh['y'=8,'x'=4,'core'=2,'env'=8] {'y'}, dimensions={0} | all-to-all | bytes 327680 | tf_op jit(solution)/shard_map/all_to_all | solution.py:255
  101.3 0.6 shard_map.92
  (1 shorter events, 0.0 us)
Async XLA Ops:
  3.7 11.8 %copy-start.1 = (bf16[8,8,32,32]{3,2,1,0:T(8,128)(2,1)S(1)}, bf16[8,8,32,32]{3,2,1,0:T(8,128)(2,1)}, u32[]{:S(2)}) copy-start(bf16[8,8,32,32]{3,2,1,0:T(8,128)(2,1)} %param.10) | copy-start | bytes 393220
  3.7 40.2 %all-to-all-start = ((bf16[8,256,256]{2,1,0:T(8,128)(2,1)}), bf16[8,256,256]{2,1,0:T(8,128)(2,1)S(1)}, u32[]{:S(2)}, u32[]{:S(2)}) async-start(bf16[8,256,256]{2,1,0:T(8,128)(2,1)} %shard_map.86), calls=%async_computation | async-start | bytes 2097152 | tf_op jit(solution)/shard_map/all_to_all | solution.py:207
  14.7 0.7 copy-start.2
  45.3 4.6 %copy-start = (s32[8,8]{1,0:T(8,128)S(1)}, s32[8,8]{1,0:T(8,128)}, u32[]{:S(2)}) copy-start(s32[8,8]{1,0:T(8,128)} %neighbours.3) | copy-start | bytes 772
  45.3 36.2 %all-to-all-start.1 = ((bf16[32,64,256]{2,1,0:T(8,128)(2,1)}), bf16[32,64,256]{2,1,0:T(8,128)(2,1)S(1)}, u32[]{:S(2)}, u32[]{:S(2)}) async-start(bf16[32,64,256]{2,1,0:T(8,128)(2,1)} %get-tuple-element.11), calls=%async_computation.1 | async-start | bytes 2097152 | tf_op jit(solution)/shard_map/all_to_all | solution.py:226
  51.4 8.7 %collective-permute-start = (bf16[256,384]{1,0:T(8,128)(2,1)S(1)}, bf16[256,384]{1,0:T(8,128)(2,1)S(1)}, u32[]{:S(2)}, u32[]{:S(2)}) collective-permute-start(bf16[256,384]{1,0:T(8,128)(2,1)S(1)} %get-tuple-element.14), channel_id=1, source_target_pairs={{0,8},{8,16},{16,24},{24,32},{32,40},{40,48},{48,56},{56,64},{64,7... | collective-permute-start | bytes 589832 | tf_op jit(solution)/shard_map/ppermute | solution.py:225
  55.5 9.1 %collective-permute-start.1 = (bf16[256,384]{1,0:T(8,128)(2,1)S(1)}, bf16[256,384]{1,0:T(8,128)(2,1)S(1)}, u32[]{:S(2)}, u32[]{:S(2)}) collective-permute-start(bf16[256,384]{1,0:T(8,128)(2,1)S(1)} %get-tuple-element.15), channel_id=1, source_target_pairs={{8,0},{16,8},{24,16},{32,24},{40,32},{48,40},{56,48},{64,56},{72,6... | collective-permute-start | bytes 589832 | tf_op jit(solution)/shard_map/ppermute | solution.py:224
  64.7 13.0 %collective-permute-start.4 = (bf16[272,256]{1,0:T(8,128)(2,1)S(1)}, bf16[272,256]{1,0:T(8,128)(2,1)S(1)}, u32[]{:S(2)}, u32[]{:S(2)}) collective-permute-start(bf16[272,256]{1,0:T(8,128)(2,1)S(1)} %shard_map.89.own), channel_id=1, source_target_pairs={{0,48},{16,0},{32,16},{48,32},{1,49},{17,1},{33,17},{49,33},{2,50}... | collective-permute-start | bytes 417800 | tf_op jit(solution)/shard_map/ppermute | solution.py:235
  69.9 9.5 %collective-permute-start.3 = (bf16[272,256]{1,0:T(8,128)(2,1)S(1)}, bf16[272,256]{1,0:T(8,128)(2,1)S(1)}, u32[]{:S(2)}, u32[]{:S(2)}) collective-permute-start(bf16[272,256]{1,0:T(8,128)(2,1)S(1)} %shard_map.89.own), channel_id=1, source_target_pairs={{0,32},{16,48},{32,0},{48,16},{1,33},{17,49},{33,1},{49,17},{2,34}... | collective-permute-start | bytes 417800 | tf_op jit(solution)/shard_map/ppermute | solution.py:235
  71.8 9.7 %collective-permute-start.2 = (bf16[272,256]{1,0:T(8,128)(2,1)S(1)}, bf16[272,256]{1,0:T(8,128)(2,1)S(1)}, u32[]{:S(2)}, u32[]{:S(2)}) collective-permute-start(bf16[272,256]{1,0:T(8,128)(2,1)S(1)} %shard_map.89.own), channel_id=1, source_target_pairs={{0,16},{16,32},{32,48},{48,0},{1,17},{17,33},{33,49},{49,1},{2,18}... | collective-permute-start | bytes 417800 | tf_op jit(solution)/shard_map/ppermute | solution.py:235
  82.6 3.3 %collective-permute-start.5 = (bf16[8,80,128]{2,1,0:T(8,128)(2,1)S(1)}, bf16[8,80,128]{2,1,0:T(8,128)(2,1)S(1)}, u32[]{:S(2)}, u32[]{:S(2)}) collective-permute-start(bf16[8,80,128]{2,1,0:T(8,128)(2,1)S(1)} %get-tuple-element.17), channel_id=1, source_target_pairs={{0,8},{8,0},{1,9},{9,1},{2,10},{10,2},{3,11},{11,3},{4,12},{12,4},... | collective-permute-start | bytes 491528 | tf_op jit(solution)/shard_map/ppermute | solution.py:247

commit v6 on v5

--- a/solution.py
+++ b/solution.py
@@ -53,6 +53,11 @@
         pltpu.make_async_copy(parts.at[part], out.at[part], sent.at[part]).wait()
 
 
+def unit(size):
+    row = lax.broadcasted_iota(jnp.int32, (size, size), 0)
+    return (row == lax.broadcasted_iota(jnp.int32, (size, size), 1)).astype(jnp.bfloat16)
+
+
 def sum_kernel(parts, metric, target, psi, out):
     del metric, target
     total = parts[0].astype(jnp.float32)
@@ -61,10 +66,7 @@
     total = total.astype(jnp.bfloat16)
     psi[...] = total
     rows, width = total.shape
-    unit = (
-        lax.broadcasted_iota(jnp.int32, (rows, rows), 0) == lax.broadcasted_iota(jnp.int32, (rows, rows), 1)
-    ).astype(jnp.bfloat16)
-    turned = dot(total, unit, ((0,), (0,))).astype(jnp.bfloat16)
+    turned = dot(total, unit(rows), ((0,), (0,))).astype(jnp.bfloat16)
     pieces, chunk = out.shape[0], out.shape[1]
     group = width // chunk
     planes = pieces // group
@@ -80,7 +82,7 @@
     return jnp.where(line == 0, high, jnp.where(line == 1, low, jnp.bfloat16(0)))
 
 
-def spread_kernel(neighbours, psi, metric, target, before, own, after, cells):
+def spread_kernel(neighbours, psi, metric, target, inner, own, outer, cells):
     rows, width = psi.shape
     cells[...] = jnp.zeros_like(cells)
     first = neighbours[0, 0] - rows // BLK
@@ -95,23 +97,25 @@
         for j in range(neighbours.shape[1]):
             there = pl.ds(pl.multiple_of((neighbours[b, j] - first) * BLK, BLK), BLK)
             cells[there, :] = cells[there, :] + terms[j * BLK:(j + 1) * BLK]
-    lane = lax.broadcasted_iota(jnp.int32, (rows, LANES), 1)
-    for out, start in ((before, 0), (after, 2 * rows)):
-        block = cells[start:start + rows]
+    core = neighbours[0, 0] // (rows // BLK) % 2
+    for out, start in ((inner, 2 * rows * (1 - core)), (own, rows), (outer, 2 * rows * core)):
+        block = cells[pl.ds(pl.multiple_of(start, rows), rows), :]
         weight = block[:, width:width + 1] + block[:, width + 1:width + 2]
         high = weight.astype(jnp.bfloat16)
         low = (weight - high.astype(jnp.float32)).astype(jnp.bfloat16)
-        out[:, :width] = block[:, :width].astype(jnp.bfloat16)
-        out[:, width:] = jnp.where(lane == 0, high, jnp.where(lane == 1, low, jnp.bfloat16(0)))
-    own[...] = cells[rows:2 * rows]
-
-
-def weighted_kernel(psi, own, left, right, carried):
+        column = jnp.where(lane == 0, high, jnp.where(lane == 1, low, jnp.bfloat16(0)))
+        out[0:rows] = block[:, :width].astype(out.dtype)
+        out[rows:] = dot(column, unit(rows), ((0,), (0,)))[0:EXTRA].astype(out.dtype)
+
+
+def weighted_kernel(psi, own, inner, outer, carried):
     rows, width = psi.shape
-    total = own[...] + left[...].astype(jnp.float32) + right[...].astype(jnp.float32)
-    carried[0:rows] = total[:, :width].astype(jnp.bfloat16)
-    weight = total[:, width:width + 1] + total[:, width + 1:width + 2]
-    rhs = jnp.sum(psi[...].astype(jnp.float32) * weight, axis=0, keepdims=True)
+    total = own[0:rows] + inner[0:rows].astype(jnp.float32) + outer[0:rows].astype(jnp.float32)
+    carried[0:rows] = total.astype(jnp.bfloat16)
+    rhs = jnp.zeros((1, width), jnp.float32)
+    for cells in (own, inner, outer):
+        terms = dot(cells[rows:].astype(jnp.bfloat16), psi[...], ((1,), (0,)))
+        rhs = rhs + (terms[0:1] + terms[1:2])
     carried[rows:] = high_low(rhs, carried.shape[0] - rows)
 
 
@@ -124,7 +128,7 @@
     total = jnp.zeros((planes * chunk, width), jnp.float32)
     rhs = jnp.zeros((1, width), jnp.float32)
     for step, cells in enumerate(carried):
-        source = (x + group - step) % group
+        source = x ^ step
         turned = pieces[pl.ds(source * planes, planes)].reshape(planes * chunk, rows)
         total = total + dot(turned, cells[0:rows], ((1,), (0,)))
         tail = cells[rows:].astype(jnp.float32)
@@ -212,17 +216,18 @@
         out_specs=(VMEM, VMEM),
         compiler_params=PARAMS,
     )(partial, metric_rows, target_column)
-    wide = shape((slab, width + LANES), bf16)
-    to_before, own, to_after = pl.pallas_call(
+    message = shape((slab + EXTRA, width), bf16)
+    inner, own, outer = pl.pallas_call(
         spread_kernel,
-        out_shape=(wide, shape(wide.shape, f32), wide),
-        in_specs=[SMEM, VMEM, VMEM, VMEM],
-        out_specs=(VMEM, VMEM, VMEM),
+        out_shape=(message, shape(message.shape, f32), message),
+        in_specs=[SMEM] + [VMEM] * 3,
+        out_specs=(VMEM,) * 3,
         scratch_shapes=[pltpu.VMEM((3 * slab, width + LANES), f32)],
         compiler_params=PARAMS,
     )(neighbours, psi, metric_rows, target_column)
-    from_after = lax.ppermute(to_before, ROWS_AXES, [(i + 1, i) for i in range(devices - 1)])
-    from_before = lax.ppermute(to_after, ROWS_AXES, [(i, i + 1) for i in range(devices - 1)])
+    next_chip = [(i, i + 2 * (i % 2) - 1) for i in range(1, devices - 1)]
+    outer = lax.ppermute(outer, ROWS_AXES, next_chip)
+    inner = lax.ppermute(inner, "core", [(0, 1), (1, 0)])
     turned = lax.all_to_all(turned, ("x", "env"), 0, 0, tiled=True)
     carried = pl.pallas_call(
         weighted_kernel,
@@ -230,10 +235,9 @@
         in_specs=[VMEM] * 4,
         out_specs=VMEM,
         compiler_params=PARAMS,
-    )(psi, own, from_before, from_after)
+    )(psi, own, inner, outer)
     shifted = [
-        lax.ppermute(carried, "x", [(i, (i + step) % group) for i in range(group)])
-        for step in range(1, group)
+        lax.ppermute(carried, "x", [(i, i ^ step) for i in range(group)]) for step in range(1, group)
     ]
     parts = (ys, 2 * BLK + EXTRA, width // 2)
     kept, sent = pl.pallas_call(

time: 102 us -> 101 us (level)
  waiting for transfers between devices: 43.1 us -> 40.8 us
    ppermute x5, waiting for transfers between devices: 14.3 us -> 12 us  [the longest x3 6.96 us: per_device(): lax.ppermute(carried, 'x', [(i, i ^ step) for i in range(group)])]
  transfers between devices with their start and end apart: 8 -> 8, of which waited for: 7 -> 5; matrix products, arithmetic and copies ran while one was open for 1% -> 1% of each run, Pallas kernels for 2% -> 2%
where the time goes in v6:
time: 101 us; the launch traced here: 100 us
  waiting for transfers between devices  40.8 us (40%)
  starting transfers between devices  33.5 us (33%)
  blocking collectives  15.3 us (15%)
  Pallas kernels  8.27 us (8%)
  local copies, waits for them, and re-layouts  1.38 us (1%)
    all_to_all x1, waiting for transfers between devices, per_device(): partial = lax.all_to_all(partial, 'env', 0, 0, tiled=True)  27.8 us
    all_to_all x1, blocking collectives, per_device(): terms = lax.all_to_all(terms, 'y', 0, 0, tiled=True)  15.3 us
    all_to_all x1, starting transfers between devices, per_device(): partial = lax.all_to_all(partial, 'env', 0, 0, tiled=True)  11 us
    ppermute x3, starting transfers between devices, per_device(): lax.ppermute(carried, 'x', [(i, i ^ step) for i in range(group)])  9.6 us
    ppermute x3, waiting for transfers between devices, per_device(): lax.ppermute(carried, 'x', [(i, i ^ step) for i in range(group)])  6.96 us
    ppermute x1, waiting for transfers between devices, per_device(): outer = lax.ppermute(outer, ROWS_AXES, next_chip)  5.08 us
    all_to_all x1, starting transfers between devices, per_device(): turned = lax.all_to_all(turned, ('x', 'env'), 0, 0, tiled=True)  4.54 us
    ppermute x1, starting transfers between devices, per_device(): outer = lax.ppermute(outer, ROWS_AXES, next_chip)  3.32 us
  transfers between devices with their start and end apart: 8, of which 5 were waited for; matrix products, arithmetic and copies ran while one was open for 1% of the time, Pallas kernels for 2%

profile of v6, /device:TPU:1, one launch (start us, length us, event | category | flops | bytes accessed | tf_op | source)
XLA Modules:
  0.0 100.1 jit_solution(2142318774408339488)
XLA Ops:
  0.6 3.1 %shard_map.86 = bf16[8,256,256]{2,1,0:T(8,128)(2,1)} custom-call(s32[8]{0:T(128)} %counts.1, bf16[256,1024]{1,0:T(8,128)(2,1)} %features.1, bf16[256,1024]{1,0:T(8,128)(2,1)} %environments.1, bf16[256,2048]{1,0:T(8,128)(2,1)} %projector.1), custom_call_target="tpu_custom_call" | custom-call | tf_op jit(solution)/shard_map/pallas_call | solution.py:195
  3.7 0.0 copy-start.1
  3.7 11.0 %all-to-all-start = ((bf16[8,256,256]{2,1,0:T(8,128)(2,1)}), bf16[8,256,256]{2,1,0:T(8,128)(2,1)S(1)}, u32[]{:S(2)}, u32[]{:S(2)}) async-start(bf16[8,256,256]{2,1,0:T(8,128)(2,1)} %shard_map.86), calls=%async_computation | async-start | bytes 2097152 | tf_op jit(solution)/shard_map/all_to_all | solution.py:211
  14.7 0.0 copy-start.2
  14.7 0.7 copy-done.2
  15.4 0.1 copy.11.target
  15.5 0.0 copy-done.1
  15.6 0.2 copy.10
  15.8 0.4 reshape.13.metric
  16.1 27.8 %all-to-all-done.parts = bf16[8,256,256]{2,1,0:T(8,128)(2,1)S(1)} async-done(((bf16[8,256,256]{2,1,0:T(8,128)(2,1)}), bf16[8,256,256]{2,1,0:T(8,128)(2,1)S(1)}, u32[]{:S(2)}, u32[]{:S(2)}) %all-to-all-start) | async-done | bytes 1048608 | tf_op jit(solution)/shard_map/all_to_all | solution.py:211
  43.9 1.3 %shard_map.87 = (bf16[256,256]{1,0:T(8,128)(2,1)S(1)}, bf16[32,64,256]{2,1,0:T(8,128)(2,1)}) custom-call(bf16[8,256,256]{2,1,0:T(8,128)(2,1)S(1)} %all-to-all-done.parts, bf16[256,256]{1,0:T(8,128)(2,1)S(1)} %reshape.13.metric, f32[256,1]{1,0:T(8,128)S(1)} %copy.11.target), custom_call_target="tpu_custom_call" | custom-call | tf_op jit(solution)/shard_map/pallas_call | solution.py:212
  45.3 0.0 copy-start
  45.3 4.5 %all-to-all-start.1 = ((bf16[32,64,256]{2,1,0:T(8,128)(2,1)}), bf16[32,64,256]{2,1,0:T(8,128)(2,1)S(1)}, u32[]{:S(2)}, u32[]{:S(2)}) async-start(bf16[32,64,256]{2,1,0:T(8,128)(2,1)} %get-tuple-element.11), calls=%async_computation.1 | async-start | bytes 2097152 | tf_op jit(solution)/shard_map/all_to_all | solution.py:231
  49.8 0.0 copy-done
  49.8 1.8 %shard_map.88 = (bf16[272,256]{1,0:T(8,128)(2,1)S(1)}, f32[272,256]{1,0:T(8,128)S(1)}, bf16[272,256]{1,0:T(8,128)(2,1)S(1)}) custom-call(s32[8,8]{1,0:T(8,128)S(1)} %copy-done, bf16[256,256]{1,0:T(8,128)(2,1)S(1)} %get-tuple-element.12.psi, bf16[256,256]{1,0:T(8,128)(2,1)S(1)} %reshape.13.metric, f32[256,1]{1,0:T(8,128)S(1)} %copy.11.target), custom_call_target="tpu_custom_call" | custom-call | tf_op jit(solution)/shard_map/pallas_call | solution.py:220
  51.7 2.7 %collective-permute-start = (bf16[272,256]{1,0:T(8,128)(2,1)S(1)}, bf16[272,256]{1,0:T(8,128)(2,1)S(1)}, u32[]{:S(2)}, u32[]{:S(2)}) collective-permute-start(bf16[272,256]{1,0:T(8,128)(2,1)S(1)} %get-tuple-element.14), channel_id=1, source_target_pairs={{0,8},{8,0},{1,9},{9,1},{2,10},{10,2},{3,11},{11,3},{4,12},{12,4},... | collective-permute-start | bytes 417800 | tf_op jit(solution)/shard_map/ppermute | solution.py:230
  54.4 3.3 %collective-permute-start.1 = (bf16[272,256]{1,0:T(8,128)(2,1)S(1)}, bf16[272,256]{1,0:T(8,128)(2,1)S(1)}, u32[]{:S(2)}, u32[]{:S(2)}) collective-permute-start(bf16[272,256]{1,0:T(8,128)(2,1)S(1)} %get-tuple-element.15), channel_id=1, source_target_pairs={{8,16},{16,8},{24,32},{32,24},{40,48},{48,40},{56,64},{64,56},{72,... | collective-permute-start | bytes 417800 | tf_op jit(solution)/shard_map/ppermute | solution.py:229
  57.7 0.0 collective-permute-done.inner
  57.7 5.1 %collective-permute-done.1.outer = bf16[272,256]{1,0:T(8,128)(2,1)S(1)} collective-permute-done((bf16[272,256]{1,0:T(8,128)(2,1)S(1)}, bf16[272,256]{1,0:T(8,128)(2,1)S(1)}, u32[]{:S(2)}, u32[]{:S(2)}) %collective-permute-start.1) | collective-permute-done | bytes 139296 | tf_op jit(solution)/shard_map/ppermute | solution.py:229
  62.8 0.2 shard_map.89.own
  63.0 5.2 %collective-permute-start.4 = (bf16[272,256]{1,0:T(8,128)(2,1)S(1)}, bf16[272,256]{1,0:T(8,128)(2,1)S(1)}, u32[]{:S(2)}, u32[]{:S(2)}) collective-permute-start(bf16[272,256]{1,0:T(8,128)(2,1)S(1)} %shard_map.89.own), channel_id=1, source_target_pairs={{0,48},{16,32},{32,16},{48,0},{1,49},{17,33},{33,17},{49,1},{2,50}... | collective-permute-start | bytes 417800 | tf_op jit(solution)/shard_map/ppermute | solution.py:240
  68.2 2.0 %collective-permute-start.3 = (bf16[272,256]{1,0:T(8,128)(2,1)S(1)}, bf16[272,256]{1,0:T(8,128)(2,1)S(1)}, u32[]{:S(2)}, u32[]{:S(2)}) collective-permute-start(bf16[272,256]{1,0:T(8,128)(2,1)S(1)} %shard_map.89.own), channel_id=1, source_target_pairs={{0,32},{16,48},{32,0},{48,16},{1,33},{17,49},{33,1},{49,17},{2,34}... | collective-permute-start | bytes 417800 | tf_op jit(solution)/shard_map/ppermute | solution.py:240
  70.2 2.5 %collective-permute-start.2 = (bf16[272,256]{1,0:T(8,128)(2,1)S(1)}, bf16[272,256]{1,0:T(8,128)(2,1)S(1)}, u32[]{:S(2)}, u32[]{:S(2)}) collective-permute-start(bf16[272,256]{1,0:T(8,128)(2,1)S(1)} %shard_map.89.own), channel_id=1, source_target_pairs={{0,16},{16,0},{32,48},{48,32},{1,17},{17,1},{33,49},{49,33},{2,18}... | collective-permute-start | bytes 417800 | tf_op jit(solution)/shard_map/ppermute | solution.py:240
  72.6 6.0 %collective-permute-done.4.rest_2_ = bf16[272,256]{1,0:T(8,128)(2,1)S(1)} collective-permute-done((bf16[272,256]{1,0:T(8,128)(2,1)S(1)}, bf16[272,256]{1,0:T(8,128)(2,1)S(1)}, u32[]{:S(2)}, u32[]{:S(2)}) %collective-permute-start.4) | collective-permute-done | bytes 139296 | tf_op jit(solution)/shard_map/ppermute | solution.py:240
  78.6 0.0 collective-permute-done.3.rest_1_
  78.6 1.0 %collective-permute-done.2.rest_0_ = bf16[272,256]{1,0:T(8,128)(2,1)S(1)} collective-permute-done((bf16[272,256]{1,0:T(8,128)(2,1)S(1)}, bf16[272,256]{1,0:T(8,128)(2,1)S(1)}, u32[]{:S(2)}, u32[]{:S(2)}) %collective-permute-start.2) | collective-permute-done | bytes 139296 | tf_op jit(solution)/shard_map/ppermute | solution.py:240
  79.6 0.0 all-to-all-done.1.pieces
  79.6 1.1 %shard_map.90 = (f32[8,80,128]{2,1,0:T(8,128)S(1)}, bf16[8,80,128]{2,1,0:T(8,128)(2,1)S(1)}) custom-call(s32[8,8]{1,0:T(8,128)S(1)} %copy-done, bf16[32,64,256]{2,1,0:T(8,128)(2,1)S(1)} %all-to-all-done.1.pieces, bf16[272,256]{1,0:T(8,128)(2,1)S(1)} %shard_map.89.own, bf16[272,256]{1,0:T(8,128)(2,1)S(1)} %collective-permute-done.2.rest_0_, ...), custom_call_target="tpu_custom_call" | custom-call | tf_op jit(solution)/shard_map/pallas_call | solution.py:243
  80.7 2.3 %collective-permute-start.5 = (bf16[8,80,128]{2,1,0:T(8,128)(2,1)S(1)}, bf16[8,80,128]{2,1,0:T(8,128)(2,1)S(1)}, u32[]{:S(2)}, u32[]{:S(2)}) collective-permute-start(bf16[8,80,128]{2,1,0:T(8,128)(2,1)S(1)} %get-tuple-element.17), channel_id=1, source_target_pairs={{0,8},{8,0},{1,9},{9,1},{2,10},{10,2},{3,11},{11,3},{4,12},{12,4},... | collective-permute-start | bytes 491528 | tf_op jit(solution)/shard_map/ppermute | solution.py:251
  83.0 1.0 %collective-permute-done.5.received = bf16[8,80,128]{2,1,0:T(8,128)(2,1)S(1)} collective-permute-done((bf16[8,80,128]{2,1,0:T(8,128)(2,1)S(1)}, bf16[8,80,128]{2,1,0:T(8,128)(2,1)S(1)}, u32[]{:S(2)}, u32[]{:S(2)}) %collective-permute-start.5) | collective-permute-done | bytes 163872 | tf_op jit(solution)/shard_map/ppermute | solution.py:251
  84.1 15.3 %all_to_all.15.parts = bf16[8,80,128]{2,1,0:T(8,128)(2,1)S(1)} all-to-all(bf16[8,80,128]{2,1,0:T(8,128)(2,1)S(1)} %shard_map.91), channel_id=1, replica_groups=mesh['y'=8,'x'=4,'core'=2,'env'=8] {'y'}, dimensions={0} | all-to-all | bytes 327680 | tf_op jit(solution)/shard_map/all_to_all | solution.py:259
  99.4 0.6 shard_map.92
  (1 shorter events, 0.0 us)
Async XLA Ops:
  3.7 11.8 %copy-start.1 = (bf16[8,8,32,32]{3,2,1,0:T(8,128)(2,1)S(1)}, bf16[8,8,32,32]{3,2,1,0:T(8,128)(2,1)}, u32[]{:S(2)}) copy-start(bf16[8,8,32,32]{3,2,1,0:T(8,128)(2,1)} %param.10) | copy-start | bytes 393220
  3.7 40.2 %all-to-all-start = ((bf16[8,256,256]{2,1,0:T(8,128)(2,1)}), bf16[8,256,256]{2,1,0:T(8,128)(2,1)S(1)}, u32[]{:S(2)}, u32[]{:S(2)}) async-start(bf16[8,256,256]{2,1,0:T(8,128)(2,1)} %shard_map.86), calls=%async_computation | async-start | bytes 2097152 | tf_op jit(solution)/shard_map/all_to_all | solution.py:211
  14.7 0.7 copy-start.2
  45.3 4.6 %copy-start = (s32[8,8]{1,0:T(8,128)S(1)}, s32[8,8]{1,0:T(8,128)}, u32[]{:S(2)}) copy-start(s32[8,8]{1,0:T(8,128)} %neighbours.3) | copy-start | bytes 772
  45.3 34.3 %all-to-all-start.1 = ((bf16[32,64,256]{2,1,0:T(8,128)(2,1)}), bf16[32,64,256]{2,1,0:T(8,128)(2,1)S(1)}, u32[]{:S(2)}, u32[]{:S(2)}) async-start(bf16[32,64,256]{2,1,0:T(8,128)(2,1)} %get-tuple-element.11), calls=%async_computation.1 | async-start | bytes 2097152 | tf_op jit(solution)/shard_map/all_to_all | solution.py:231
  51.7 6.0 %collective-permute-start = (bf16[272,256]{1,0:T(8,128)(2,1)S(1)}, bf16[272,256]{1,0:T(8,128)(2,1)S(1)}, u32[]{:S(2)}, u32[]{:S(2)}) collective-permute-start(bf16[272,256]{1,0:T(8,128)(2,1)S(1)} %get-tuple-element.14), channel_id=1, source_target_pairs={{0,8},{8,0},{1,9},{9,1},{2,10},{10,2},{3,11},{11,3},{4,12},{12,4},... | collective-permute-start | bytes 417800 | tf_op jit(solution)/shard_map/ppermute | solution.py:230
  54.4 8.4 %collective-permute-start.1 = (bf16[272,256]{1,0:T(8,128)(2,1)S(1)}, bf16[272,256]{1,0:T(8,128)(2,1)S(1)}, u32[]{:S(2)}, u32[]{:S(2)}) collective-permute-start(bf16[272,256]{1,0:T(8,128)(2,1)S(1)} %get-tuple-element.15), channel_id=1, source_target_pairs={{8,16},{16,8},{24,32},{32,24},{40,48},{48,40},{56,64},{64,56},{72,... | collective-permute-start | bytes 417800 | tf_op jit(solution)/shard_map/ppermute | solution.py:229
  63.0 15.6 %collective-permute-start.4 = (bf16[272,256]{1,0:T(8,128)(2,1)S(1)}, bf16[272,256]{1,0:T(8,128)(2,1)S(1)}, u32[]{:S(2)}, u32[]{:S(2)}) collective-permute-start(bf16[272,256]{1,0:T(8,128)(2,1)S(1)} %shard_map.89.own), channel_id=1, source_target_pairs={{0,48},{16,32},{32,16},{48,0},{1,49},{17,33},{33,17},{49,1},{2,50}... | collective-permute-start | bytes 417800 | tf_op jit(solution)/shard_map/ppermute | solution.py:240
  68.2 10.4 %collective-permute-start.3 = (bf16[272,256]{1,0:T(8,128)(2,1)S(1)}, bf16[272,256]{1,0:T(8,128)(2,1)S(1)}, u32[]{:S(2)}, u32[]{:S(2)}) collective-permute-start(bf16[272,256]{1,0:T(8,128)(2,1)S(1)} %shard_map.89.own), channel_id=1, source_target_pairs={{0,32},{16,48},{32,0},{48,16},{1,33},{17,49},{33,1},{49,17},{2,34}... | collective-permute-start | bytes 417800 | tf_op jit(solution)/shard_map/ppermute | solution.py:240
  70.2 9.4 %collective-permute-start.2 = (bf16[272,256]{1,0:T(8,128)(2,1)S(1)}, bf16[272,256]{1,0:T(8,128)(2,1)S(1)}, u32[]{:S(2)}, u32[]{:S(2)}) collective-permute-start(bf16[272,256]{1,0:T(8,128)(2,1)S(1)} %shard_map.89.own), channel_id=1, source_target_pairs={{0,16},{16,0},{32,48},{48,32},{1,17},{17,1},{33,49},{49,33},{2,18}... | collective-permute-start | bytes 417800 | tf_op jit(solution)/shard_map/ppermute | solution.py:240
  80.7 3.3 %collective-permute-start.5 = (bf16[8,80,128]{2,1,0:T(8,128)(2,1)S(1)}, bf16[8,80,128]{2,1,0:T(8,128)(2,1)S(1)}, u32[]{:S(2)}, u32[]{:S(2)}) collective-permute-start(bf16[8,80,128]{2,1,0:T(8,128)(2,1)S(1)} %get-tuple-element.17), channel_id=1, source_target_pairs={{0,8},{8,0},{1,9},{9,1},{2,10},{10,2},{3,11},{11,3},{4,12},{12,4},... | collective-permute-start | bytes 491528 | tf_op jit(solution)/shard_map/ppermute | solution.py:251

commit v7 on v6

--- a/solution.py
+++ b/solution.py
@@ -9,6 +9,7 @@
 EXTRA = 16
 LANES = 128
 ROWS_AXES = ("y", "x", "core")
+ORDER = (0, 2, 4, 6, 1, 3, 5, 7)
 VMEM = pl.BlockSpec(memory_space=pltpu.VMEM)
 SMEM = pl.BlockSpec(memory_space=pltpu.SMEM)
 ANY = pl.BlockSpec(memory_space=pl.ANY)
@@ -48,9 +49,9 @@
     for part in range(out.shape[0]):
         cols = slice(part * width, (part + 1) * width)
         parts[part] = dot(masked, weights[:, cols], ((1,), (0,))).astype(jnp.bfloat16)
-        pltpu.make_async_copy(parts.at[part], out.at[part], sent.at[part]).start()
+        pltpu.make_async_copy(parts.at[part], out.at[ORDER.index(part)], sent.at[part]).start()
     for part in range(out.shape[0]):
-        pltpu.make_async_copy(parts.at[part], out.at[part], sent.at[part]).wait()
+        pltpu.make_async_copy(parts.at[part], out.at[ORDER.index(part)], sent.at[part]).wait()
 
 
 def unit(size):
@@ -208,7 +209,7 @@
         ],
         compiler_params=WHOLE,
     )(counts, features, environments, projector)
-    partial = lax.all_to_all(partial, "env", 0, 0, tiled=True)
+    partial = lax.all_to_all(partial, "env", 0, 0, tiled=True, axis_index_groups=[list(ORDER)])
     psi, turned = pl.pallas_call(
         sum_kernel,
         out_shape=(shape((slab, width), bf16), shape((group * planes, width // group, slab), bf16)),
@@ -228,7 +229,8 @@
     next_chip = [(i, i + 2 * (i % 2) - 1) for i in range(1, devices - 1)]
     outer = lax.ppermute(outer, ROWS_AXES, next_chip)
     inner = lax.ppermute(inner, "core", [(0, 1), (1, 0)])
-    turned = lax.all_to_all(turned, ("x", "env"), 0, 0, tiled=True)
+    both = [part * planes + z for part in range(group) for z in ORDER]
+    turned = lax.all_to_all(turned, ("x", "env"), 0, 0, tiled=True, axis_index_groups=[both])
     carried = pl.pallas_call(
         weighted_kernel,
         out_shape=shape((slab + EXTRA, width), bf16),
@@ -256,7 +258,7 @@
         out_specs=VMEM,
         compiler_params=PARAMS,
     )(kept, received)
-    terms = lax.all_to_all(terms, "y", 0, 0, tiled=True)
+    terms = lax.all_to_all(terms, "y", 0, 0, tiled=True, axis_index_groups=[list(ORDER)])
 
     def finish(parts, gram, rhs):
         final_kernel(parts, gram, rhs, factor=1.0 / (slab * devices) ** 0.5)

time: 101 us -> 100 us (0.990)
  starting transfers between devices: 33.5 us -> 38 us
  waiting for transfers between devices: 40.8 us -> 36.4 us
    all_to_all x2, waiting for transfers between devices: 27.8 us -> 24.1 us  [the longest x1 24.1 us: per_device(): lax.all_to_all(partial, 'env', 0, 0, tiled=True, axis_index_groups=[list(...]
    all_to_all x2, starting transfers between devices: 15.5 us -> 19 us  [the longest x1 11 us: per_device(): lax.all_to_all(partial, 'env', 0, 0, tiled=True, axis_index_groups=[list(...]
    all_to_all x1, blocking collectives: 15.3 us -> 14.3 us  [per_device(): lax.all_to_all(terms, 'y', 0, 0, tiled=True, axis_index_groups=[list(ORDE...]
  transfers between devices with their start and end apart: 8 -> 8, of which waited for: 5 -> 6; matrix products, arithmetic and copies ran while one was open for 1% -> 1% of each run, Pallas kernels for 2% -> 2%
where the time goes in v7:
time: 100 us; the launch traced here: 99.1 us
  starting transfers between devices  38 us (38%)
  waiting for transfers between devices  36.4 us (36%)
  blocking collectives  14.3 us (14%)
  Pallas kernels  8.28 us (8%)
  local copies, waits for them, and re-layouts  1.38 us (1%)
    all_to_all x1, waiting for transfers between devices, per_device(): lax.all_to_all(partial, 'env', 0, 0, tiled=True, axis_index_groups=[list(...  24.1 us
    all_to_all x1, blocking collectives, per_device(): lax.all_to_all(terms, 'y', 0, 0, tiled=True, axis_index_groups=[list(ORDE...  14.3 us
    all_to_all x1, starting transfers between devices, per_device(): lax.all_to_all(partial, 'env', 0, 0, tiled=True, axis_index_groups=[list(...  11 us
    ppermute x3, starting transfers between devices, per_device(): lax.ppermute(carried, 'x', [(i, i ^ step) for i in range(group)])  10.4 us
    all_to_all x1, starting transfers between devices, per_device(): lax.all_to_all(turned, ('x', 'env'), 0, 0, tiled=True, axis_index_groups=...  7.95 us
    ppermute x3, waiting for transfers between devices, per_device(): lax.ppermute(carried, 'x', [(i, i ^ step) for i in range(group)])  6.25 us
    ppermute x1, waiting for transfers between devices, per_device(): outer = lax.ppermute(outer, ROWS_AXES, next_chip)  4.97 us
    ppermute x1, starting transfers between devices, per_device(): outer = lax.ppermute(outer, ROWS_AXES, next_chip)  3.32 us
  transfers between devices with their start and end apart: 8, of which 6 were waited for; matrix products, arithmetic and copies ran while one was open for 1% of the time, Pallas kernels for 2%

profile of v7, /device:TPU:1, one launch (start us, length us, event | category | flops | bytes accessed | tf_op | source)
XLA Modules:
  0.0 99.1 jit_solution(968421954478557982)
XLA Ops:
  0.6 3.1 %shard_map.86 = bf16[8,256,256]{2,1,0:T(8,128)(2,1)} custom-call(s32[8]{0:T(128)} %counts.1, bf16[256,1024]{1,0:T(8,128)(2,1)} %features.1, bf16[256,1024]{1,0:T(8,128)(2,1)} %environments.1, bf16[256,2048]{1,0:T(8,128)(2,1)} %projector.1), custom_call_target="tpu_custom_call" | custom-call | tf_op jit(solution)/shard_map/pallas_call | solution.py:196
  3.7 0.0 copy-start.1
  3.7 11.0 %all-to-all-start = ((bf16[8,256,256]{2,1,0:T(8,128)(2,1)}), bf16[8,256,256]{2,1,0:T(8,128)(2,1)S(1)}, u32[]{:S(2)}, u32[]{:S(2)}) async-start(bf16[8,256,256]{2,1,0:T(8,128)(2,1)} %shard_map.86), calls=%async_computation | async-start | bytes 2097152 | tf_op jit(solution)/shard_map/all_to_all | solution.py:212
  14.8 0.0 copy-start.2
  14.8 0.7 copy-done.2
  15.4 0.1 copy.11.target
  15.6 0.0 copy-done.1
  15.6 0.2 copy.10
  15.8 0.4 reshape.13.metric
  16.2 24.1 %all-to-all-done.parts = bf16[8,256,256]{2,1,0:T(8,128)(2,1)S(1)} async-done(((bf16[8,256,256]{2,1,0:T(8,128)(2,1)}), bf16[8,256,256]{2,1,0:T(8,128)(2,1)S(1)}, u32[]{:S(2)}, u32[]{:S(2)}) %all-to-all-start) | async-done | bytes 1048608 | tf_op jit(solution)/shard_map/all_to_all | solution.py:212
  40.3 1.3 %shard_map.87 = (bf16[256,256]{1,0:T(8,128)(2,1)S(1)}, bf16[32,64,256]{2,1,0:T(8,128)(2,1)}) custom-call(bf16[8,256,256]{2,1,0:T(8,128)(2,1)S(1)} %all-to-all-done.parts, bf16[256,256]{1,0:T(8,128)(2,1)S(1)} %reshape.13.metric, f32[256,1]{1,0:T(8,128)S(1)} %copy.11.target), custom_call_target="tpu_custom_call" | custom-call | tf_op jit(solution)/shard_map/pallas_call | solution.py:213
  41.6 0.0 copy-start
  41.6 8.0 %all-to-all-start.1 = ((bf16[32,64,256]{2,1,0:T(8,128)(2,1)}), bf16[32,64,256]{2,1,0:T(8,128)(2,1)S(1)}, u32[]{:S(2)}, u32[]{:S(2)}) async-start(bf16[32,64,256]{2,1,0:T(8,128)(2,1)} %get-tuple-element.11), calls=%async_computation.1 | async-start | bytes 2097152 | tf_op jit(solution)/shard_map/all_to_all | solution.py:233
  49.6 0.0 copy-done
  49.6 1.8 %shard_map.88 = (bf16[272,256]{1,0:T(8,128)(2,1)S(1)}, f32[272,256]{1,0:T(8,128)S(1)}, bf16[272,256]{1,0:T(8,128)(2,1)S(1)}) custom-call(s32[8,8]{1,0:T(8,128)S(1)} %copy-done, bf16[256,256]{1,0:T(8,128)(2,1)S(1)} %get-tuple-element.12.psi, bf16[256,256]{1,0:T(8,128)(2,1)S(1)} %reshape.13.metric, f32[256,1]{1,0:T(8,128)S(1)} %copy.11.target), custom_call_target="tpu_custom_call" | custom-call | tf_op jit(solution)/shard_map/pallas_call | solution.py:221
  51.4 3.0 %collective-permute-start = (bf16[272,256]{1,0:T(8,128)(2,1)S(1)}, bf16[272,256]{1,0:T(8,128)(2,1)S(1)}, u32[]{:S(2)}, u32[]{:S(2)}) collective-permute-start(bf16[272,256]{1,0:T(8,128)(2,1)S(1)} %get-tuple-element.14), channel_id=1, source_target_pairs={{0,8},{8,0},{1,9},{9,1},{2,10},{10,2},{3,11},{11,3},{4,12},{12,4},... | collective-permute-start | bytes 417800 | tf_op jit(solution)/shard_map/ppermute | solution.py:231
  54.4 3.3 %collective-permute-start.1 = (bf16[272,256]{1,0:T(8,128)(2,1)S(1)}, bf16[272,256]{1,0:T(8,128)(2,1)S(1)}, u32[]{:S(2)}, u32[]{:S(2)}) collective-permute-start(bf16[272,256]{1,0:T(8,128)(2,1)S(1)} %get-tuple-element.15), channel_id=1, source_target_pairs={{8,16},{16,8},{24,32},{32,24},{40,48},{48,40},{56,64},{64,56},{72,... | collective-permute-start | bytes 417800 | tf_op jit(solution)/shard_map/ppermute | solution.py:230
  57.8 0.0 collective-permute-done.inner
  57.8 5.0 %collective-permute-done.1.outer = bf16[272,256]{1,0:T(8,128)(2,1)S(1)} collective-permute-done((bf16[272,256]{1,0:T(8,128)(2,1)S(1)}, bf16[272,256]{1,0:T(8,128)(2,1)S(1)}, u32[]{:S(2)}, u32[]{:S(2)}) %collective-permute-start.1) | collective-permute-done | bytes 139296 | tf_op jit(solution)/shard_map/ppermute | solution.py:230
  62.7 0.2 shard_map.89.own
  63.0 6.0 %collective-permute-start.4 = (bf16[272,256]{1,0:T(8,128)(2,1)S(1)}, bf16[272,256]{1,0:T(8,128)(2,1)S(1)}, u32[]{:S(2)}, u32[]{:S(2)}) collective-permute-start(bf16[272,256]{1,0:T(8,128)(2,1)S(1)} %shard_map.89.own), channel_id=1, source_target_pairs={{0,48},{16,32},{32,16},{48,0},{1,49},{17,33},{33,17},{49,1},{2,50}... | collective-permute-start | bytes 417800 | tf_op jit(solution)/shard_map/ppermute | solution.py:242
  69.0 1.9 %collective-permute-start.3 = (bf16[272,256]{1,0:T(8,128)(2,1)S(1)}, bf16[272,256]{1,0:T(8,128)(2,1)S(1)}, u32[]{:S(2)}, u32[]{:S(2)}) collective-permute-start(bf16[272,256]{1,0:T(8,128)(2,1)S(1)} %shard_map.89.own), channel_id=1, source_target_pairs={{0,32},{16,48},{32,0},{48,16},{1,33},{17,49},{33,1},{49,17},{2,34}... | collective-permute-start | bytes 417800 | tf_op jit(solution)/shard_map/ppermute | solution.py:242
  70.9 2.5 %collective-permute-start.2 = (bf16[272,256]{1,0:T(8,128)(2,1)S(1)}, bf16[272,256]{1,0:T(8,128)(2,1)S(1)}, u32[]{:S(2)}, u32[]{:S(2)}) collective-permute-start(bf16[272,256]{1,0:T(8,128)(2,1)S(1)} %shard_map.89.own), channel_id=1, source_target_pairs={{0,16},{16,0},{32,48},{48,32},{1,17},{17,1},{33,49},{49,33},{2,18}... | collective-permute-start | bytes 417800 | tf_op jit(solution)/shard_map/ppermute | solution.py:242
  73.4 4.2 %collective-permute-done.4.rest_2_ = bf16[272,256]{1,0:T(8,128)(2,1)S(1)} collective-permute-done((bf16[272,256]{1,0:T(8,128)(2,1)S(1)}, bf16[272,256]{1,0:T(8,128)(2,1)S(1)}, u32[]{:S(2)}, u32[]{:S(2)}) %collective-permute-start.4) | collective-permute-done | bytes 139296 | tf_op jit(solution)/shard_map/ppermute | solution.py:242
  77.6 1.3 %collective-permute-done.3.rest_1_ = bf16[272,256]{1,0:T(8,128)(2,1)S(1)} collective-permute-done((bf16[272,256]{1,0:T(8,128)(2,1)S(1)}, bf16[272,256]{1,0:T(8,128)(2,1)S(1)}, u32[]{:S(2)}, u32[]{:S(2)}) %collective-permute-start.3) | collective-permute-done | bytes 139296 | tf_op jit(solution)/shard_map/ppermute | solution.py:242
  79.0 0.7 collective-permute-done.2.rest_0_
  79.7 0.0 all-to-all-done.1.pieces
  79.7 1.1 %shard_map.90 = (f32[8,80,128]{2,1,0:T(8,128)S(1)}, bf16[8,80,128]{2,1,0:T(8,128)(2,1)S(1)}) custom-call(s32[8,8]{1,0:T(8,128)S(1)} %copy-done, bf16[32,64,256]{2,1,0:T(8,128)(2,1)S(1)} %all-to-all-done.1.pieces, bf16[272,256]{1,0:T(8,128)(2,1)S(1)} %shard_map.89.own, bf16[272,256]{1,0:T(8,128)(2,1)S(1)} %collective-permute-done.2.rest_0_, ...), custom_call_target="tpu_custom_call" | custom-call | tf_op jit(solution)/shard_map/pallas_call | solution.py:245
  80.8 2.3 %collective-permute-start.5 = (bf16[8,80,128]{2,1,0:T(8,128)(2,1)S(1)}, bf16[8,80,128]{2,1,0:T(8,128)(2,1)S(1)}, u32[]{:S(2)}, u32[]{:S(2)}) collective-permute-start(bf16[8,80,128]{2,1,0:T(8,128)(2,1)S(1)} %get-tuple-element.17), channel_id=1, source_target_pairs={{0,8},{8,0},{1,9},{9,1},{2,10},{10,2},{3,11},{11,3},{4,12},{12,4},... | collective-permute-start | bytes 491528 | tf_op jit(solution)/shard_map/ppermute | solution.py:253
  83.1 1.0 %collective-permute-done.5.received = bf16[8,80,128]{2,1,0:T(8,128)(2,1)S(1)} collective-permute-done((bf16[8,80,128]{2,1,0:T(8,128)(2,1)S(1)}, bf16[8,80,128]{2,1,0:T(8,128)(2,1)S(1)}, u32[]{:S(2)}, u32[]{:S(2)}) %collective-permute-start.5) | collective-permute-done | bytes 163872 | tf_op jit(solution)/shard_map/ppermute | solution.py:253
  84.2 14.3 %all_to_all.15.parts = bf16[8,80,128]{2,1,0:T(8,128)(2,1)S(1)} all-to-all(bf16[8,80,128]{2,1,0:T(8,128)(2,1)S(1)} %shard_map.91), channel_id=1, replica_groups={{0,128,256,384,64,192,320,448},{1,129,257,385,65,193,321,449},{2,130,25..., dimensions={0} | all-to-all | bytes 327680 | tf_op jit(solution)/shard_map/all_to_all | solution.py:261
  98.5 0.6 shard_map.92
  (1 shorter events, 0.0 us)
Async XLA Ops:
  3.7 11.8 %copy-start.1 = (bf16[8,8,32,32]{3,2,1,0:T(8,128)(2,1)S(1)}, bf16[8,8,32,32]{3,2,1,0:T(8,128)(2,1)}, u32[]{:S(2)}) copy-start(bf16[8,8,32,32]{3,2,1,0:T(8,128)(2,1)} %param.10) | copy-start | bytes 393220
  3.7 36.6 %all-to-all-start = ((bf16[8,256,256]{2,1,0:T(8,128)(2,1)}), bf16[8,256,256]{2,1,0:T(8,128)(2,1)S(1)}, u32[]{:S(2)}, u32[]{:S(2)}) async-start(bf16[8,256,256]{2,1,0:T(8,128)(2,1)} %shard_map.86), calls=%async_computation | async-start | bytes 2097152 | tf_op jit(solution)/shard_map/all_to_all | solution.py:212
  14.8 0.7 copy-start.2
  41.6 8.0 %copy-start = (s32[8,8]{1,0:T(8,128)S(1)}, s32[8,8]{1,0:T(8,128)}, u32[]{:S(2)}) copy-start(s32[8,8]{1,0:T(8,128)} %neighbours.3) | copy-start | bytes 772
  41.6 38.1 %all-to-all-start.1 = ((bf16[32,64,256]{2,1,0:T(8,128)(2,1)}), bf16[32,64,256]{2,1,0:T(8,128)(2,1)S(1)}, u32[]{:S(2)}, u32[]{:S(2)}) async-start(bf16[32,64,256]{2,1,0:T(8,128)(2,1)} %get-tuple-element.11), calls=%async_computation.1 | async-start | bytes 2097152 | tf_op jit(solution)/shard_map/all_to_all | solution.py:233
  51.4 6.3 %collective-permute-start = (bf16[272,256]{1,0:T(8,128)(2,1)S(1)}, bf16[272,256]{1,0:T(8,128)(2,1)S(1)}, u32[]{:S(2)}, u32[]{:S(2)}) collective-permute-start(bf16[272,256]{1,0:T(8,128)(2,1)S(1)} %get-tuple-element.14), channel_id=1, source_target_pairs={{0,8},{8,0},{1,9},{9,1},{2,10},{10,2},{3,11},{11,3},{4,12},{12,4},... | collective-permute-start | bytes 417800 | tf_op jit(solution)/shard_map/ppermute | solution.py:231
  54.4 8.3 %collective-permute-start.1 = (bf16[272,256]{1,0:T(8,128)(2,1)S(1)}, bf16[272,256]{1,0:T(8,128)(2,1)S(1)}, u32[]{:S(2)}, u32[]{:S(2)}) collective-permute-start(bf16[272,256]{1,0:T(8,128)(2,1)S(1)} %get-tuple-element.15), channel_id=1, source_target_pairs={{8,16},{16,8},{24,32},{32,24},{40,48},{48,40},{56,64},{64,56},{72,... | collective-permute-start | bytes 417800 | tf_op jit(solution)/shard_map/ppermute | solution.py:230
  63.0 14.7 %collective-permute-start.4 = (bf16[272,256]{1,0:T(8,128)(2,1)S(1)}, bf16[272,256]{1,0:T(8,128)(2,1)S(1)}, u32[]{:S(2)}, u32[]{:S(2)}) collective-permute-start(bf16[272,256]{1,0:T(8,128)(2,1)S(1)} %shard_map.89.own), channel_id=1, source_target_pairs={{0,48},{16,32},{32,16},{48,0},{1,49},{17,33},{33,17},{49,1},{2,50}... | collective-permute-start | bytes 417800 | tf_op jit(solution)/shard_map/ppermute | solution.py:242
  69.0 10.0 %collective-permute-start.3 = (bf16[272,256]{1,0:T(8,128)(2,1)S(1)}, bf16[272,256]{1,0:T(8,128)(2,1)S(1)}, u32[]{:S(2)}, u32[]{:S(2)}) collective-permute-start(bf16[272,256]{1,0:T(8,128)(2,1)S(1)} %shard_map.89.own), channel_id=1, source_target_pairs={{0,32},{16,48},{32,0},{48,16},{1,33},{17,49},{33,1},{49,17},{2,34}... | collective-permute-start | bytes 417800 | tf_op jit(solution)/shard_map/ppermute | solution.py:242
  70.9 8.7 %collective-permute-start.2 = (bf16[272,256]{1,0:T(8,128)(2,1)S(1)}, bf16[272,256]{1,0:T(8,128)(2,1)S(1)}, u32[]{:S(2)}, u32[]{:S(2)}) collective-permute-start(bf16[272,256]{1,0:T(8,128)(2,1)S(1)} %shard_map.89.own), channel_id=1, source_target_pairs={{0,16},{16,0},{32,48},{48,32},{1,17},{17,1},{33,49},{49,33},{2,18}... | collective-permute-start | bytes 417800 | tf_op jit(solution)/shard_map/ppermute | solution.py:242
  80.8 3.3 %collective-permute-start.5 = (bf16[8,80,128]{2,1,0:T(8,128)(2,1)S(1)}, bf16[8,80,128]{2,1,0:T(8,128)(2,1)S(1)}, u32[]{:S(2)}, u32[]{:S(2)}) collective-permute-start(bf16[8,80,128]{2,1,0:T(8,128)(2,1)S(1)} %get-tuple-element.17), channel_id=1, source_target_pairs={{0,8},{8,0},{1,9},{9,1},{2,10},{10,2},{3,11},{11,3},{4,12},{12,4},... | collective-permute-start | bytes 491528 | tf_op jit(solution)/shard_map/ppermute | solution.py:253

commit v8 on v7

--- a/solution.py
+++ b/solution.py
@@ -8,6 +8,7 @@
 BLK = 32
 EXTRA = 16
 LANES = 128
+STEPS = (1, 3, 2)
 ROWS_AXES = ("y", "x", "core")
 ORDER = (0, 2, 4, 6, 1, 3, 5, 7)
 VMEM = pl.BlockSpec(memory_space=pltpu.VMEM)
@@ -109,7 +110,7 @@
         out[rows:] = dot(column, unit(rows), ((0,), (0,)))[0:EXTRA].astype(out.dtype)
 
 
-def weighted_kernel(psi, own, inner, outer, carried):
+def weighted_kernel(psi, own, outer, inner, carried):
     rows, width = psi.shape
     total = own[0:rows] + inner[0:rows].astype(jnp.float32) + outer[0:rows].astype(jnp.float32)
     carried[0:rows] = total.astype(jnp.bfloat16)
@@ -128,7 +129,7 @@
     x = neighbours[0, 0] // (2 * (rows // BLK)) % group
     total = jnp.zeros((planes * chunk, width), jnp.float32)
     rhs = jnp.zeros((1, width), jnp.float32)
-    for step, cells in enumerate(carried):
+    for step, cells in zip((0,) + STEPS, carried):
         source = x ^ step
         turned = pieces[pl.ds(source * planes, planes)].reshape(planes * chunk, rows)
         total = total + dot(turned, cells[0:rows], ((1,), (0,)))
@@ -227,8 +228,8 @@
         compiler_params=PARAMS,
     )(neighbours, psi, metric_rows, target_column)
     next_chip = [(i, i + 2 * (i % 2) - 1) for i in range(1, devices - 1)]
+    inner = lax.ppermute(inner, "core", [(0, 1), (1, 0)])
     outer = lax.ppermute(outer, ROWS_AXES, next_chip)
-    inner = lax.ppermute(inner, "core", [(0, 1), (1, 0)])
     both = [part * planes + z for part in range(group) for z in ORDER]
     turned = lax.all_to_all(turned, ("x", "env"), 0, 0, tiled=True, axis_index_groups=[both])
     carried = pl.pallas_call(
@@ -237,9 +238,9 @@
         in_specs=[VMEM] * 4,
         out_specs=VMEM,
         compiler_params=PARAMS,
-    )(psi, own, inner, outer)
+    )(psi, own, outer, inner)
     shifted = [
-        lax.ppermute(carried, "x", [(i, i ^ step) for i in range(group)]) for step in range(1, group)
+        lax.ppermute(carried, "x", [(i, i ^ step) for i in range(group)]) for step in STEPS
     ]
     parts = (ys, 2 * BLK + EXTRA, width // 2)
     kept, sent = pl.pallas_call(

time: 100 us -> 98.2 us (0.982)
  waiting for transfers between devices: 36.4 us -> 33.7 us
  starting transfers between devices: 38 us -> 39 us
    ppermute x1, waiting for transfers between devices: 4.97 us -> 2.34 us  [per_device(): outer = lax.ppermute(outer, ROWS_AXES, next_chip)]
    ppermute x1, starting transfers between devices: 2.3 us -> 4.02 us  [per_device(): received = lax.ppermute(sent, 'core', [(0, 1), (1, 0)])]
    ppermute x1, starting transfers between devices: 2.98 us -> 1.92 us  [per_device(): inner = lax.ppermute(inner, 'core', [(0, 1), (1, 0)])]
    ppermute x1, starting transfers between devices: 3.32 us -> 4.37 us  [per_device(): outer = lax.ppermute(outer, ROWS_AXES, next_chip)]
  transfers between devices with their start and end apart: 8 -> 8, of which waited for: 6 -> 5; matrix products, arithmetic and copies ran while one was open for 1% -> 1% of each run, Pallas kernels for 2% -> 2%
where the time goes in v8:
time: 98.2 us; the launch traced here: 96.9 us
  starting transfers between devices  39 us (40%)
  waiting for transfers between devices  33.7 us (34%)
  blocking collectives  13.8 us (14%)
  Pallas kernels  8.29 us (8%)
  local copies, waits for them, and re-layouts  1.38 us (1%)
    all_to_all x1, waiting for transfers between devices, per_device(): lax.all_to_all(partial, 'env', 0, 0, tiled=True, axis_index_groups=[list(...  24.1 us
    all_to_all x1, blocking collectives, per_device(): lax.all_to_all(terms, 'y', 0, 0, tiled=True, axis_index_groups=[list(ORDE...  13.8 us
    all_to_all x1, starting transfers between devices, per_device(): lax.all_to_all(partial, 'env', 0, 0, tiled=True, axis_index_groups=[list(...  11 us
    ppermute x3, starting transfers between devices, per_device(): lax.ppermute(carried, 'x', [(i, i ^ step) for i in range(group)])  9.74 us
    all_to_all x1, starting transfers between devices, per_device(): lax.all_to_all(turned, ('x', 'env'), 0, 0, tiled=True, axis_index_groups=...  7.95 us
    ppermute x3, waiting for transfers between devices, per_device(): lax.ppermute(carried, 'x', [(i, i ^ step) for i in range(group)])  6.18 us
    ppermute x1, starting transfers between devices, per_device(): outer = lax.ppermute(outer, ROWS_AXES, next_chip)  4.37 us
    ppermute x1, starting transfers between devices, per_device(): received = lax.ppermute(sent, 'core', [(0, 1), (1, 0)])  4.02 us
  transfers between devices with their start and end apart: 8, of which 5 were waited for; matrix products, arithmetic and copies ran while one was open for 1% of the time, Pallas kernels for 2%

profile of v8, /device:TPU:1, one launch (start us, length us, event | category | flops | bytes accessed | tf_op | source)
XLA Modules:
  0.0 96.9 jit_solution(80413083905677820)
XLA Ops:
  0.6 3.1 %shard_map.86 = bf16[8,256,256]{2,1,0:T(8,128)(2,1)} custom-call(s32[8]{0:T(128)} %counts.1, bf16[256,1024]{1,0:T(8,128)(2,1)} %features.1, bf16[256,1024]{1,0:T(8,128)(2,1)} %environments.1, bf16[256,2048]{1,0:T(8,128)(2,1)} %projector.1), custom_call_target="tpu_custom_call" | custom-call | tf_op jit(solution)/shard_map/pallas_call | solution.py:197
  3.7 0.0 copy-start.1
  3.7 11.0 %all-to-all-start = ((bf16[8,256,256]{2,1,0:T(8,128)(2,1)}), bf16[8,256,256]{2,1,0:T(8,128)(2,1)S(1)}, u32[]{:S(2)}, u32[]{:S(2)}) async-start(bf16[8,256,256]{2,1,0:T(8,128)(2,1)} %shard_map.86), calls=%async_computation | async-start | bytes 2097152 | tf_op jit(solution)/shard_map/all_to_all | solution.py:213
  14.8 0.0 copy-start.2
  14.8 0.7 copy-done.2
  15.4 0.1 copy.11.target
  15.6 0.0 copy-done.1
  15.6 0.2 copy.10
  15.8 0.4 reshape.13.metric
  16.2 24.1 %all-to-all-done.parts = bf16[8,256,256]{2,1,0:T(8,128)(2,1)S(1)} async-done(((bf16[8,256,256]{2,1,0:T(8,128)(2,1)}), bf16[8,256,256]{2,1,0:T(8,128)(2,1)S(1)}, u32[]{:S(2)}, u32[]{:S(2)}) %all-to-all-start) | async-done | bytes 1048608 | tf_op jit(solution)/shard_map/all_to_all | solution.py:213
  40.3 1.3 %shard_map.87 = (bf16[256,256]{1,0:T(8,128)(2,1)S(1)}, bf16[32,64,256]{2,1,0:T(8,128)(2,1)}) custom-call(bf16[8,256,256]{2,1,0:T(8,128)(2,1)S(1)} %all-to-all-done.parts, bf16[256,256]{1,0:T(8,128)(2,1)S(1)} %reshape.13.metric, f32[256,1]{1,0:T(8,128)S(1)} %copy.11.target), custom_call_target="tpu_custom_call" | custom-call | tf_op jit(solution)/shard_map/pallas_call | solution.py:214
  41.6 0.0 copy-start
  41.6 8.0 %all-to-all-start.1 = ((bf16[32,64,256]{2,1,0:T(8,128)(2,1)}), bf16[32,64,256]{2,1,0:T(8,128)(2,1)S(1)}, u32[]{:S(2)}, u32[]{:S(2)}) async-start(bf16[32,64,256]{2,1,0:T(8,128)(2,1)} %get-tuple-element.11), calls=%async_computation.1 | async-start | bytes 2097152 | tf_op jit(solution)/shard_map/all_to_all | solution.py:234
  49.6 0.0 copy-done
  49.6 1.8 %shard_map.88 = (bf16[272,256]{1,0:T(8,128)(2,1)S(1)}, f32[272,256]{1,0:T(8,128)S(1)}, bf16[272,256]{1,0:T(8,128)(2,1)S(1)}) custom-call(s32[8,8]{1,0:T(8,128)S(1)} %copy-done, bf16[256,256]{1,0:T(8,128)(2,1)S(1)} %get-tuple-element.12.psi, bf16[256,256]{1,0:T(8,128)(2,1)S(1)} %reshape.13.metric, f32[256,1]{1,0:T(8,128)S(1)} %copy.11.target), custom_call_target="tpu_custom_call" | custom-call | tf_op jit(solution)/shard_map/pallas_call | solution.py:222
  51.5 4.4 %collective-permute-start = (bf16[272,256]{1,0:T(8,128)(2,1)S(1)}, bf16[272,256]{1,0:T(8,128)(2,1)S(1)}, u32[]{:S(2)}, u32[]{:S(2)}) collective-permute-start(bf16[272,256]{1,0:T(8,128)(2,1)S(1)} %get-tuple-element.14), channel_id=1, source_target_pairs={{8,16},{16,8},{24,32},{32,24},{40,48},{48,40},{56,64},{64,56},{72,... | collective-permute-start | bytes 417800 | tf_op jit(solution)/shard_map/ppermute | solution.py:232
  55.8 1.9 %collective-permute-start.1 = (bf16[272,256]{1,0:T(8,128)(2,1)S(1)}, bf16[272,256]{1,0:T(8,128)(2,1)S(1)}, u32[]{:S(2)}, u32[]{:S(2)}) collective-permute-start(bf16[272,256]{1,0:T(8,128)(2,1)S(1)} %get-tuple-element.15), channel_id=1, source_target_pairs={{0,8},{8,0},{1,9},{9,1},{2,10},{10,2},{3,11},{11,3},{4,12},{12,4},... | collective-permute-start | bytes 417800 | tf_op jit(solution)/shard_map/ppermute | solution.py:231
  57.8 2.3 %collective-permute-done.outer = bf16[272,256]{1,0:T(8,128)(2,1)S(1)} collective-permute-done((bf16[272,256]{1,0:T(8,128)(2,1)S(1)}, bf16[272,256]{1,0:T(8,128)(2,1)S(1)}, u32[]{:S(2)}, u32[]{:S(2)}) %collective-permute-start) | collective-permute-done | bytes 139296 | tf_op jit(solution)/shard_map/ppermute | solution.py:232
  60.1 0.0 collective-permute-done.1.inner
  60.1 0.2 shard_map.89.own
  60.3 4.4 %collective-permute-start.4 = (bf16[272,256]{1,0:T(8,128)(2,1)S(1)}, bf16[272,256]{1,0:T(8,128)(2,1)S(1)}, u32[]{:S(2)}, u32[]{:S(2)}) collective-permute-start(bf16[272,256]{1,0:T(8,128)(2,1)S(1)} %shard_map.89.own), channel_id=1, source_target_pairs={{0,32},{16,48},{32,0},{48,16},{1,33},{17,49},{33,1},{49,17},{2,34}... | collective-permute-start | bytes 417800 | tf_op jit(solution)/shard_map/ppermute | solution.py:243
  64.7 3.4 %collective-permute-start.3 = (bf16[272,256]{1,0:T(8,128)(2,1)S(1)}, bf16[272,256]{1,0:T(8,128)(2,1)S(1)}, u32[]{:S(2)}, u32[]{:S(2)}) collective-permute-start(bf16[272,256]{1,0:T(8,128)(2,1)S(1)} %shard_map.89.own), channel_id=1, source_target_pairs={{0,48},{16,32},{32,16},{48,0},{1,49},{17,33},{33,17},{49,1},{2,50}... | collective-permute-start | bytes 417800 | tf_op jit(solution)/shard_map/ppermute | solution.py:243
  68.2 1.9 %collective-permute-start.2 = (bf16[272,256]{1,0:T(8,128)(2,1)S(1)}, bf16[272,256]{1,0:T(8,128)(2,1)S(1)}, u32[]{:S(2)}, u32[]{:S(2)}) collective-permute-start(bf16[272,256]{1,0:T(8,128)(2,1)S(1)} %shard_map.89.own), channel_id=1, source_target_pairs={{0,16},{16,0},{32,48},{48,32},{1,17},{17,1},{33,49},{49,33},{2,18}... | collective-permute-start | bytes 417800 | tf_op jit(solution)/shard_map/ppermute | solution.py:243
  70.1 0.0 collective-permute-done.4.rest_2_
  70.1 4.6 %collective-permute-done.3.rest_1_ = bf16[272,256]{1,0:T(8,128)(2,1)S(1)} collective-permute-done((bf16[272,256]{1,0:T(8,128)(2,1)S(1)}, bf16[272,256]{1,0:T(8,128)(2,1)S(1)}, u32[]{:S(2)}, u32[]{:S(2)}) %collective-permute-start.3) | collective-permute-done | bytes 139296 | tf_op jit(solution)/shard_map/ppermute | solution.py:243
  74.7 1.5 %collective-permute-done.2.rest_0_ = bf16[272,256]{1,0:T(8,128)(2,1)S(1)} collective-permute-done((bf16[272,256]{1,0:T(8,128)(2,1)S(1)}, bf16[272,256]{1,0:T(8,128)(2,1)S(1)}, u32[]{:S(2)}, u32[]{:S(2)}) %collective-permute-start.2) | collective-permute-done | bytes 139296 | tf_op jit(solution)/shard_map/ppermute | solution.py:243
  76.3 0.0 all-to-all-done.1.pieces
  76.3 1.1 %shard_map.90 = (f32[8,80,128]{2,1,0:T(8,128)S(1)}, bf16[8,80,128]{2,1,0:T(8,128)(2,1)S(1)}) custom-call(s32[8,8]{1,0:T(8,128)S(1)} %copy-done, bf16[32,64,256]{2,1,0:T(8,128)(2,1)S(1)} %all-to-all-done.1.pieces, bf16[272,256]{1,0:T(8,128)(2,1)S(1)} %shard_map.89.own, bf16[272,256]{1,0:T(8,128)(2,1)S(1)} %collective-permute-done.2.rest_0_, ...), custom_call_target="tpu_custom_call" | custom-call | tf_op jit(solution)/shard_map/pallas_call | solution.py:246
  77.4 4.0 %collective-permute-start.5 = (bf16[8,80,128]{2,1,0:T(8,128)(2,1)S(1)}, bf16[8,80,128]{2,1,0:T(8,128)(2,1)S(1)}, u32[]{:S(2)}, u32[]{:S(2)}) collective-permute-start(bf16[8,80,128]{2,1,0:T(8,128)(2,1)S(1)} %get-tuple-element.17), channel_id=1, source_target_pairs={{0,8},{8,0},{1,9},{9,1},{2,10},{10,2},{3,11},{11,3},{4,12},{12,4},... | collective-permute-start | bytes 491528 | tf_op jit(solution)/shard_map/ppermute | solution.py:254
  81.4 1.0 %collective-permute-done.5.received = bf16[8,80,128]{2,1,0:T(8,128)(2,1)S(1)} collective-permute-done((bf16[8,80,128]{2,1,0:T(8,128)(2,1)S(1)}, bf16[8,80,128]{2,1,0:T(8,128)(2,1)S(1)}, u32[]{:S(2)}, u32[]{:S(2)}) %collective-permute-start.5) | collective-permute-done | bytes 163872 | tf_op jit(solution)/shard_map/ppermute | solution.py:254
  82.5 13.8 %all_to_all.15.parts = bf16[8,80,128]{2,1,0:T(8,128)(2,1)S(1)} all-to-all(bf16[8,80,128]{2,1,0:T(8,128)(2,1)S(1)} %shard_map.91), channel_id=1, replica_groups={{0,128,256,384,64,192,320,448},{1,129,257,385,65,193,321,449},{2,130,25..., dimensions={0} | all-to-all | bytes 327680 | tf_op jit(solution)/shard_map/all_to_all | solution.py:262
  96.3 0.6 shard_map.92
  (1 shorter events, 0.0 us)
Async XLA Ops:
  3.7 11.8 %copy-start.1 = (bf16[8,8,32,32]{3,2,1,0:T(8,128)(2,1)S(1)}, bf16[8,8,32,32]{3,2,1,0:T(8,128)(2,1)}, u32[]{:S(2)}) copy-start(bf16[8,8,32,32]{3,2,1,0:T(8,128)(2,1)} %param.10) | copy-start | bytes 393220
  3.7 36.6 %all-to-all-start = ((bf16[8,256,256]{2,1,0:T(8,128)(2,1)}), bf16[8,256,256]{2,1,0:T(8,128)(2,1)S(1)}, u32[]{:S(2)}, u32[]{:S(2)}) async-start(bf16[8,256,256]{2,1,0:T(8,128)(2,1)} %shard_map.86), calls=%async_computation | async-start | bytes 2097152 | tf_op jit(solution)/shard_map/all_to_all | solution.py:213
  14.8 0.7 copy-start.2
  41.6 8.0 %copy-start = (s32[8,8]{1,0:T(8,128)S(1)}, s32[8,8]{1,0:T(8,128)}, u32[]{:S(2)}) copy-start(s32[8,8]{1,0:T(8,128)} %neighbours.3) | copy-start | bytes 772
  41.6 34.6 %all-to-all-start.1 = ((bf16[32,64,256]{2,1,0:T(8,128)(2,1)}), bf16[32,64,256]{2,1,0:T(8,128)(2,1)S(1)}, u32[]{:S(2)}, u32[]{:S(2)}) async-start(bf16[32,64,256]{2,1,0:T(8,128)(2,1)} %get-tuple-element.11), calls=%async_computation.1 | async-start | bytes 2097152 | tf_op jit(solution)/shard_map/all_to_all | solution.py:234
  51.5 8.6 %collective-permute-start = (bf16[272,256]{1,0:T(8,128)(2,1)S(1)}, bf16[272,256]{1,0:T(8,128)(2,1)S(1)}, u32[]{:S(2)}, u32[]{:S(2)}) collective-permute-start(bf16[272,256]{1,0:T(8,128)(2,1)S(1)} %get-tuple-element.14), channel_id=1, source_target_pairs={{8,16},{16,8},{24,32},{32,24},{40,48},{48,40},{56,64},{64,56},{72,... | collective-permute-start | bytes 417800 | tf_op jit(solution)/shard_map/ppermute | solution.py:232
  55.8 4.3 %collective-permute-start.1 = (bf16[272,256]{1,0:T(8,128)(2,1)S(1)}, bf16[272,256]{1,0:T(8,128)(2,1)S(1)}, u32[]{:S(2)}, u32[]{:S(2)}) collective-permute-start(bf16[272,256]{1,0:T(8,128)(2,1)S(1)} %get-tuple-element.15), channel_id=1, source_target_pairs={{0,8},{8,0},{1,9},{9,1},{2,10},{10,2},{3,11},{11,3},{4,12},{12,4},... | collective-permute-start | bytes 417800 | tf_op jit(solution)/shard_map/ppermute | solution.py:231
  60.3 9.8 %collective-permute-start.4 = (bf16[272,256]{1,0:T(8,128)(2,1)S(1)}, bf16[272,256]{1,0:T(8,128)(2,1)S(1)}, u32[]{:S(2)}, u32[]{:S(2)}) collective-permute-start(bf16[272,256]{1,0:T(8,128)(2,1)S(1)} %shard_map.89.own), channel_id=1, source_target_pairs={{0,32},{16,48},{32,0},{48,16},{1,33},{17,49},{33,1},{49,17},{2,34}... | collective-permute-start | bytes 417800 | tf_op jit(solution)/shard_map/ppermute | solution.py:243
  64.7 10.0 %collective-permute-start.3 = (bf16[272,256]{1,0:T(8,128)(2,1)S(1)}, bf16[272,256]{1,0:T(8,128)(2,1)S(1)}, u32[]{:S(2)}, u32[]{:S(2)}) collective-permute-start(bf16[272,256]{1,0:T(8,128)(2,1)S(1)} %shard_map.89.own), channel_id=1, source_target_pairs={{0,48},{16,32},{32,16},{48,0},{1,49},{17,33},{33,17},{49,1},{2,50}... | collective-permute-start | bytes 417800 | tf_op jit(solution)/shard_map/ppermute | solution.py:243
  68.2 8.1 %collective-permute-start.2 = (bf16[272,256]{1,0:T(8,128)(2,1)S(1)}, bf16[272,256]{1,0:T(8,128)(2,1)S(1)}, u32[]{:S(2)}, u32[]{:S(2)}) collective-permute-start(bf16[272,256]{1,0:T(8,128)(2,1)S(1)} %shard_map.89.own), channel_id=1, source_target_pairs={{0,16},{16,0},{32,48},{48,32},{1,17},{17,1},{33,49},{49,33},{2,18}... | collective-permute-start | bytes 417800 | tf_op jit(solution)/shard_map/ppermute | solution.py:243
  77.4 5.0 %collective-permute-start.5 = (bf16[8,80,128]{2,1,0:T(8,128)(2,1)S(1)}, bf16[8,80,128]{2,1,0:T(8,128)(2,1)S(1)}, u32[]{:S(2)}, u32[]{:S(2)}) collective-permute-start(bf16[8,80,128]{2,1,0:T(8,128)(2,1)S(1)} %get-tuple-element.17), channel_id=1, source_target_pairs={{0,8},{8,0},{1,9},{9,1},{2,10},{10,2},{3,11},{11,3},{4,12},{12,4},... | collective-permute-start | bytes 491528 | tf_op jit(solution)/shard_map/ppermute | solution.py:254

commit v9 on v8

--- a/solution.py
+++ b/solution.py
@@ -11,6 +11,7 @@
 STEPS = (1, 3, 2)
 ROWS_AXES = ("y", "x", "core")
 ORDER = (0, 2, 4, 6, 1, 3, 5, 7)
+FIRST = (0, 4, 1, 5, 2, 6, 3, 7)
 VMEM = pl.BlockSpec(memory_space=pltpu.VMEM)
 SMEM = pl.BlockSpec(memory_space=pltpu.SMEM)
 ANY = pl.BlockSpec(memory_space=pl.ANY)
@@ -50,9 +51,9 @@
     for part in range(out.shape[0]):
         cols = slice(part * width, (part + 1) * width)
         parts[part] = dot(masked, weights[:, cols], ((1,), (0,))).astype(jnp.bfloat16)
-        pltpu.make_async_copy(parts.at[part], out.at[ORDER.index(part)], sent.at[part]).start()
+        pltpu.make_async_copy(parts.at[part], out.at[FIRST.index(part)], sent.at[part]).start()
     for part in range(out.shape[0]):
-        pltpu.make_async_copy(parts.at[part], out.at[ORDER.index(part)], sent.at[part]).wait()
+        pltpu.make_async_copy(parts.at[part], out.at[FIRST.index(part)], sent.at[part]).wait()
 
 
 def unit(size):
@@ -210,7 +211,7 @@
         ],
         compiler_params=WHOLE,
     )(counts, features, environments, projector)
-    partial = lax.all_to_all(partial, "env", 0, 0, tiled=True, axis_index_groups=[list(ORDER)])
+    partial = lax.all_to_all(partial, "env", 0, 0, tiled=True, axis_index_groups=[list(FIRST)])
     psi, turned = pl.pallas_call(
         sum_kernel,
         out_shape=(shape((slab, width), bf16), shape((group * planes, width // group, slab), bf16)),

time: 98.2 us -> 98.1 us (level)
  waiting for transfers between devices: 33.7 us -> 31.6 us
  starting transfers between devices: 39 us -> 40.9 us
    all_to_all x1, waiting for transfers between devices: 24.1 us -> 22.1 us  [per_device(): lax.all_to_all(partial, 'env', 0, 0, tiled=True, axis_index_groups=[list(...]
    all_to_all x1, starting transfers between devices: 7.95 us -> 9.85 us  [per_device(): lax.all_to_all(turned, ('x', 'env'), 0, 0, tiled=True, axis_index_groups=...]
where the time goes in v9:
time: 98.1 us; the launch traced here: 96.7 us
  starting transfers between devices  40.9 us (42%)
  waiting for transfers between devices  31.6 us (32%)
  blocking collectives  13.8 us (14%)
  Pallas kernels  8.26 us (8%)
  local copies, waits for them, and re-layouts  1.38 us (1%)
    all_to_all x1, waiting for transfers between devices, per_device(): lax.all_to_all(partial, 'env', 0, 0, tiled=True, axis_index_groups=[list(...  22.1 us
    all_to_all x1, blocking collectives, per_device(): lax.all_to_all(terms, 'y', 0, 0, tiled=True, axis_index_groups=[list(ORDE...  13.8 us
    all_to_all x1, starting transfers between devices, per_device(): lax.all_to_all(partial, 'env', 0, 0, tiled=True, axis_index_groups=[list(...  11 us
    all_to_all x1, starting transfers between devices, per_device(): lax.all_to_all(turned, ('x', 'env'), 0, 0, tiled=True, axis_index_groups=...  9.85 us
    ppermute x3, starting transfers between devices, per_device(): lax.ppermute(carried, 'x', [(i, i ^ step) for i in range(group)])  9.65 us
    ppermute x3, waiting for transfers between devices, per_device(): lax.ppermute(carried, 'x', [(i, i ^ step) for i in range(group)])  6.11 us
    ppermute x1, starting transfers between devices, per_device(): outer = lax.ppermute(outer, ROWS_AXES, next_chip)  4.5 us
    ppermute x1, starting transfers between devices, per_device(): received = lax.ppermute(sent, 'core', [(0, 1), (1, 0)])  3.99 us
  transfers between devices with their start and end apart: 8, of which 5 were waited for; matrix products, arithmetic and copies ran while one was open for 1% of the time, Pallas kernels for 2%

profile of v9, /device:TPU:1, one launch (start us, length us, event | category | flops | bytes accessed | tf_op | source)
XLA Modules:
  0.0 96.7 jit_solution(10393847975963732343)
XLA Ops:
  0.6 3.1 %shard_map.86 = bf16[8,256,256]{2,1,0:T(8,128)(2,1)} custom-call(s32[8]{0:T(128)} %counts.1, bf16[256,1024]{1,0:T(8,128)(2,1)} %features.1, bf16[256,1024]{1,0:T(8,128)(2,1)} %environments.1, bf16[256,2048]{1,0:T(8,128)(2,1)} %projector.1), custom_call_target="tpu_custom_call" | custom-call | tf_op jit(solution)/shard_map/pallas_call | solution.py:198
  3.7 0.0 copy-start.1
  3.7 11.0 %all-to-all-start = ((bf16[8,256,256]{2,1,0:T(8,128)(2,1)}), bf16[8,256,256]{2,1,0:T(8,128)(2,1)S(1)}, u32[]{:S(2)}, u32[]{:S(2)}) async-start(bf16[8,256,256]{2,1,0:T(8,128)(2,1)} %shard_map.86), calls=%async_computation | async-start | bytes 2097152 | tf_op jit(solution)/shard_map/all_to_all | solution.py:214
  14.7 0.0 copy-start.2
  14.7 0.7 copy-done.2
  15.4 0.1 copy.11.target
  15.5 0.0 copy-done.1
  15.6 0.2 copy.10
  15.8 0.4 reshape.13.metric
  16.1 22.1 %all-to-all-done.parts = bf16[8,256,256]{2,1,0:T(8,128)(2,1)S(1)} async-done(((bf16[8,256,256]{2,1,0:T(8,128)(2,1)}), bf16[8,256,256]{2,1,0:T(8,128)(2,1)S(1)}, u32[]{:S(2)}, u32[]{:S(2)}) %all-to-all-start) | async-done | bytes 1048608 | tf_op jit(solution)/shard_map/all_to_all | solution.py:214
  38.2 1.3 %shard_map.87 = (bf16[256,256]{1,0:T(8,128)(2,1)S(1)}, bf16[32,64,256]{2,1,0:T(8,128)(2,1)}) custom-call(bf16[8,256,256]{2,1,0:T(8,128)(2,1)S(1)} %all-to-all-done.parts, bf16[256,256]{1,0:T(8,128)(2,1)S(1)} %reshape.13.metric, f32[256,1]{1,0:T(8,128)S(1)} %copy.11.target), custom_call_target="tpu_custom_call" | custom-call | tf_op jit(solution)/shard_map/pallas_call | solution.py:215
  39.6 0.0 copy-start
  39.6 9.8 %all-to-all-start.1 = ((bf16[32,64,256]{2,1,0:T(8,128)(2,1)}), bf16[32,64,256]{2,1,0:T(8,128)(2,1)S(1)}, u32[]{:S(2)}, u32[]{:S(2)}) async-start(bf16[32,64,256]{2,1,0:T(8,128)(2,1)} %get-tuple-element.11), calls=%async_computation.1 | async-start | bytes 2097152 | tf_op jit(solution)/shard_map/all_to_all | solution.py:235
  49.4 0.0 copy-done
  49.4 1.8 %shard_map.88 = (bf16[272,256]{1,0:T(8,128)(2,1)S(1)}, f32[272,256]{1,0:T(8,128)S(1)}, bf16[272,256]{1,0:T(8,128)(2,1)S(1)}) custom-call(s32[8,8]{1,0:T(8,128)S(1)} %copy-done, bf16[256,256]{1,0:T(8,128)(2,1)S(1)} %get-tuple-element.12.psi, bf16[256,256]{1,0:T(8,128)(2,1)S(1)} %reshape.13.metric, f32[256,1]{1,0:T(8,128)S(1)} %copy.11.target), custom_call_target="tpu_custom_call" | custom-call | tf_op jit(solution)/shard_map/pallas_call | solution.py:223
  51.3 4.5 %collective-permute-start = (bf16[272,256]{1,0:T(8,128)(2,1)S(1)}, bf16[272,256]{1,0:T(8,128)(2,1)S(1)}, u32[]{:S(2)}, u32[]{:S(2)}) collective-permute-start(bf16[272,256]{1,0:T(8,128)(2,1)S(1)} %get-tuple-element.14), channel_id=1, source_target_pairs={{8,16},{16,8},{24,32},{32,24},{40,48},{48,40},{56,64},{64,56},{72,... | collective-permute-start | bytes 417800 | tf_op jit(solution)/shard_map/ppermute | solution.py:233
  55.8 1.9 %collective-permute-start.1 = (bf16[272,256]{1,0:T(8,128)(2,1)S(1)}, bf16[272,256]{1,0:T(8,128)(2,1)S(1)}, u32[]{:S(2)}, u32[]{:S(2)}) collective-permute-start(bf16[272,256]{1,0:T(8,128)(2,1)S(1)} %get-tuple-element.15), channel_id=1, source_target_pairs={{0,8},{8,0},{1,9},{9,1},{2,10},{10,2},{3,11},{11,3},{4,12},{12,4},... | collective-permute-start | bytes 417800 | tf_op jit(solution)/shard_map/ppermute | solution.py:232
  57.7 2.4 %collective-permute-done.outer = bf16[272,256]{1,0:T(8,128)(2,1)S(1)} collective-permute-done((bf16[272,256]{1,0:T(8,128)(2,1)S(1)}, bf16[272,256]{1,0:T(8,128)(2,1)S(1)}, u32[]{:S(2)}, u32[]{:S(2)}) %collective-permute-start) | collective-permute-done | bytes 139296 | tf_op jit(solution)/shard_map/ppermute | solution.py:233
  60.1 0.0 collective-permute-done.1.inner
  60.1 0.2 shard_map.89.own
  60.3 4.3 %collective-permute-start.4 = (bf16[272,256]{1,0:T(8,128)(2,1)S(1)}, bf16[272,256]{1,0:T(8,128)(2,1)S(1)}, u32[]{:S(2)}, u32[]{:S(2)}) collective-permute-start(bf16[272,256]{1,0:T(8,128)(2,1)S(1)} %shard_map.89.own), channel_id=1, source_target_pairs={{0,32},{16,48},{32,0},{48,16},{1,33},{17,49},{33,1},{49,17},{2,34}... | collective-permute-start | bytes 417800 | tf_op jit(solution)/shard_map/ppermute | solution.py:244
  64.7 3.4 %collective-permute-start.3 = (bf16[272,256]{1,0:T(8,128)(2,1)S(1)}, bf16[272,256]{1,0:T(8,128)(2,1)S(1)}, u32[]{:S(2)}, u32[]{:S(2)}) collective-permute-start(bf16[272,256]{1,0:T(8,128)(2,1)S(1)} %shard_map.89.own), channel_id=1, source_target_pairs={{0,48},{16,32},{32,16},{48,0},{1,49},{17,33},{33,17},{49,1},{2,50}... | collective-permute-start | bytes 417800 | tf_op jit(solution)/shard_map/ppermute | solution.py:244
  68.1 1.9 %collective-permute-start.2 = (bf16[272,256]{1,0:T(8,128)(2,1)S(1)}, bf16[272,256]{1,0:T(8,128)(2,1)S(1)}, u32[]{:S(2)}, u32[]{:S(2)}) collective-permute-start(bf16[272,256]{1,0:T(8,128)(2,1)S(1)} %shard_map.89.own), channel_id=1, source_target_pairs={{0,16},{16,0},{32,48},{48,32},{1,17},{17,1},{33,49},{49,33},{2,18}... | collective-permute-start | bytes 417800 | tf_op jit(solution)/shard_map/ppermute | solution.py:244
  70.0 0.0 collective-permute-done.4.rest_2_
  70.0 4.9 %collective-permute-done.3.rest_1_ = bf16[272,256]{1,0:T(8,128)(2,1)S(1)} collective-permute-done((bf16[272,256]{1,0:T(8,128)(2,1)S(1)}, bf16[272,256]{1,0:T(8,128)(2,1)S(1)}, u32[]{:S(2)}, u32[]{:S(2)}) %collective-permute-start.3) | collective-permute-done | bytes 139296 | tf_op jit(solution)/shard_map/ppermute | solution.py:244
  74.9 1.2 %collective-permute-done.2.rest_0_ = bf16[272,256]{1,0:T(8,128)(2,1)S(1)} collective-permute-done((bf16[272,256]{1,0:T(8,128)(2,1)S(1)}, bf16[272,256]{1,0:T(8,128)(2,1)S(1)}, u32[]{:S(2)}, u32[]{:S(2)}) %collective-permute-start.2) | collective-permute-done | bytes 139296 | tf_op jit(solution)/shard_map/ppermute | solution.py:244
  76.1 0.0 all-to-all-done.1.pieces
  76.1 1.1 %shard_map.90 = (f32[8,80,128]{2,1,0:T(8,128)S(1)}, bf16[8,80,128]{2,1,0:T(8,128)(2,1)S(1)}) custom-call(s32[8,8]{1,0:T(8,128)S(1)} %copy-done, bf16[32,64,256]{2,1,0:T(8,128)(2,1)S(1)} %all-to-all-done.1.pieces, bf16[272,256]{1,0:T(8,128)(2,1)S(1)} %shard_map.89.own, bf16[272,256]{1,0:T(8,128)(2,1)S(1)} %collective-permute-done.2.rest_0_, ...), custom_call_target="tpu_custom_call" | custom-call | tf_op jit(solution)/shard_map/pallas_call | solution.py:247
  77.3 4.0 %collective-permute-start.5 = (bf16[8,80,128]{2,1,0:T(8,128)(2,1)S(1)}, bf16[8,80,128]{2,1,0:T(8,128)(2,1)S(1)}, u32[]{:S(2)}, u32[]{:S(2)}) collective-permute-start(bf16[8,80,128]{2,1,0:T(8,128)(2,1)S(1)} %get-tuple-element.17), channel_id=1, source_target_pairs={{0,8},{8,0},{1,9},{9,1},{2,10},{10,2},{3,11},{11,3},{4,12},{12,4},... | collective-permute-start | bytes 491528 | tf_op jit(solution)/shard_map/ppermute | solution.py:255
  81.3 1.0 %collective-permute-done.5.received = bf16[8,80,128]{2,1,0:T(8,128)(2,1)S(1)} collective-permute-done((bf16[8,80,128]{2,1,0:T(8,128)(2,1)S(1)}, bf16[8,80,128]{2,1,0:T(8,128)(2,1)S(1)}, u32[]{:S(2)}, u32[]{:S(2)}) %collective-permute-start.5) | collective-permute-done | bytes 163872 | tf_op jit(solution)/shard_map/ppermute | solution.py:255
  82.3 13.8 %all_to_all.15.parts = bf16[8,80,128]{2,1,0:T(8,128)(2,1)S(1)} all-to-all(bf16[8,80,128]{2,1,0:T(8,128)(2,1)S(1)} %shard_map.91), channel_id=1, replica_groups={{0,128,256,384,64,192,320,448},{1,129,257,385,65,193,321,449},{2,130,25..., dimensions={0} | all-to-all | bytes 327680 | tf_op jit(solution)/shard_map/all_to_all | solution.py:263
  96.1 0.6 shard_map.92
  (1 shorter events, 0.0 us)
Async XLA Ops:
  3.7 11.8 %copy-start.1 = (bf16[8,8,32,32]{3,2,1,0:T(8,128)(2,1)S(1)}, bf16[8,8,32,32]{3,2,1,0:T(8,128)(2,1)}, u32[]{:S(2)}) copy-start(bf16[8,8,32,32]{3,2,1,0:T(8,128)(2,1)} %param.10) | copy-start | bytes 393220
  3.7 34.5 %all-to-all-start = ((bf16[8,256,256]{2,1,0:T(8,128)(2,1)}), bf16[8,256,256]{2,1,0:T(8,128)(2,1)S(1)}, u32[]{:S(2)}, u32[]{:S(2)}) async-start(bf16[8,256,256]{2,1,0:T(8,128)(2,1)} %shard_map.86), calls=%async_computation | async-start | bytes 2097152 | tf_op jit(solution)/shard_map/all_to_all | solution.py:214
  14.7 0.7 copy-start.2
  39.6 9.9 %copy-start = (s32[8,8]{1,0:T(8,128)S(1)}, s32[8,8]{1,0:T(8,128)}, u32[]{:S(2)}) copy-start(s32[8,8]{1,0:T(8,128)} %neighbours.3) | copy-start | bytes 772
  39.6 36.6 %all-to-all-start.1 = ((bf16[32,64,256]{2,1,0:T(8,128)(2,1)}), bf16[32,64,256]{2,1,0:T(8,128)(2,1)S(1)}, u32[]{:S(2)}, u32[]{:S(2)}) async-start(bf16[32,64,256]{2,1,0:T(8,128)(2,1)} %get-tuple-element.11), calls=%async_computation.1 | async-start | bytes 2097152 | tf_op jit(solution)/shard_map/all_to_all | solution.py:235
  51.3 8.8 %collective-permute-start = (bf16[272,256]{1,0:T(8,128)(2,1)S(1)}, bf16[272,256]{1,0:T(8,128)(2,1)S(1)}, u32[]{:S(2)}, u32[]{:S(2)}) collective-permute-start(bf16[272,256]{1,0:T(8,128)(2,1)S(1)} %get-tuple-element.14), channel_id=1, source_target_pairs={{8,16},{16,8},{24,32},{32,24},{40,48},{48,40},{56,64},{64,56},{72,... | collective-permute-start | bytes 417800 | tf_op jit(solution)/shard_map/ppermute | solution.py:233
  55.8 4.3 %collective-permute-start.1 = (bf16[272,256]{1,0:T(8,128)(2,1)S(1)}, bf16[272,256]{1,0:T(8,128)(2,1)S(1)}, u32[]{:S(2)}, u32[]{:S(2)}) collective-permute-start(bf16[272,256]{1,0:T(8,128)(2,1)S(1)} %get-tuple-element.15), channel_id=1, source_target_pairs={{0,8},{8,0},{1,9},{9,1},{2,10},{10,2},{3,11},{11,3},{4,12},{12,4},... | collective-permute-start | bytes 417800 | tf_op jit(solution)/shard_map/ppermute | solution.py:232
  60.3 9.7 %collective-permute-start.4 = (bf16[272,256]{1,0:T(8,128)(2,1)S(1)}, bf16[272,256]{1,0:T(8,128)(2,1)S(1)}, u32[]{:S(2)}, u32[]{:S(2)}) collective-permute-start(bf16[272,256]{1,0:T(8,128)(2,1)S(1)} %shard_map.89.own), channel_id=1, source_target_pairs={{0,32},{16,48},{32,0},{48,16},{1,33},{17,49},{33,1},{49,17},{2,34}... | collective-permute-start | bytes 417800 | tf_op jit(solution)/shard_map/ppermute | solution.py:244
  64.7 10.2 %collective-permute-start.3 = (bf16[272,256]{1,0:T(8,128)(2,1)S(1)}, bf16[272,256]{1,0:T(8,128)(2,1)S(1)}, u32[]{:S(2)}, u32[]{:S(2)}) collective-permute-start(bf16[272,256]{1,0:T(8,128)(2,1)S(1)} %shard_map.89.own), channel_id=1, source_target_pairs={{0,48},{16,32},{32,16},{48,0},{1,49},{17,33},{33,17},{49,1},{2,50}... | collective-permute-start | bytes 417800 | tf_op jit(solution)/shard_map/ppermute | solution.py:244
  68.1 8.0 %collective-permute-start.2 = (bf16[272,256]{1,0:T(8,128)(2,1)S(1)}, bf16[272,256]{1,0:T(8,128)(2,1)S(1)}, u32[]{:S(2)}, u32[]{:S(2)}) collective-permute-start(bf16[272,256]{1,0:T(8,128)(2,1)S(1)} %shard_map.89.own), channel_id=1, source_target_pairs={{0,16},{16,0},{32,48},{48,32},{1,17},{17,1},{33,49},{49,33},{2,18}... | collective-permute-start | bytes 417800 | tf_op jit(solution)/shard_map/ppermute | solution.py:244
  77.3 5.0 %collective-permute-start.5 = (bf16[8,80,128]{2,1,0:T(8,128)(2,1)S(1)}, bf16[8,80,128]{2,1,0:T(8,128)(2,1)S(1)}, u32[]{:S(2)}, u32[]{:S(2)}) collective-permute-start(bf16[8,80,128]{2,1,0:T(8,128)(2,1)S(1)} %get-tuple-element.17), channel_id=1, source_target_pairs={{0,8},{8,0},{1,9},{9,1},{2,10},{10,2},{3,11},{11,3},{4,12},{12,4},... | collective-permute-start | bytes 491528 | tf_op jit(solution)/shard_map/ppermute | solution.py:255

commit v10 on v9

--- a/solution.py
+++ b/solution.py
@@ -143,14 +143,15 @@
     row = lax.broadcasted_iota(jnp.int32, (EXTRA, half), 0)
     tail = jnp.where(row == 0, rhs[:, :half], jnp.where(row == 2, rhs[:, half:], 0.0))
     for part in range(kept.shape[0]):
+        place = FIRST.index(ORDER[part])
         here = block[pl.ds(pl.multiple_of((2 * part + core) * BLK, BLK), BLK), :]
-        kept[part, 0:BLK] = here[:, :half]
-        kept[part, BLK:2 * BLK] = here[:, half:]
-        kept[part, 2 * BLK:] = tail
+        kept[place, 0:BLK] = here[:, :half]
+        kept[place, BLK:2 * BLK] = here[:, half:]
+        kept[place, 2 * BLK:] = tail
         here = block[pl.ds(pl.multiple_of((2 * part + 1 - core) * BLK, BLK), BLK), :].astype(jnp.bfloat16)
-        sent[part, 0:BLK] = here[:, :half]
-        sent[part, BLK:2 * BLK] = here[:, half:]
-        sent[part, 2 * BLK:] = split_rows(tail)
+        sent[place, 0:BLK] = here[:, :half]
+        sent[place, BLK:2 * BLK] = here[:, half:]
+        sent[place, 2 * BLK:] = split_rows(tail)
 
 
 def split_rows(tail):
@@ -260,7 +261,7 @@
         out_specs=VMEM,
         compiler_params=PARAMS,
     )(kept, received)
-    terms = lax.all_to_all(terms, "y", 0, 0, tiled=True, axis_index_groups=[list(ORDER)])
+    terms = lax.all_to_all(terms, "y", 0, 0, tiled=True, axis_index_groups=[list(FIRST)])
 
     def finish(parts, gram, rhs):
         final_kernel(parts, gram, rhs, factor=1.0 / (slab * devices) ** 0.5)

time: 98.1 us -> 98.1 us (level)
  no operation moved by 1% of the time
where the time goes in v10:
time: 98.1 us; the launch traced here: 96.4 us
  starting transfers between devices  40.9 us (42%)
  waiting for transfers between devices  31.6 us (32%)
  blocking collectives  13.4 us (14%)
  Pallas kernels  8.26 us (8%)
  local copies, waits for them, and re-layouts  1.38 us (1%)
    all_to_all x1, waiting for transfers between devices, per_device(): lax.all_to_all(partial, 'env', 0, 0, tiled=True, axis_index_groups=[list(...  22.1 us
    all_to_all x1, blocking collectives, per_device(): lax.all_to_all(terms, 'y', 0, 0, tiled=True, axis_index_groups=[list(FIRS...  13.4 us
    all_to_all x1, starting transfers between devices, per_device(): lax.all_to_all(partial, 'env', 0, 0, tiled=True, axis_index_groups=[list(...  11 us
    all_to_all x1, starting transfers between devices, per_device(): lax.all_to_all(turned, ('x', 'env'), 0, 0, tiled=True, axis_index_groups=...  9.85 us
    ppermute x3, starting transfers between devices, per_device(): lax.ppermute(carried, 'x', [(i, i ^ step) for i in range(group)])  9.64 us
    ppermute x3, waiting for transfers between devices, per_device(): lax.ppermute(carried, 'x', [(i, i ^ step) for i in range(group)])  6.09 us
    ppermute x1, starting transfers between devices, per_device(): outer = lax.ppermute(outer, ROWS_AXES, next_chip)  4.5 us
    ppermute x1, starting transfers between devices, per_device(): received = lax.ppermute(sent, 'core', [(0, 1), (1, 0)])  4.01 us
  transfers between devices with their start and end apart: 8, of which 5 were waited for; matrix products, arithmetic and copies ran while one was open for 1% of the time, Pallas kernels for 2%

profile of v10, /device:TPU:1, one launch (start us, length us, event | category | flops | bytes accessed | tf_op | source)
XLA Modules:
  0.0 96.4 jit_solution(14652912351974606486)
XLA Ops:
  0.6 3.1 %shard_map.86 = bf16[8,256,256]{2,1,0:T(8,128)(2,1)} custom-call(s32[8]{0:T(128)} %counts.1, bf16[256,1024]{1,0:T(8,128)(2,1)} %features.1, bf16[256,1024]{1,0:T(8,128)(2,1)} %environments.1, bf16[256,2048]{1,0:T(8,128)(2,1)} %projector.1), custom_call_target="tpu_custom_call" | custom-call | tf_op jit(solution)/shard_map/pallas_call | solution.py:199
  3.7 0.0 copy-start.1
  3.7 11.0 %all-to-all-start = ((bf16[8,256,256]{2,1,0:T(8,128)(2,1)}), bf16[8,256,256]{2,1,0:T(8,128)(2,1)S(1)}, u32[]{:S(2)}, u32[]{:S(2)}) async-start(bf16[8,256,256]{2,1,0:T(8,128)(2,1)} %shard_map.86), calls=%async_computation | async-start | bytes 2097152 | tf_op jit(solution)/shard_map/all_to_all | solution.py:215
  14.7 0.0 copy-start.2
  14.7 0.7 copy-done.2
  15.4 0.1 copy.11.target
  15.5 0.0 copy-done.1
  15.6 0.2 copy.10
  15.8 0.4 reshape.13.metric
  16.1 22.1 %all-to-all-done.parts = bf16[8,256,256]{2,1,0:T(8,128)(2,1)S(1)} async-done(((bf16[8,256,256]{2,1,0:T(8,128)(2,1)}), bf16[8,256,256]{2,1,0:T(8,128)(2,1)S(1)}, u32[]{:S(2)}, u32[]{:S(2)}) %all-to-all-start) | async-done | bytes 1048608 | tf_op jit(solution)/shard_map/all_to_all | solution.py:215
  38.2 1.3 %shard_map.87 = (bf16[256,256]{1,0:T(8,128)(2,1)S(1)}, bf16[32,64,256]{2,1,0:T(8,128)(2,1)}) custom-call(bf16[8,256,256]{2,1,0:T(8,128)(2,1)S(1)} %all-to-all-done.parts, bf16[256,256]{1,0:T(8,128)(2,1)S(1)} %reshape.13.metric, f32[256,1]{1,0:T(8,128)S(1)} %copy.11.target), custom_call_target="tpu_custom_call" | custom-call | tf_op jit(solution)/shard_map/pallas_call | solution.py:216
  39.6 0.0 copy-start
  39.6 9.8 %all-to-all-start.1 = ((bf16[32,64,256]{2,1,0:T(8,128)(2,1)}), bf16[32,64,256]{2,1,0:T(8,128)(2,1)S(1)}, u32[]{:S(2)}, u32[]{:S(2)}) async-start(bf16[32,64,256]{2,1,0:T(8,128)(2,1)} %get-tuple-element.11), calls=%async_computation.1 | async-start | bytes 2097152 | tf_op jit(solution)/shard_map/all_to_all | solution.py:236
  49.4 0.0 copy-done
  49.4 1.8 %shard_map.88 = (bf16[272,256]{1,0:T(8,128)(2,1)S(1)}, f32[272,256]{1,0:T(8,128)S(1)}, bf16[272,256]{1,0:T(8,128)(2,1)S(1)}) custom-call(s32[8,8]{1,0:T(8,128)S(1)} %copy-done, bf16[256,256]{1,0:T(8,128)(2,1)S(1)} %get-tuple-element.12.psi, bf16[256,256]{1,0:T(8,128)(2,1)S(1)} %reshape.13.metric, f32[256,1]{1,0:T(8,128)S(1)} %copy.11.target), custom_call_target="tpu_custom_call" | custom-call | tf_op jit(solution)/shard_map/pallas_call | solution.py:224
  51.3 4.5 %collective-permute-start = (bf16[272,256]{1,0:T(8,128)(2,1)S(1)}, bf16[272,256]{1,0:T(8,128)(2,1)S(1)}, u32[]{:S(2)}, u32[]{:S(2)}) collective-permute-start(bf16[272,256]{1,0:T(8,128)(2,1)S(1)} %get-tuple-element.14), channel_id=1, source_target_pairs={{8,16},{16,8},{24,32},{32,24},{40,48},{48,40},{56,64},{64,56},{72,... | collective-permute-start | bytes 417800 | tf_op jit(solution)/shard_map/ppermute | solution.py:234
  55.8 1.9 %collective-permute-start.1 = (bf16[272,256]{1,0:T(8,128)(2,1)S(1)}, bf16[272,256]{1,0:T(8,128)(2,1)S(1)}, u32[]{:S(2)}, u32[]{:S(2)}) collective-permute-start(bf16[272,256]{1,0:T(8,128)(2,1)S(1)} %get-tuple-element.15), channel_id=1, source_target_pairs={{0,8},{8,0},{1,9},{9,1},{2,10},{10,2},{3,11},{11,3},{4,12},{12,4},... | collective-permute-start | bytes 417800 | tf_op jit(solution)/shard_map/ppermute | solution.py:233
  57.7 2.4 %collective-permute-done.outer = bf16[272,256]{1,0:T(8,128)(2,1)S(1)} collective-permute-done((bf16[272,256]{1,0:T(8,128)(2,1)S(1)}, bf16[272,256]{1,0:T(8,128)(2,1)S(1)}, u32[]{:S(2)}, u32[]{:S(2)}) %collective-permute-start) | collective-permute-done | bytes 139296 | tf_op jit(solution)/shard_map/ppermute | solution.py:234
  60.1 0.0 collective-permute-done.1.inner
  60.1 0.2 shard_map.89.own
  60.3 4.4 %collective-permute-start.4 = (bf16[272,256]{1,0:T(8,128)(2,1)S(1)}, bf16[272,256]{1,0:T(8,128)(2,1)S(1)}, u32[]{:S(2)}, u32[]{:S(2)}) collective-permute-start(bf16[272,256]{1,0:T(8,128)(2,1)S(1)} %shard_map.89.own), channel_id=1, source_target_pairs={{0,32},{16,48},{32,0},{48,16},{1,33},{17,49},{33,1},{49,17},{2,34}... | collective-permute-start | bytes 417800 | tf_op jit(solution)/shard_map/ppermute | solution.py:245
  64.7 3.4 %collective-permute-start.3 = (bf16[272,256]{1,0:T(8,128)(2,1)S(1)}, bf16[272,256]{1,0:T(8,128)(2,1)S(1)}, u32[]{:S(2)}, u32[]{:S(2)}) collective-permute-start(bf16[272,256]{1,0:T(8,128)(2,1)S(1)} %shard_map.89.own), channel_id=1, source_target_pairs={{0,48},{16,32},{32,16},{48,0},{1,49},{17,33},{33,17},{49,1},{2,50}... | collective-permute-start | bytes 417800 | tf_op jit(solution)/shard_map/ppermute | solution.py:245
  68.1 1.9 %collective-permute-start.2 = (bf16[272,256]{1,0:T(8,128)(2,1)S(1)}, bf16[272,256]{1,0:T(8,128)(2,1)S(1)}, u32[]{:S(2)}, u32[]{:S(2)}) collective-permute-start(bf16[272,256]{1,0:T(8,128)(2,1)S(1)} %shard_map.89.own), channel_id=1, source_target_pairs={{0,16},{16,0},{32,48},{48,32},{1,17},{17,1},{33,49},{49,33},{2,18}... | collective-permute-start | bytes 417800 | tf_op jit(solution)/shard_map/ppermute | solution.py:245
  70.0 0.0 collective-permute-done.4.rest_2_
  70.0 4.9 %collective-permute-done.3.rest_1_ = bf16[272,256]{1,0:T(8,128)(2,1)S(1)} collective-permute-done((bf16[272,256]{1,0:T(8,128)(2,1)S(1)}, bf16[272,256]{1,0:T(8,128)(2,1)S(1)}, u32[]{:S(2)}, u32[]{:S(2)}) %collective-permute-start.3) | collective-permute-done | bytes 139296 | tf_op jit(solution)/shard_map/ppermute | solution.py:245
  74.9 1.2 %collective-permute-done.2.rest_0_ = bf16[272,256]{1,0:T(8,128)(2,1)S(1)} collective-permute-done((bf16[272,256]{1,0:T(8,128)(2,1)S(1)}, bf16[272,256]{1,0:T(8,128)(2,1)S(1)}, u32[]{:S(2)}, u32[]{:S(2)}) %collective-permute-start.2) | collective-permute-done | bytes 139296 | tf_op jit(solution)/shard_map/ppermute | solution.py:245
  76.1 0.0 all-to-all-done.1.pieces
  76.1 1.1 %shard_map.90 = (f32[8,80,128]{2,1,0:T(8,128)S(1)}, bf16[8,80,128]{2,1,0:T(8,128)(2,1)S(1)}) custom-call(s32[8,8]{1,0:T(8,128)S(1)} %copy-done, bf16[32,64,256]{2,1,0:T(8,128)(2,1)S(1)} %all-to-all-done.1.pieces, bf16[272,256]{1,0:T(8,128)(2,1)S(1)} %shard_map.89.own, bf16[272,256]{1,0:T(8,128)(2,1)S(1)} %collective-permute-done.2.rest_0_, ...), custom_call_target="tpu_custom_call" | custom-call | tf_op jit(solution)/shard_map/pallas_call | solution.py:248
  77.2 4.0 %collective-permute-start.5 = (bf16[8,80,128]{2,1,0:T(8,128)(2,1)S(1)}, bf16[8,80,128]{2,1,0:T(8,128)(2,1)S(1)}, u32[]{:S(2)}, u32[]{:S(2)}) collective-permute-start(bf16[8,80,128]{2,1,0:T(8,128)(2,1)S(1)} %get-tuple-element.17), channel_id=1, source_target_pairs={{0,8},{8,0},{1,9},{9,1},{2,10},{10,2},{3,11},{11,3},{4,12},{12,4},... | collective-permute-start | bytes 491528 | tf_op jit(solution)/shard_map/ppermute | solution.py:256
  81.3 1.0 %collective-permute-done.5.received = bf16[8,80,128]{2,1,0:T(8,128)(2,1)S(1)} collective-permute-done((bf16[8,80,128]{2,1,0:T(8,128)(2,1)S(1)}, bf16[8,80,128]{2,1,0:T(8,128)(2,1)S(1)}, u32[]{:S(2)}, u32[]{:S(2)}) %collective-permute-start.5) | collective-permute-done | bytes 163872 | tf_op jit(solution)/shard_map/ppermute | solution.py:256
  82.3 13.4 %all_to_all.15.parts = bf16[8,80,128]{2,1,0:T(8,128)(2,1)S(1)} all-to-all(bf16[8,80,128]{2,1,0:T(8,128)(2,1)S(1)} %shard_map.91), channel_id=1, replica_groups={{0,256,64,320,128,384,192,448},{1,257,65,321,129,385,193,449},{2,258,66..., dimensions={0} | all-to-all | bytes 327680 | tf_op jit(solution)/shard_map/all_to_all | solution.py:264
  95.7 0.6 shard_map.92
  (1 shorter events, 0.0 us)
Async XLA Ops:
  3.7 11.8 %copy-start.1 = (bf16[8,8,32,32]{3,2,1,0:T(8,128)(2,1)S(1)}, bf16[8,8,32,32]{3,2,1,0:T(8,128)(2,1)}, u32[]{:S(2)}) copy-start(bf16[8,8,32,32]{3,2,1,0:T(8,128)(2,1)} %param.10) | copy-start | bytes 393220
  3.7 34.5 %all-to-all-start = ((bf16[8,256,256]{2,1,0:T(8,128)(2,1)}), bf16[8,256,256]{2,1,0:T(8,128)(2,1)S(1)}, u32[]{:S(2)}, u32[]{:S(2)}) async-start(bf16[8,256,256]{2,1,0:T(8,128)(2,1)} %shard_map.86), calls=%async_computation | async-start | bytes 2097152 | tf_op jit(solution)/shard_map/all_to_all | solution.py:215
  14.7 0.7 copy-start.2
  39.6 9.9 %copy-start = (s32[8,8]{1,0:T(8,128)S(1)}, s32[8,8]{1,0:T(8,128)}, u32[]{:S(2)}) copy-start(s32[8,8]{1,0:T(8,128)} %neighbours.3) | copy-start | bytes 772
  39.6 36.5 %all-to-all-start.1 = ((bf16[32,64,256]{2,1,0:T(8,128)(2,1)}), bf16[32,64,256]{2,1,0:T(8,128)(2,1)S(1)}, u32[]{:S(2)}, u32[]{:S(2)}) async-start(bf16[32,64,256]{2,1,0:T(8,128)(2,1)} %get-tuple-element.11), calls=%async_computation.1 | async-start | bytes 2097152 | tf_op jit(solution)/shard_map/all_to_all | solution.py:236
  51.3 8.8 %collective-permute-start = (bf16[272,256]{1,0:T(8,128)(2,1)S(1)}, bf16[272,256]{1,0:T(8,128)(2,1)S(1)}, u32[]{:S(2)}, u32[]{:S(2)}) collective-permute-start(bf16[272,256]{1,0:T(8,128)(2,1)S(1)} %get-tuple-element.14), channel_id=1, source_target_pairs={{8,16},{16,8},{24,32},{32,24},{40,48},{48,40},{56,64},{64,56},{72,... | collective-permute-start | bytes 417800 | tf_op jit(solution)/shard_map/ppermute | solution.py:234
  55.8 4.3 %collective-permute-start.1 = (bf16[272,256]{1,0:T(8,128)(2,1)S(1)}, bf16[272,256]{1,0:T(8,128)(2,1)S(1)}, u32[]{:S(2)}, u32[]{:S(2)}) collective-permute-start(bf16[272,256]{1,0:T(8,128)(2,1)S(1)} %get-tuple-element.15), channel_id=1, source_target_pairs={{0,8},{8,0},{1,9},{9,1},{2,10},{10,2},{3,11},{11,3},{4,12},{12,4},... | collective-permute-start | bytes 417800 | tf_op jit(solution)/shard_map/ppermute | solution.py:233
  60.3 9.7 %collective-permute-start.4 = (bf16[272,256]{1,0:T(8,128)(2,1)S(1)}, bf16[272,256]{1,0:T(8,128)(2,1)S(1)}, u32[]{:S(2)}, u32[]{:S(2)}) collective-permute-start(bf16[272,256]{1,0:T(8,128)(2,1)S(1)} %shard_map.89.own), channel_id=1, source_target_pairs={{0,32},{16,48},{32,0},{48,16},{1,33},{17,49},{33,1},{49,17},{2,34}... | collective-permute-start | bytes 417800 | tf_op jit(solution)/shard_map/ppermute | solution.py:245
  64.7 10.2 %collective-permute-start.3 = (bf16[272,256]{1,0:T(8,128)(2,1)S(1)}, bf16[272,256]{1,0:T(8,128)(2,1)S(1)}, u32[]{:S(2)}, u32[]{:S(2)}) collective-permute-start(bf16[272,256]{1,0:T(8,128)(2,1)S(1)} %shard_map.89.own), channel_id=1, source_target_pairs={{0,48},{16,32},{32,16},{48,0},{1,49},{17,33},{33,17},{49,1},{2,50}... | collective-permute-start | bytes 417800 | tf_op jit(solution)/shard_map/ppermute | solution.py:245
  68.1 8.0 %collective-permute-start.2 = (bf16[272,256]{1,0:T(8,128)(2,1)S(1)}, bf16[272,256]{1,0:T(8,128)(2,1)S(1)}, u32[]{:S(2)}, u32[]{:S(2)}) collective-permute-start(bf16[272,256]{1,0:T(8,128)(2,1)S(1)} %shard_map.89.own), channel_id=1, source_target_pairs={{0,16},{16,0},{32,48},{48,32},{1,17},{17,1},{33,49},{49,33},{2,18}... | collective-permute-start | bytes 417800 | tf_op jit(solution)/shard_map/ppermute | solution.py:245
  77.2 5.0 %collective-permute-start.5 = (bf16[8,80,128]{2,1,0:T(8,128)(2,1)S(1)}, bf16[8,80,128]{2,1,0:T(8,128)(2,1)S(1)}, u32[]{:S(2)}, u32[]{:S(2)}) collective-permute-start(bf16[8,80,128]{2,1,0:T(8,128)(2,1)S(1)} %get-tuple-element.17), channel_id=1, source_target_pairs={{0,8},{8,0},{1,9},{9,1},{2,10},{10,2},{3,11},{11,3},{4,12},{12,4},... | collective-permute-start | bytes 491528 | tf_op jit(solution)/shard_map/ppermute | solution.py:256

commit v11 on v9

--- a/solution.py
+++ b/solution.py
@@ -34,10 +34,11 @@
     ]
     for copy in copies:
         copy.start()
-    for copy in copies[:3]:
+    for copy in copies[:2]:
         copy.wait()
     kern = dot(left[...], right[...], ((1,), (1,)))
     kern = (kern * kern).astype(jnp.bfloat16)
+    copies[2].wait()
     rows, width = kern.shape
     slots = lax.broadcasted_iota(jnp.int32, (BLK, width), 0)
     masked = jnp.concatenate(

time: 98.1 us -> 98.1 us (level)
  no operation moved by 1% of the time
where the time goes in v11:
time: 98.1 us; the launch traced here: 96.8 us
  starting transfers between devices  40.9 us (42%)
  waiting for transfers between devices  31.6 us (32%)
  blocking collectives  13.8 us (14%)
  Pallas kernels  8.28 us (8%)
  local copies, waits for them, and re-layouts  1.38 us (1%)
    all_to_all x1, waiting for transfers between devices, per_device(): lax.all_to_all(partial, 'env', 0, 0, tiled=True, axis_index_groups=[list(...  22.1 us
    all_to_all x1, blocking collectives, per_device(): lax.all_to_all(terms, 'y', 0, 0, tiled=True, axis_index_groups=[list(ORDE...  13.8 us
    all_to_all x1, starting transfers between devices, per_device(): lax.all_to_all(partial, 'env', 0, 0, tiled=True, axis_index_groups=[list(...  11 us
    all_to_all x1, starting transfers between devices, per_device(): lax.all_to_all(turned, ('x', 'env'), 0, 0, tiled=True, axis_index_groups=...  9.85 us
    ppermute x3, starting transfers between devices, per_device(): lax.ppermute(carried, 'x', [(i, i ^ step) for i in range(group)])  9.64 us
    ppermute x3, waiting for transfers between devices, per_device(): lax.ppermute(carried, 'x', [(i, i ^ step) for i in range(group)])  6.11 us
    ppermute x1, starting transfers between devices, per_device(): outer = lax.ppermute(outer, ROWS_AXES, next_chip)  4.5 us
    ppermute x1, starting transfers between devices, per_device(): received = lax.ppermute(sent, 'core', [(0, 1), (1, 0)])  4 us
  transfers between devices with their start and end apart: 8, of which 5 were waited for; matrix products, arithmetic and copies ran while one was open for 1% of the time, Pallas kernels for 2%

profile of v11, /device:TPU:1, one launch (start us, length us, event | category | flops | bytes accessed | tf_op | source)
XLA Modules:
  0.0 96.8 jit_solution(4694781332724533360)
XLA Ops:
  0.6 3.1 %shard_map.86 = bf16[8,256,256]{2,1,0:T(8,128)(2,1)} custom-call(s32[8]{0:T(128)} %counts.1, bf16[256,1024]{1,0:T(8,128)(2,1)} %features.1, bf16[256,1024]{1,0:T(8,128)(2,1)} %environments.1, bf16[256,2048]{1,0:T(8,128)(2,1)} %projector.1), custom_call_target="tpu_custom_call" | custom-call | tf_op jit(solution)/shard_map/pallas_call | solution.py:199
  3.7 0.0 copy-start.1
  3.7 11.0 %all-to-all-start = ((bf16[8,256,256]{2,1,0:T(8,128)(2,1)}), bf16[8,256,256]{2,1,0:T(8,128)(2,1)S(1)}, u32[]{:S(2)}, u32[]{:S(2)}) async-start(bf16[8,256,256]{2,1,0:T(8,128)(2,1)} %shard_map.86), calls=%async_computation | async-start | bytes 2097152 | tf_op jit(solution)/shard_map/all_to_all | solution.py:215
  14.7 0.0 copy-start.2
  14.8 0.7 copy-done.2
  15.4 0.1 copy.11.target
  15.6 0.0 copy-done.1
  15.6 0.2 copy.10
  15.8 0.4 reshape.13.metric
  16.2 22.1 %all-to-all-done.parts = bf16[8,256,256]{2,1,0:T(8,128)(2,1)S(1)} async-done(((bf16[8,256,256]{2,1,0:T(8,128)(2,1)}), bf16[8,256,256]{2,1,0:T(8,128)(2,1)S(1)}, u32[]{:S(2)}, u32[]{:S(2)}) %all-to-all-start) | async-done | bytes 1048608 | tf_op jit(solution)/shard_map/all_to_all | solution.py:215
  38.3 1.3 %shard_map.87 = (bf16[256,256]{1,0:T(8,128)(2,1)S(1)}, bf16[32,64,256]{2,1,0:T(8,128)(2,1)}) custom-call(bf16[8,256,256]{2,1,0:T(8,128)(2,1)S(1)} %all-to-all-done.parts, bf16[256,256]{1,0:T(8,128)(2,1)S(1)} %reshape.13.metric, f32[256,1]{1,0:T(8,128)S(1)} %copy.11.target), custom_call_target="tpu_custom_call" | custom-call | tf_op jit(solution)/shard_map/pallas_call | solution.py:216
  39.6 0.0 copy-start
  39.6 9.8 %all-to-all-start.1 = ((bf16[32,64,256]{2,1,0:T(8,128)(2,1)}), bf16[32,64,256]{2,1,0:T(8,128)(2,1)S(1)}, u32[]{:S(2)}, u32[]{:S(2)}) async-start(bf16[32,64,256]{2,1,0:T(8,128)(2,1)} %get-tuple-element.11), calls=%async_computation.1 | async-start | bytes 2097152 | tf_op jit(solution)/shard_map/all_to_all | solution.py:236
  49.5 0.0 copy-done
  49.5 1.8 %shard_map.88 = (bf16[272,256]{1,0:T(8,128)(2,1)S(1)}, f32[272,256]{1,0:T(8,128)S(1)}, bf16[272,256]{1,0:T(8,128)(2,1)S(1)}) custom-call(s32[8,8]{1,0:T(8,128)S(1)} %copy-done, bf16[256,256]{1,0:T(8,128)(2,1)S(1)} %get-tuple-element.12.psi, bf16[256,256]{1,0:T(8,128)(2,1)S(1)} %reshape.13.metric, f32[256,1]{1,0:T(8,128)S(1)} %copy.11.target), custom_call_target="tpu_custom_call" | custom-call | tf_op jit(solution)/shard_map/pallas_call | solution.py:224
  51.3 4.5 %collective-permute-start = (bf16[272,256]{1,0:T(8,128)(2,1)S(1)}, bf16[272,256]{1,0:T(8,128)(2,1)S(1)}, u32[]{:S(2)}, u32[]{:S(2)}) collective-permute-start(bf16[272,256]{1,0:T(8,128)(2,1)S(1)} %get-tuple-element.14), channel_id=1, source_target_pairs={{8,16},{16,8},{24,32},{32,24},{40,48},{48,40},{56,64},{64,56},{72,... | collective-permute-start | bytes 417800 | tf_op jit(solution)/shard_map/ppermute | solution.py:234
  55.8 1.9 %collective-permute-start.1 = (bf16[272,256]{1,0:T(8,128)(2,1)S(1)}, bf16[272,256]{1,0:T(8,128)(2,1)S(1)}, u32[]{:S(2)}, u32[]{:S(2)}) collective-permute-start(bf16[272,256]{1,0:T(8,128)(2,1)S(1)} %get-tuple-element.15), channel_id=1, source_target_pairs={{0,8},{8,0},{1,9},{9,1},{2,10},{10,2},{3,11},{11,3},{4,12},{12,4},... | collective-permute-start | bytes 417800 | tf_op jit(solution)/shard_map/ppermute | solution.py:233
  57.7 2.4 %collective-permute-done.outer = bf16[272,256]{1,0:T(8,128)(2,1)S(1)} collective-permute-done((bf16[272,256]{1,0:T(8,128)(2,1)S(1)}, bf16[272,256]{1,0:T(8,128)(2,1)S(1)}, u32[]{:S(2)}, u32[]{:S(2)}) %collective-permute-start) | collective-permute-done | bytes 139296 | tf_op jit(solution)/shard_map/ppermute | solution.py:234
  60.1 0.0 collective-permute-done.1.inner
  60.1 0.2 shard_map.89.own
  60.4 4.4 %collective-permute-start.4 = (bf16[272,256]{1,0:T(8,128)(2,1)S(1)}, bf16[272,256]{1,0:T(8,128)(2,1)S(1)}, u32[]{:S(2)}, u32[]{:S(2)}) collective-permute-start(bf16[272,256]{1,0:T(8,128)(2,1)S(1)} %shard_map.89.own), channel_id=1, source_target_pairs={{0,32},{16,48},{32,0},{48,16},{1,33},{17,49},{33,1},{49,17},{2,34}... | collective-permute-start | bytes 417800 | tf_op jit(solution)/shard_map/ppermute | solution.py:245
  64.7 3.4 %collective-permute-start.3 = (bf16[272,256]{1,0:T(8,128)(2,1)S(1)}, bf16[272,256]{1,0:T(8,128)(2,1)S(1)}, u32[]{:S(2)}, u32[]{:S(2)}) collective-permute-start(bf16[272,256]{1,0:T(8,128)(2,1)S(1)} %shard_map.89.own), channel_id=1, source_target_pairs={{0,48},{16,32},{32,16},{48,0},{1,49},{17,33},{33,17},{49,1},{2,50}... | collective-permute-start | bytes 417800 | tf_op jit(solution)/shard_map/ppermute | solution.py:245
  68.1 1.9 %collective-permute-start.2 = (bf16[272,256]{1,0:T(8,128)(2,1)S(1)}, bf16[272,256]{1,0:T(8,128)(2,1)S(1)}, u32[]{:S(2)}, u32[]{:S(2)}) collective-permute-start(bf16[272,256]{1,0:T(8,128)(2,1)S(1)} %shard_map.89.own), channel_id=1, source_target_pairs={{0,16},{16,0},{32,48},{48,32},{1,17},{17,1},{33,49},{49,33},{2,18}... | collective-permute-start | bytes 417800 | tf_op jit(solution)/shard_map/ppermute | solution.py:245
  70.0 0.0 collective-permute-done.4.rest_2_
  70.0 4.9 %collective-permute-done.3.rest_1_ = bf16[272,256]{1,0:T(8,128)(2,1)S(1)} collective-permute-done((bf16[272,256]{1,0:T(8,128)(2,1)S(1)}, bf16[272,256]{1,0:T(8,128)(2,1)S(1)}, u32[]{:S(2)}, u32[]{:S(2)}) %collective-permute-start.3) | collective-permute-done | bytes 139296 | tf_op jit(solution)/shard_map/ppermute | solution.py:245
  74.9 1.2 %collective-permute-done.2.rest_0_ = bf16[272,256]{1,0:T(8,128)(2,1)S(1)} collective-permute-done((bf16[272,256]{1,0:T(8,128)(2,1)S(1)}, bf16[272,256]{1,0:T(8,128)(2,1)S(1)}, u32[]{:S(2)}, u32[]{:S(2)}) %collective-permute-start.2) | collective-permute-done | bytes 139296 | tf_op jit(solution)/shard_map/ppermute | solution.py:245
  76.1 0.0 all-to-all-done.1.pieces
  76.1 1.1 %shard_map.90 = (f32[8,80,128]{2,1,0:T(8,128)S(1)}, bf16[8,80,128]{2,1,0:T(8,128)(2,1)S(1)}) custom-call(s32[8,8]{1,0:T(8,128)S(1)} %copy-done, bf16[32,64,256]{2,1,0:T(8,128)(2,1)S(1)} %all-to-all-done.1.pieces, bf16[272,256]{1,0:T(8,128)(2,1)S(1)} %shard_map.89.own, bf16[272,256]{1,0:T(8,128)(2,1)S(1)} %collective-permute-done.2.rest_0_, ...), custom_call_target="tpu_custom_call" | custom-call | tf_op jit(solution)/shard_map/pallas_call | solution.py:248
  77.3 4.0 %collective-permute-start.5 = (bf16[8,80,128]{2,1,0:T(8,128)(2,1)S(1)}, bf16[8,80,128]{2,1,0:T(8,128)(2,1)S(1)}, u32[]{:S(2)}, u32[]{:S(2)}) collective-permute-start(bf16[8,80,128]{2,1,0:T(8,128)(2,1)S(1)} %get-tuple-element.17), channel_id=1, source_target_pairs={{0,8},{8,0},{1,9},{9,1},{2,10},{10,2},{3,11},{11,3},{4,12},{12,4},... | collective-permute-start | bytes 491528 | tf_op jit(solution)/shard_map/ppermute | solution.py:256
  81.3 1.0 %collective-permute-done.5.received = bf16[8,80,128]{2,1,0:T(8,128)(2,1)S(1)} collective-permute-done((bf16[8,80,128]{2,1,0:T(8,128)(2,1)S(1)}, bf16[8,80,128]{2,1,0:T(8,128)(2,1)S(1)}, u32[]{:S(2)}, u32[]{:S(2)}) %collective-permute-start.5) | collective-permute-done | bytes 163872 | tf_op jit(solution)/shard_map/ppermute | solution.py:256
  82.3 13.8 %all_to_all.15.parts = bf16[8,80,128]{2,1,0:T(8,128)(2,1)S(1)} all-to-all(bf16[8,80,128]{2,1,0:T(8,128)(2,1)S(1)} %shard_map.91), channel_id=1, replica_groups={{0,128,256,384,64,192,320,448},{1,129,257,385,65,193,321,449},{2,130,25..., dimensions={0} | all-to-all | bytes 327680 | tf_op jit(solution)/shard_map/all_to_all | solution.py:264
  96.1 0.6 shard_map.92
  (1 shorter events, 0.0 us)
Async XLA Ops:
  3.7 11.8 %copy-start.1 = (bf16[8,8,32,32]{3,2,1,0:T(8,128)(2,1)S(1)}, bf16[8,8,32,32]{3,2,1,0:T(8,128)(2,1)}, u32[]{:S(2)}) copy-start(bf16[8,8,32,32]{3,2,1,0:T(8,128)(2,1)} %param.10) | copy-start | bytes 393220
  3.7 34.5 %all-to-all-start = ((bf16[8,256,256]{2,1,0:T(8,128)(2,1)}), bf16[8,256,256]{2,1,0:T(8,128)(2,1)S(1)}, u32[]{:S(2)}, u32[]{:S(2)}) async-start(bf16[8,256,256]{2,1,0:T(8,128)(2,1)} %shard_map.86), calls=%async_computation | async-start | bytes 2097152 | tf_op jit(solution)/shard_map/all_to_all | solution.py:215
  14.7 0.7 copy-start.2
  39.6 9.9 %copy-start = (s32[8,8]{1,0:T(8,128)S(1)}, s32[8,8]{1,0:T(8,128)}, u32[]{:S(2)}) copy-start(s32[8,8]{1,0:T(8,128)} %neighbours.3) | copy-start | bytes 772
  39.6 36.5 %all-to-all-start.1 = ((bf16[32,64,256]{2,1,0:T(8,128)(2,1)}), bf16[32,64,256]{2,1,0:T(8,128)(2,1)S(1)}, u32[]{:S(2)}, u32[]{:S(2)}) async-start(bf16[32,64,256]{2,1,0:T(8,128)(2,1)} %get-tuple-element.11), calls=%async_computation.1 | async-start | bytes 2097152 | tf_op jit(solution)/shard_map/all_to_all | solution.py:236
  51.3 8.8 %collective-permute-start = (bf16[272,256]{1,0:T(8,128)(2,1)S(1)}, bf16[272,256]{1,0:T(8,128)(2,1)S(1)}, u32[]{:S(2)}, u32[]{:S(2)}) collective-permute-start(bf16[272,256]{1,0:T(8,128)(2,1)S(1)} %get-tuple-element.14), channel_id=1, source_target_pairs={{8,16},{16,8},{24,32},{32,24},{40,48},{48,40},{56,64},{64,56},{72,... | collective-permute-start | bytes 417800 | tf_op jit(solution)/shard_map/ppermute | solution.py:234
  55.8 4.3 %collective-permute-start.1 = (bf16[272,256]{1,0:T(8,128)(2,1)S(1)}, bf16[272,256]{1,0:T(8,128)(2,1)S(1)}, u32[]{:S(2)}, u32[]{:S(2)}) collective-permute-start(bf16[272,256]{1,0:T(8,128)(2,1)S(1)} %get-tuple-element.15), channel_id=1, source_target_pairs={{0,8},{8,0},{1,9},{9,1},{2,10},{10,2},{3,11},{11,3},{4,12},{12,4},... | collective-permute-start | bytes 417800 | tf_op jit(solution)/shard_map/ppermute | solution.py:233
  60.4 9.7 %collective-permute-start.4 = (bf16[272,256]{1,0:T(8,128)(2,1)S(1)}, bf16[272,256]{1,0:T(8,128)(2,1)S(1)}, u32[]{:S(2)}, u32[]{:S(2)}) collective-permute-start(bf16[272,256]{1,0:T(8,128)(2,1)S(1)} %shard_map.89.own), channel_id=1, source_target_pairs={{0,32},{16,48},{32,0},{48,16},{1,33},{17,49},{33,1},{49,17},{2,34}... | collective-permute-start | bytes 417800 | tf_op jit(solution)/shard_map/ppermute | solution.py:245
  64.7 10.2 %collective-permute-start.3 = (bf16[272,256]{1,0:T(8,128)(2,1)S(1)}, bf16[272,256]{1,0:T(8,128)(2,1)S(1)}, u32[]{:S(2)}, u32[]{:S(2)}) collective-permute-start(bf16[272,256]{1,0:T(8,128)(2,1)S(1)} %shard_map.89.own), channel_id=1, source_target_pairs={{0,48},{16,32},{32,16},{48,0},{1,49},{17,33},{33,17},{49,1},{2,50}... | collective-permute-start | bytes 417800 | tf_op jit(solution)/shard_map/ppermute | solution.py:245
  68.1 8.0 %collective-permute-start.2 = (bf16[272,256]{1,0:T(8,128)(2,1)S(1)}, bf16[272,256]{1,0:T(8,128)(2,1)S(1)}, u32[]{:S(2)}, u32[]{:S(2)}) collective-permute-start(bf16[272,256]{1,0:T(8,128)(2,1)S(1)} %shard_map.89.own), channel_id=1, source_target_pairs={{0,16},{16,0},{32,48},{48,32},{1,17},{17,1},{33,49},{49,33},{2,18}... | collective-permute-start | bytes 417800 | tf_op jit(solution)/shard_map/ppermute | solution.py:245
  77.3 5.0 %collective-permute-start.5 = (bf16[8,80,128]{2,1,0:T(8,128)(2,1)S(1)}, bf16[8,80,128]{2,1,0:T(8,128)(2,1)S(1)}, u32[]{:S(2)}, u32[]{:S(2)}) collective-permute-start(bf16[8,80,128]{2,1,0:T(8,128)(2,1)S(1)} %get-tuple-element.17), channel_id=1, source_target_pairs={{0,8},{8,0},{1,9},{9,1},{2,10},{10,2},{3,11},{11,3},{4,12},{12,4},... | collective-permute-start | bytes 491528 | tf_op jit(solution)/shard_map/ppermute | solution.py:256
